TPU v7x, 32 devices: a whole 2x2x4 slice. The times are simulated.
32 devices in a mesh: heads: 4 (over z), experts: 8 (over y, x, core).
Axes of the slice: x: 2, y: 2, z: 4, core: 2. Of those that a mesh axis runs over, the one named last changes fastest.
Arguments:
- layer_input: bfloat16 [1024, 16, 1024], P('heads', 'experts'), may hold values from -6 to 6
- seq_lengths: int32 [16], P('experts'), may hold values from 256 to 1024, as said below
- expert_ids: int32 [1024, 16, 8], P('heads', 'experts'), may hold values from 0 to 31, all different within a row
- route_weight: float32 [1024, 16, 8], P('heads', 'experts'), may hold values from 0.06 to 0.25
- priority: int32 [1024, 16], P('heads', 'experts'), may hold values from 0 to 511, as said below
- attn_gain: float32 [1024], replicated, may hold values from 0.25 to 1.75
- moe_gain: float32 [1024], replicated, may hold values from 0.25 to 1.75
- query_matrix: bfloat16 [1024, 1024], P(None, 'heads'), may hold values from -0.375 to 0.375
- key_matrix: bfloat16 [1024, 512], P(None, 'heads'), may hold values from -0.1875 to 0.1875
- value_matrix: bfloat16 [1024, 512], P(None, 'heads'), may hold values from -0.1875 to 0.1875
- output_matrix: bfloat16 [1024, 1024], P('heads'), may hold values from -0.75 to 0.75
- expert_in: bfloat16 [32, 1024, 1024], P('experts'), may hold values from -0.1875 to 0.1875
- expert_down: bfloat16 [32, 512, 1024], P('experts'), may hold values from -1 to 1
- out_grad: bfloat16 [1024, 16, 1024], P('heads', 'experts'), may hold values from -6 to 6
Outputs:
- out: bfloat16 [1024, 16, 1024], P('heads', 'experts')
- x_grad: float32 [1024, 16, 1024], P('heads', 'experts')
- grad_attn_gain: float32 [1024], replicated
- grad_moe_gain: float32 [1024], replicated
- grad_query_weight: float32 [1024, 1024], P(None, 'heads')
- grad_key_weight: float32 [1024, 512], P(None, 'heads')
- grad_value_weight: float32 [1024, 512], P(None, 'heads')
- grad_output_weight: float32 [1024, 1024], P('heads')
- grad_expert_in: float32 [32, 1024, 1024], P('experts')
- grad_expert_down: float32 [32, 512, 1024], P('experts')
Inputs may be any that keep to these rules, and one draw needn't show every extreme that they name: `seq_lengths`: in each group of 2 sequences that one index of experts holds, one sequence has the full length 1024. `priority`: among the tokens of one device (positions of one index of heads in the sequences of one index of experts), each value appears exactly once. `expert_ids`: the 8 experts of a token are different.
All inputs are finite; a program needn't handle non-finite values.
Results may differ from a plain program's by a relative error of at most 0.017.
The roundings to bfloat16 on the way count: a program that leaves them out, or rounds other values in their place, can miss the bound.
Values may be sent and summed in bfloat16 or wider, within the bound.
A program may use at most 256 MiB of HBM per device.

v0:
```python
import math

import jax
import jax.numpy as jnp
from jax import lax
from jax.sharding import PartitionSpec as P

HEAD_SIZE = 64
EXPERTS = 32


epsilon = 1e-06


def rms_scale(values):
    return lax.rsqrt(jnp.mean(values * values, axis=-1, keepdims=True) + epsilon)


def scaled_norm(values, gain):
    return values * rms_scale(values) * gain


def rotary_tables(length, head_dim):
    half_dim = head_dim // 2
    frequency = jnp.exp(
        jnp.arange(half_dim, dtype=jnp.float32) * (-2.0 * math.log(10000.0) / head_dim)
    )
    angles = jnp.arange(length, dtype=jnp.float32)[:, None] * frequency[None, :]
    return (jnp.cos(angles), jnp.sin(angles))


def apply_rotary(values, cosine_table, sine_table):
    half_dim = values.shape[-1] // 2
    lower_half = values[..., :half_dim]
    upper_half = values[..., half_dim:]
    return jnp.concatenate(
        [
            lower_half * cosine_table - upper_half * sine_table,
            upper_half * cosine_table + lower_half * sine_table,
        ],
        axis=-1,
    )


def block_slots(block_ids, block_order, block_live, expert_count, capacity):
    token_count, top_count = block_ids.shape
    ranked = (
        jnp.zeros((token_count,), jnp.int32)
        .at[block_order]
        .set(jnp.arange(token_count, dtype=jnp.int32))
    )
    sorted_ids = block_ids[ranked].reshape(-1)
    sorted_live = jnp.repeat(block_live[ranked], top_count)
    matches = (
        (sorted_ids[:, None] == jnp.arange(expert_count, dtype=jnp.int32)[None, :])
        & sorted_live[:, None]
    ).astype(jnp.int32)
    before = jnp.cumsum(matches, axis=0) - matches
    slot_sorted = jnp.sum(before * matches, axis=1)
    keep_sorted = sorted_live & (slot_sorted < capacity)
    target_sorted = jnp.where(
        keep_sorted, sorted_ids * capacity + slot_sorted, expert_count * capacity
    )
    target = target_sorted.reshape(token_count, top_count)[block_order]
    owners = jnp.full((expert_count * capacity + 1,), token_count, jnp.int32)
    owners = owners.at[target.reshape(-1)].set(
        jnp.repeat(jnp.arange(token_count, dtype=jnp.int32), top_count)
    )
    return (target, owners[: expert_count * capacity])


def masked_scores(query_block, key_seq, offset, length_one, score_scale):
    raw = jnp.einsum("qgrd,kgd->grqk", query_block, key_seq, preferred_element_type=jnp.float32)
    query_pos = offset + jnp.arange(query_block.shape[0], dtype=jnp.int32)
    key_pos = jnp.arange(key_seq.shape[0], dtype=jnp.int32)
    allowed = (key_pos[None, :] <= query_pos[:, None]) & (key_pos[None, :] < length_one)
    return jnp.where(allowed, raw * score_scale, -1e30)


def body(
    layer_input,
    seq_lengths,
    expert_ids,
    route_weight,
    priority,
    attn_gain,
    moe_gain,
    query_matrix,
    key_matrix,
    value_matrix,
    output_matrix,
    expert_in,
    expert_down,
    out_grad,
):
    seg_rows, seq_count, width = layer_input.shape
    full_len = seg_rows * lax.axis_size("heads")
    tok_count = seg_rows * seq_count
    top_count = expert_ids.shape[-1]
    kv_local = key_matrix.shape[1] // HEAD_SIZE
    q_local = query_matrix.shape[1] // HEAD_SIZE
    group_width = q_local // kv_local
    exp_local = expert_in.shape[0]
    hidden_width = expert_down.shape[1]
    capacity = (5 * tok_count * top_count + 4 * EXPERTS - 1) // (4 * EXPERTS)
    slot_count = EXPERTS * capacity
    block_rows = min(512, full_len)
    score_scale = HEAD_SIZE ** (-0.5)
    inputs_f = layer_input.astype(jnp.float32)
    norm_one, attn_pull = jax.vjp(scaled_norm, inputs_f, attn_gain)
    attention_input = norm_one.astype(jnp.bfloat16)
    collected_rows = lax.all_gather(attention_input, "heads", axis=0, tiled=True)
    query_linear = jnp.einsum(
        "gro,ox->grx", collected_rows, query_matrix, preferred_element_type=jnp.float32
    )
    key_linear = jnp.einsum(
        "gro,ox->grx", collected_rows, key_matrix, preferred_element_type=jnp.float32
    )
    value_linear = jnp.einsum(
        "gro,ox->grx", collected_rows, value_matrix, preferred_element_type=jnp.float32
    )
    cosine_table, sine_table = rotary_tables(full_len, HEAD_SIZE)
    cos_query = cosine_table[:, None, None, None, :]
    sin_query = sine_table[:, None, None, None, :]
    cos_key = cosine_table[:, None, None, :]
    sin_key = sine_table[:, None, None, :]
    query_rotated = apply_rotary(
        query_linear.reshape(full_len, seq_count, kv_local, group_width, HEAD_SIZE),
        cos_query,
        sin_query,
    ).astype(jnp.bfloat16)
    key_rotated = apply_rotary(
        key_linear.reshape(full_len, seq_count, kv_local, HEAD_SIZE), cos_key, sin_key
    ).astype(jnp.bfloat16)
    value_reduced = value_linear.reshape(full_len, seq_count, kv_local, HEAD_SIZE).astype(
        jnp.bfloat16
    )
    head_rows = []
    lse_list = []
    for member in range(seq_count):
        seq_blocks = []
        seq_lse = []
        for offset in range(0, full_len, block_rows):
            scores = masked_scores(
                query_rotated[offset : offset + block_rows, member],
                key_rotated[:, member],
                offset,
                seq_lengths[member],
                score_scale,
            )
            row_max = jnp.max(scores, axis=-1, keepdims=True)
            raised = jnp.exp(scores - row_max)
            row_sum = jnp.sum(raised, axis=-1, keepdims=True)
            probs = raised / row_sum
            seq_lse.append(row_max + jnp.log(row_sum))
            seq_blocks.append(
                jnp.einsum(
                    "grqk,kgd->qgrd",
                    probs.astype(jnp.bfloat16),
                    value_reduced[:, member],
                    preferred_element_type=jnp.float32,
                ).astype(jnp.bfloat16)
            )
        head_rows.append(jnp.concatenate(seq_blocks, axis=0))
        lse_list.append(seq_lse)
    head_result = jnp.stack(head_rows, axis=1).reshape(full_len, seq_count, q_local * HEAD_SIZE)
    attention_path = lax.psum_scatter(
        jnp.einsum("gwm,mr->gwr", head_result, output_matrix, preferred_element_type=jnp.float32),
        "heads",
        scatter_dimension=0,
        tiled=True,
    )
    mid = inputs_f + attention_path
    mid_flat = mid.reshape(tok_count, width)
    norm_two, moe_pull = jax.vjp(scaled_norm, mid_flat, moe_gain)
    moe_in = norm_two.astype(jnp.bfloat16)
    position = lax.axis_index("heads") * seg_rows + jnp.arange(seg_rows, dtype=jnp.int32)
    live = position[:, None] < seq_lengths[None, :]
    target, owners = block_slots(
        expert_ids.reshape(tok_count, top_count),
        priority.reshape(tok_count),
        live.reshape(tok_count),
        EXPERTS,
        capacity,
    )
    padded_in = jnp.concatenate([moe_in, jnp.zeros((1, width), jnp.bfloat16)], axis=0)
    send_rows = padded_in[owners].reshape(EXPERTS, capacity, width)
    arrived = lax.all_to_all(send_rows, "experts", split_axis=0, concat_axis=0, tiled=True)
    src_count = arrived.shape[0] // exp_local
    grouped = arrived.reshape(src_count, exp_local, arrived.shape[1], width)
    gate_up = jnp.einsum("sjcd,jdf->sjcf", grouped, expert_in, preferred_element_type=jnp.float32)
    hidden = (jax.nn.silu(gate_up[..., :hidden_width]) * gate_up[..., hidden_width:]).astype(
        jnp.bfloat16
    )
    result = jnp.einsum(
        "sjcf,jfd->sjcd", hidden, expert_down, preferred_element_type=jnp.float32
    ).astype(jnp.bfloat16)
    result_rows = result.reshape(arrived.shape)
    gate_up_kept = gate_up.reshape(arrived.shape[0], arrived.shape[1], 2 * hidden_width)
    returned = lax.all_to_all(result_rows, "experts", split_axis=0, concat_axis=0, tiled=True)
    padded_ret = jnp.concatenate(
        [returned.reshape(slot_count, width), jnp.zeros((1, width), jnp.bfloat16)], axis=0
    )
    picked = padded_ret[target]
    weights_flat = route_weight.reshape(tok_count, top_count)
    moe_sum = jnp.sum(weights_flat[:, :, None] * picked.astype(jnp.float32), axis=1)
    out = (mid_flat + moe_sum).astype(jnp.bfloat16).reshape(seg_rows, seq_count, width)
    grad_flat = out_grad.astype(jnp.float32).reshape(tok_count, width)
    slot_table = (
        jnp.zeros((slot_count + 1,), jnp.float32)
        .at[target.reshape(-1)]
        .set(weights_flat.reshape(-1))
    )
    padded_grad = jnp.concatenate([grad_flat, jnp.zeros((1, width), jnp.float32)], axis=0)
    d_send = (slot_table[:slot_count, None] * padded_grad[owners]).astype(jnp.bfloat16)
    grad_arrived = lax.all_to_all(
        d_send.reshape(EXPERTS, capacity, width), "experts", split_axis=0, concat_axis=0, tiled=True
    )
    src_total = grad_arrived.shape[0] // exp_local
    d_out = grad_arrived.reshape(src_total, exp_local, capacity, width)
    grouped_in = arrived.reshape(src_total, exp_local, capacity, width)
    gate_up = gate_up_kept.reshape(src_total, exp_local, capacity, 2 * hidden_width)
    gate = gate_up[..., :hidden_width]
    up_part = gate_up[..., hidden_width:]
    sigmoid_gate = jax.nn.sigmoid(gate)
    activated = jax.nn.silu(gate)
    hidden = (activated * up_part).astype(jnp.bfloat16)
    grad_down = jnp.einsum("sjcf,sjcd->jfd", hidden, d_out, preferred_element_type=jnp.float32)
    d_hidden = jnp.einsum("sjcd,jfd->sjcf", d_out, expert_down, preferred_element_type=jnp.float32)
    d_gate = d_hidden * up_part * (sigmoid_gate * (1.0 + gate * (1.0 - sigmoid_gate)))
    d_up = d_hidden * activated
    d_gate_up = jnp.concatenate([d_gate, d_up], axis=-1).astype(jnp.bfloat16)
    grad_in = jnp.einsum(
        "sjcd,sjcf->jdf", grouped_in, d_gate_up, preferred_element_type=jnp.float32
    )
    d_rows = jnp.einsum(
        "sjcf,jdf->sjcd", d_gate_up, expert_in, preferred_element_type=jnp.float32
    ).astype(jnp.bfloat16)
    back_rows = lax.all_to_all(
        d_rows.reshape(src_total * exp_local, capacity, width),
        "experts",
        split_axis=0,
        concat_axis=0,
        tiled=True,
    )
    padded_back = jnp.concatenate(
        [back_rows.reshape(slot_count, width), jnp.zeros((1, width), jnp.bfloat16)], axis=0
    )
    d_moe_in = jnp.sum(padded_back[target].astype(jnp.float32), axis=1)
    d_mid_norm, grad_gain_two = moe_pull(d_moe_in)
    d_mid = (grad_flat + d_mid_norm).reshape(seg_rows, seq_count, width)
    d_branch = d_mid.astype(jnp.bfloat16)
    path_combined = lax.all_gather(d_branch, "heads", axis=0, tiled=True)
    grad_output = jnp.einsum(
        "iem,iea->ma", head_result, path_combined, preferred_element_type=jnp.float32
    )
    d_head = jnp.einsum(
        "zgk,ck->zgc", path_combined, output_matrix, preferred_element_type=jnp.float32
    ).astype(jnp.bfloat16)
    d_head = d_head.reshape(full_len, seq_count, kv_local, group_width, HEAD_SIZE)
    query_grads = []
    key_grads = []
    value_grads = []
    for member in range(seq_count):
        key_grad = jnp.zeros((full_len, kv_local, HEAD_SIZE), jnp.float32)
        value_grad = jnp.zeros((full_len, kv_local, HEAD_SIZE), jnp.float32)
        query_parts = []
        for block_number, offset in enumerate(range(0, full_len, block_rows)):
            query_block = query_rotated[offset : offset + block_rows, member]
            scores = masked_scores(
                query_block, key_rotated[:, member], offset, seq_lengths[member], score_scale
            )
            probs = jnp.exp(scores - lse_list[member][block_number])
            grad_block = d_head[offset : offset + block_rows, member]
            prob_grad = jnp.einsum(
                "qgrd,kgd->grqk",
                grad_block,
                value_reduced[:, member],
                preferred_element_type=jnp.float32,
            )
            delta_sum = jnp.sum(probs * prob_grad, axis=-1, keepdims=True)
            raw_grad = (probs * (prob_grad - delta_sum) * score_scale).astype(jnp.bfloat16)
            value_grad = value_grad + jnp.einsum(
                "grqk,qgrd->kgd",
                probs.astype(jnp.bfloat16),
                grad_block,
                preferred_element_type=jnp.float32,
            )
            key_grad = key_grad + jnp.einsum(
                "grqk,qgrd->kgd", raw_grad, query_block, preferred_element_type=jnp.float32
            )
            query_parts.append(
                jnp.einsum(
                    "grqk,kgd->qgrd",
                    raw_grad,
                    key_rotated[:, member],
                    preferred_element_type=jnp.float32,
                )
            )
        query_grads.append(jnp.concatenate(query_parts, axis=0))
        key_grads.append(key_grad)
        value_grads.append(value_grad)
    d_query_rot = jnp.stack(query_grads, axis=1)
    d_key_rot = jnp.stack(key_grads, axis=1)
    d_value = jnp.stack(value_grads, axis=1)
    query_cotangent = (
        apply_rotary(d_query_rot, cos_query, -sin_query)
        .astype(jnp.bfloat16)
        .reshape(full_len, seq_count, q_local * HEAD_SIZE)
    )
    key_cotangent = (
        apply_rotary(d_key_rot, cos_key, -sin_key)
        .astype(jnp.bfloat16)
        .reshape(full_len, seq_count, kv_local * HEAD_SIZE)
    )
    value_reduced_cotangent = d_value.astype(jnp.bfloat16).reshape(
        full_len, seq_count, kv_local * HEAD_SIZE
    )
    query_gradient = jnp.einsum(
        "kjt,kjc->tc", collected_rows, query_cotangent, preferred_element_type=jnp.float32
    )
    key_gradient = jnp.einsum(
        "kjt,kjc->tc", collected_rows, key_cotangent, preferred_element_type=jnp.float32
    )
    grad_value = jnp.einsum(
        "kjt,kjc->tc", collected_rows, value_reduced_cotangent, preferred_element_type=jnp.float32
    )
    total_rows = jnp.einsum(
        "ugw,ew->uge", query_cotangent, query_matrix, preferred_element_type=jnp.float32
    )
    total_rows = total_rows + jnp.einsum(
        "ugw,ew->uge", key_cotangent, key_matrix, preferred_element_type=jnp.float32
    )
    d_attn_in = lax.psum_scatter(
        total_rows
        + jnp.einsum(
            "ugw,ew->uge", value_reduced_cotangent, value_matrix, preferred_element_type=jnp.float32
        ),
        "heads",
        scatter_dimension=0,
        tiled=True,
    )
    d_input_norm, grad_gain_one = attn_pull(d_attn_in)
    x_grad = d_mid + d_input_norm
    summed = lax.psum(
        (query_gradient, key_gradient, grad_value, grad_output, grad_gain_one, grad_gain_two),
        "experts",
    )
    expert_summed = lax.psum((grad_in, grad_down, summed[4], summed[5]), "heads")
    return (
        out,
        x_grad,
        expert_summed[2],
        expert_summed[3],
        summed[0],
        summed[1],
        summed[2],
        summed[3],
        expert_summed[0],
        expert_summed[1],
    )


def solution(mesh):
    in_specs = (
        P("heads", "experts", None),
        P("experts"),
        P("heads", "experts", None),
        P("heads", "experts", None),
        P("heads", "experts"),
        P(),
        P(),
        P(None, "heads"),
        P(None, "heads"),
        P(None, "heads"),
        P("heads", None),
        P("experts", None, None),
        P("experts", None, None),
        P("heads", "experts", None),
    )
    out_specs = (
        P("heads", "experts", None),
        P("heads", "experts", None),
        P(),
        P(),
        P(None, "heads"),
        P(None, "heads"),
        P(None, "heads"),
        P("heads", None),
        P("experts", None, None),
        P("experts", None, None),
    )
    return jax.shard_map(body, mesh=mesh, in_specs=in_specs, out_specs=out_specs, check_vma=False)
```

profile of v0, /device:TPU:0, one launch (start us, length us, event | category | flops | bytes accessed | tf_op | source)
XLA Modules:
  0.0 2144.7 jit_solution(16322780013341744125)
XLA Ops:
  18.9 77.3 %all-gather.3.cloned.1.call-done = bf16[1024,2,1024]{2,0,1:T(8,128)(2,1)} async-done(((bf16[256,2,1024]{2,0,1:T(8,128)(2,1)}), bf16[1024,2,1024]{2,0,1:T(8,128)(2,1)}) %all-gather.3.cloned.1.call-update) | async-done | bytes 4194320 | tf_op jit(solution)/shard_map/all_gather | solution.py:112
  154.7 15.5 scatter_custom_fusion.1
  170.3 106.2 %reduce-scatter.3.cloned.1.call-done = f32[256,2,1024]{2,0,1:T(8,128)} async-done(((f32[1024,2,1024]{2,0,1:T(8,128)}), f32[256,2,1024]{2,0,1:T(8,128)}) %reduce-scatter.3.cloned.1.call-update) | async-done | bytes 2097168 | tf_op jit(solution)/shard_map/reduce_scatter | solution.py:167
  288.2 22.4 %gather_fusion.3 = bf16[5120,1024]{1,0:T(8,128)(2,1)} fusion(bf16[513,1024]{1,0:T(8,128)(2,1)S(1)} %concatenate.51, s32[5120]{0:T(1024)S(1)} %fusion.178), kind=kCustom, calls=%fused_computation.3 | custom fusion | bytes 20992000 | tf_op jit(solution)/shard_map/gather | solution.py:187
  316.5 15.5 scatter_custom_fusion.2
  338.3 22.9 %gather_fusion.5 = f32[5120,1024]{1,0:T(8,128)} fusion(f32[513,1024]{1,0:T(8,128)S(1)} %concatenate.53, s32[5120]{0:T(1024)S(1)} %fusion.178), kind=kCustom, calls=%fused_computation.5 | custom fusion | bytes 41963520 | tf_op jit(solution)/shard_map/gather | solution.py:215
  361.1 12.3 multiply_convert_fusion
  373.5 59.0 %all-to-all-done = bf16[32,160,1024]{2,1,0:T(8,128)(2,1)} async-done(((bf16[32,160,1024]{2,1,0:T(8,128)(2,1)}), bf16[32,160,1024]{2,1,0:T(8,128)(2,1)}, u32[]{:S(2)}, u32[]{:S(2)}) %all-to-all-start) | async-done | bytes 10485792 | tf_op jit(solution)/shard_map/all_to_all | solution.py:188
  438.1 20.1 fusion.35
  458.2 96.4 %all-to-all-done.2 = bf16[32,160,1024]{2,1,0:T(8,128)(2,1)} async-done(((bf16[32,160,1024]{2,1,0:T(8,128)(2,1)}), bf16[32,160,1024]{2,1,0:T(8,128)(2,1)}, u32[]{:S(2)}, u32[]{:S(2)}) %all-to-all-start.2) | async-done | bytes 10485792 | tf_op jit(solution)/shard_map/all_to_all | solution.py:216
  554.6 21.9 %fusion.6 = (bf16[8,4,160,512]{3,2,0,1:T(8,128)(2,1)}, bf16[8,4,160,512]{3,2,0,1:T(8,128)(2,1)}, bf16[8,4,160,512]{3,2,0,1:T(8,128)(2,1)}) fusion(f32[8,4,160,1024]{3,2,0,1:T(8,128)} %fusion.35, bf16[4,512,1024]{2,1,0:T(8,128)(2,1)} %param.26, bf16[8,4,160,1024]{3,2,1,0:T(8,128)(2,1)} %bitcast.58), kind=kOutput, calls=%fused_computation.22 | convolution fusion | flops 5408030720 | bytes 51380224 | tf_op jit(solution)/shard_map/sjcd,jfd->sjcf/dot_general | solution.py:229
  576.5 17.6 convert_bitcast_fusion
  609.5 116.3 %all-to-all-done.3 = bf16[32,160,1024]{2,1,0:T(8,128)(2,1)} async-done(((bf16[32,160,1024]{2,1,0:T(8,128)(2,1)}), bf16[32,160,1024]{2,1,0:T(8,128)(2,1)}, u32[]{:S(2)}, u32[]{:S(2)}) %all-to-all-start.3) | async-done | bytes 10485792 | tf_op jit(solution)/shard_map/all_to_all | solution.py:239
  735.8 26.1 %gather_fusion.6 = bf16[4096,1024]{1,0:T(8,128)(2,1)} fusion(bf16[5121,1024]{1,0:T(8,128)(2,1)} %concatenate.55, s32[4096]{0:T(1024)S(1)} %broadcast_clamp_fusion), kind=kCustom, calls=%fused_computation.6 | custom fusion | bytes 16793600 | tf_op jit(solution)/shard_map/gather | solution.py:249
  761.9 12.0 convert_reduce_fusion
  785.5 79.7 %all-gather.5.cloned.1.call-done = bf16[1024,2,1024]{2,0,1:T(8,128)(2,1)} async-done(((bf16[256,2,1024]{2,0,1:T(8,128)(2,1)}), bf16[1024,2,1024]{2,0,1:T(8,128)(2,1)}) %all-gather.5.cloned.1.call-update) | async-done | bytes 4194320 | tf_op jit(solution)/shard_map/all_gather | solution.py:253
  873.3 13.7 fusion.97
  887.0 15.6 fusion.96
  912.0 15.5 fusion.100
  927.5 13.4 fusion.101
  962.0 15.7 fusion.98
  977.7 13.7 fusion.119
  991.4 15.5 fusion.102
  1007.0 13.5 fusion.117
  1031.1 19.2 fusion.17
  1063.7 12.2 fusion.68
  1075.9 11.2 convert_bitcast_fusion.1
  1097.3 133.3 %all_to_all.20 = bf16[32,160,1024]{2,1,0:T(8,128)(2,1)S(1)} all-to-all(bf16[32,160,1024]{2,1,0:T(8,128)(2,1)} %bitcast.429), channel_id=1, replica_groups=mesh['heads'=4,'experts'=8] {'experts'}, dimensions={0} | all-to-all | bytes 20971520 | tf_op jit(solution)/shard_map/all_to_all | solution.py:200
  1235.4 26.3 %gather_fusion.4 = bf16[4096,1024]{1,0:T(8,128)(2,1)} fusion(bf16[5121,1024]{1,0:T(8,128)(2,1)} %concatenate.52, s32[4096]{0:T(1024)S(1)} %copy-done.12), kind=kCustom, calls=%fused_computation.4 | custom fusion | bytes 16793600 | tf_op jit(solution)/shard_map/gather | solution.py:204
  1288.9 13.1 all-reduce.4
  1312.1 800.7 %all-reduce.13.cloned.1.call-done = (f32[4,1024,1024]{2,1,0:T(8,128)}, f32[4,512,1024]{2,1,0:T(8,128)}) async-done(((f32[4,1024,1024]{2,1,0:T(8,128)}, f32[4,512,1024]{2,1,0:T(8,128)}), (f32[4,1024,1024]{2,1,0:T(8,128)}, f32[4,512,1024]{2,1,0:T(8,128)})) %all-reduce.13.cloned.1.call-update) | async-done | bytes 25165840 | tf_op jit(solution)/shard_map/psum | solution.py:349
  2121.3 12.9 copy.269
  (336 shorter events, 262.1 us)
Async XLA Ops:
  7.2 121.4 %copy-start = (bf16[256,1024]{1,0:T(8,128)(2,1)S(1)}, bf16[256,1024]{1,0:T(8,128)(2,1)}, u32[]{:S(2)}) copy-start(bf16[256,1024]{1,0:T(8,128)(2,1)} %param.24) | copy-start | bytes 1572868
  7.2 93.0 %copy-start.40 = (bf16[1024,256]{1,0:T(8,128)(2,1)S(1)}, bf16[1024,256]{1,0:T(8,128)(2,1)}, u32[]{:S(2)}) copy-start(bf16[1024,256]{1,0:T(8,128)(2,1)} %param.21) | copy-start | bytes 1572868
  7.2 89.0 %all-gather.3.cloned.1.call-start = ((), (), s32[]{:S(2)}) async-start(), calls=%async_computation.6 | async-start | bytes 5242880 | tf_op jit(solution)/shard_map/all_gather | solution.py:112
  12.6 263.8 %reduce-scatter.3.cloned.1.call-start = ((), (), s32[]{:S(2)}) async-start(), calls=%async_computation.7 | async-start | bytes 10485760 | tf_op jit(solution)/shard_map/reduce_scatter | solution.py:167
  16.5 87.4 %copy-start.26 = (f32[1024,32]{0,1:T(8,128)}, f32[1024,32]{0,1:T(8,128)S(1)}, u32[]{:S(2)}) copy-start(f32[1024,32]{0,1:T(8,128)S(1)} %get-tuple-element.77) | copy-start | bytes 393220
  104.0 19.3 copy-start.13
  104.0 19.3 copy-start.15
  104.1 19.2 copy-start.37
  108.9 17.2 copy-start.18
  153.4 132.9 %copy-start.55 = (f32[1024]{0:T(1024)S(1)}, f32[1024]{0:T(1024)}, u32[]{:S(2)}) copy-start(f32[1024]{0:T(1024)} %param.20) | copy-start | bytes 12292
  279.4 31.2 %copy-start.58 = (f32[256,2]{0,1:T(2,128)}, f32[256,2]{0,1:T(2,128)S(1)}, u32[]{:S(2)}) copy-start(f32[256,2]{0,1:T(2,128)S(1)} %fusion.184) | copy-start | bytes 6148
  310.6 21.5 %copy-start.17 = (bf16[256,2,1024]{2,1,0:T(2,128)(2,1)S(1)}, bf16[256,2,1024]{2,1,0:T(2,128)(2,1)}, u32[]{:S(2)}) copy-start(bf16[256,2,1024]{2,1,0:T(2,128)(2,1)} %param.27) | copy-start | bytes 3145732
  310.6 121.8 %all-to-all-start = ((bf16[32,160,1024]{2,1,0:T(8,128)(2,1)}), bf16[32,160,1024]{2,1,0:T(8,128)(2,1)}, u32[]{:S(2)}, u32[]{:S(2)}) async-start(bf16[32,160,1024]{2,1,0:T(8,128)(2,1)} %bitcast.426), calls=%async_computation.1 | async-start | bytes 20971520 | tf_op jit(solution)/shard_map/all_to_all | solution.py:188
  432.5 122.2 %all-to-all-start.2 = ((bf16[32,160,1024]{2,1,0:T(8,128)(2,1)}), bf16[32,160,1024]{2,1,0:T(8,128)(2,1)}, u32[]{:S(2)}, u32[]{:S(2)}) async-start(bf16[32,160,1024]{2,1,0:T(8,128)(2,1)} %multiply_convert_fusion), calls=%async_computation.3 | async-start | bytes 20971520 | tf_op jit(solution)/shard_map/all_to_all | solution.py:216
  603.9 121.8 %all-to-all-start.3 = ((bf16[32,160,1024]{2,1,0:T(8,128)(2,1)}), bf16[32,160,1024]{2,1,0:T(8,128)(2,1)}, u32[]{:S(2)}, u32[]{:S(2)}) async-start(bf16[32,160,1024]{2,1,0:T(8,128)(2,1)} %bitcast.427), calls=%async_computation.4 | async-start | bytes 20971520 | tf_op jit(solution)/shard_map/all_to_all | solution.py:239
  609.2 255.9 %all-gather.5.cloned.1.call-start = ((), (), s32[]{:S(2)}) async-start(), calls=%async_computation.8 | async-start | bytes 5242880 | tf_op jit(solution)/shard_map/all_gather | solution.py:253
  609.5 126.3 %copy-start.11 = (s32[4096]{0:T(1024)}, s32[4096]{0:T(1024)S(1)}, u32[]{:S(2)}) copy-start(s32[4096]{0:T(1024)S(1)} %broadcast_clamp_fusion) | copy-start | bytes 49156
  761.9 19.1 copy-start.77
  777.7 90.9 %copy-start.19 = (bf16[1024,2,128]{0,2,1:T(8,128)(2,1)S(1)}, bf16[1024,2,128]{0,2,1:T(8,128)(2,1)}, u32[]{:S(2)}) copy-start(bf16[1024,2,128]{0,2,1:T(8,128)(2,1)} %copy-done.18) | copy-start | bytes 1572868
  785.3 88.1 %copy-start.47 = (bf16[512,2,2,64]{0,3,2,1:T(8,128)(2,1)S(1)}, bf16[512,2,2,64]{0,3,2,1:T(8,128)(2,1)}, u32[]{:S(2)}) copy-start(bf16[512,2,2,64]{0,3,2,1:T(8,128)(2,1)} %copy-done.46) | copy-start | bytes 786436
  785.3 490.1 %reduce-scatter.5.cloned.1.call-start = ((), (), s32[]{:S(2)}) async-start(), calls=%async_computation.9 | async-start | bytes 10485760 | tf_op jit(solution)/shard_map/reduce_scatter | solution.py:334
  1007.0 16.1 copy-start.34
  1007.0 16.5 copy-start.41
  1031.0 281.1 %all-reduce.11.cloned.1.call-start = ((), (), s32[]{:S(2)}) async-start(), calls=%async_computation.10 | async-start | bytes 6291456 | tf_op jit(solution)/shard_map/psum | solution.py:345
  1063.6 1049.2 %all-reduce.13.cloned.1.call-start = ((), (), s32[]{:S(2)}) async-start(), calls=%async_computation.11 | async-start | bytes 50331648 | tf_op jit(solution)/shard_map/psum | solution.py:349
  1235.4 26.3 %copy-start.33 = (f32[256,2,8]{2,1,0:T(2,128)S(1)}, f32[256,2,8]{2,1,0:T(2,128)}, u32[]{:S(2)}) copy-start(f32[256,2,8]{2,1,0:T(2,128)} %copy-done.32) | copy-start | bytes 49156
  1261.8 16.3 copy-start.75
  1261.8 16.3 copy-start.7
  1261.8 16.3 copy-start.57
  1261.8 16.3 copy-start.60
  1261.8 16.3 copy-start.79
  2121.3 16.4 copy-start.1
  (67 other events, 518.4 us)
Sparse Core Ops, SparseCore 0:
  12.8 83.4 all-gather.2
  133.4 142.9 reduce-scatter.2
  785.4 79.7 all-gather.4
  1031.2 143.0 reduce-scatter.4
  1178.2 96.5 all-reduce.10
  1278.1 834.6 all-reduce.12
where the time goes:
time: 2150 us; the launch traced here: 2140 us
  waiting for transfers between devices  1340 us (62%)
  matrix products  305 us (14%)
  local copies, waits for them, and re-layouts  232 us (11%)
  blocking collectives  157 us (7%)
  other arithmetic  83.1 us (4%)
    psum x1, waiting for transfers between devices, body(): lax.psum((grad_in, grad_down, summed[4], summed[5]), 'heads')  801 us
    all_to_all x1, blocking collectives, body(): lax.all_to_all(result_rows, 'experts', split_axis=0, concat_axis=0, tiled...  133 us
    all_to_all x1, waiting for transfers between devices, body(): lax.all_to_all(d_rows.reshape(src_total * exp_local, capacity, width), 'e...  116 us
    reduce_scatter x1, waiting for transfers between devices, body(): lax.psum_scatter(jnp.einsum('gwm,mr->gwr', head_result, output_matrix, pr...  106 us
    all_to_all x1, waiting for transfers between devices, body(): lax.all_to_all(d_send.reshape(EXPERTS, capacity, width), 'experts', split...  96.4 us
    all_gather x1, waiting for transfers between devices, body(): path_combined = lax.all_gather(d_branch, 'heads', axis=0, tiled=True)  79.7 us
    all_gather x1, waiting for transfers between devices, body(): lax.all_gather(attention_input, 'heads', axis=0, tiled=True)  77.3 us
    dot_general x4, matrix products, body(): jnp.einsum('grqk,kgd->qgrd', raw_grad, key_rotated[:, member], preferred_...  62.4 us
  transfers between devices with their start and end apart: 9, of which 7 were waited for; matrix products, arithmetic and copies ran while one was open for 11% of the time, Pallas kernels for 0%

commit v1 on v0

v1 whole, which is shorter than its diff:
```python
import functools
import math

import jax
import jax.numpy as jnp
from jax import lax
from jax.experimental import pallas as pl
from jax.experimental.pallas import tpu as pltpu
from jax.sharding import PartitionSpec as P

HEAD = 64
EXPERTS = 32
EPS = 1e-06
BF = jnp.bfloat16
F32 = jnp.float32
SCALE = HEAD ** (-0.5)
NEG = -1e30
VMEM = 60 * 1024 * 1024


def dot(a, b):
    return jnp.dot(a, b, preferred_element_type=F32)


def dot_nt(a, b):
    return lax.dot_general(a, b, (((1,), (1,)), ((), ())), preferred_element_type=F32)


def dot_tn(a, b):
    return lax.dot_general(a, b, (((0,), (0,)), ((), ())), preferred_element_type=F32)


def params(n):
    return pltpu.CompilerParams(
        dimension_semantics=("arbitrary",) * n, vmem_limit_bytes=VMEM
    )


def swap_halves(v):
    lane = lax.broadcasted_iota(jnp.int32, v.shape, 1)
    return jnp.where(lane % 64 < 32, pltpu.roll(v, 96, 1), pltpu.roll(v, 32, 1))


def attn_mask(offset, n, block, length):
    key = lax.broadcasted_iota(jnp.int32, (n, 2 * block), 0)
    query = lax.broadcasted_iota(jnp.int32, (n, 2 * block), 1)
    query = jnp.where(query >= block, query - block, query) + offset
    return (key <= query) & (key < length)


def two_heads(v):
    return jnp.concatenate([v[:, :HEAD], v[:, HEAD:]], axis=0)


def untwo(vt, block):
    return jnp.concatenate([vt[:, :block], vt[:, block:]], axis=0).T


def fwd_kernel(len_ref, x_ref, w_ref, cq, sq, ckv, skv, qkv_ref, head_ref, lse_ref):
    nh, _, seg, width = x_ref.shape
    full = nh * seg
    block = seg
    length = len_ref[pl.program_id(0)]
    lin = dot(x_ref[...].reshape(full, width), w_ref[0])
    ql, kvl = lin[:, :128], lin[:, 128:]
    q = (ql * cq[...] + swap_halves(ql) * sq[...]).astype(BF)
    kvr = kvl * ckv[...] + swap_halves(kvl) * skv[...]
    kv = kvr.astype(BF)
    qkv_ref[0, 0, :, :128] = q
    qkv_ref[0, 0, :, 128:] = kv
    k = kv[:, :HEAD]
    vt = kvr.T[HEAD:].astype(BF)
    for i in range(nh):
        n = (i + 1) * block
        q2 = two_heads(q[i * block : n])
        s = dot_nt(k[:n], q2)
        s = jnp.where(attn_mask(i * block, n, block, length), s * SCALE, NEG)
        m = jnp.max(s, axis=0, keepdims=True)
        e = jnp.exp(s - m)
        total = jnp.sum(e, axis=0, keepdims=True)
        p = (e * (1.0 / total)).astype(BF)
        lse_ref[0, 0, i : i + 1, :] = m + jnp.log(total)
        head_ref[i, 0] = untwo(dot(vt[:, :n], p), block).astype(BF)


def attn_forward(x, w, lengths, tables):
    nh, nseq, seg, width = x.shape
    groups = w.shape[0]
    full = nh * seg
    cq, sq, ckv, skv = tables
    tab = pl.BlockSpec((full, 128), lambda s, g: (0, 0))
    return pl.pallas_call(
        fwd_kernel,
        grid=(nseq, groups),
        in_specs=[
            pl.BlockSpec(memory_space=pltpu.SMEM),
            pl.BlockSpec((nh, 1, seg, width), lambda s, g: (0, s, 0, 0)),
            pl.BlockSpec((1, width, 256), lambda s, g: (g, 0, 0)),
            tab,
            tab,
            tab,
            tab,
        ],
        out_specs=[
            pl.BlockSpec((1, 1, full, 256), lambda s, g: (s, g, 0, 0)),
            pl.BlockSpec((nh, 1, seg, 128), lambda s, g: (0, s, 0, g)),
            pl.BlockSpec((1, 1, nh, 2 * seg), lambda s, g: (s, g, 0, 0)),
        ],
        out_shape=[
            jax.ShapeDtypeStruct((nseq, groups, full, 256), BF),
            jax.ShapeDtypeStruct((nh, nseq, seg, groups * 128), BF),
            jax.ShapeDtypeStruct((nseq, groups, nh, 2 * seg), F32),
        ],
        compiler_params=params(2),
        cost_estimate=pl.CostEstimate(flops=6 * 10**9, bytes_accessed=12 * 2**20, transcendentals=10**7),
        name="attn_forward",
    )(lengths, x, w, cq, sq, ckv, skv)


def bwd_kernel(len_ref, qkv_ref, do_ref, lse_ref, cq, sq, ckv, skv, out_ref, dkv_ref):
    nh, _, seg, _ = do_ref.shape
    full = nh * seg
    block = seg
    length = len_ref[pl.program_id(0)]
    q = qkv_ref[0, 0, :, :128]
    kv = qkv_ref[0, 0, :, 128:]
    k, v = kv[:, :HEAD], kv[:, HEAD:]
    kt = kv.astype(F32).T[:HEAD].astype(BF)
    dkv_ref[...] = jnp.zeros_like(dkv_ref)
    for i in range(nh):
        n = (i + 1) * block
        rows = pl.ds(i * block, block)
        q2 = two_heads(q[i * block : n])
        do2 = two_heads(do_ref[i, 0])
        s = dot_nt(k[:n], q2)
        p = jnp.exp(
            jnp.where(
                attn_mask(i * block, n, block, length),
                s * SCALE - lse_ref[0, 0, i : i + 1, :],
                NEG,
            )
        )
        dp = dot_nt(v[:n], do2)
        delta = jnp.sum(p * dp, axis=0, keepdims=True)
        ds = (p * (dp - delta) * SCALE).astype(BF)
        dkv_ref[:n, :HEAD] += dot(ds, q2)
        dkv_ref[:n, HEAD:] += dot(p.astype(BF), do2)
        dq = untwo(dot(kt[:, :n], ds), block)
        dq = dq * cq[rows, :] - swap_halves(dq) * sq[rows, :]
        out_ref[i, 0, :, :128] = dq.astype(BF)
    dkv = dkv_ref[...]
    dkv = (dkv * ckv[...] - swap_halves(dkv) * skv[...]).astype(BF)
    for i in range(nh):
        out_ref[i, 0, :, 128:] = dkv[i * block : (i + 1) * block]


def attn_backward(qkv, d_head, lse, lengths, tables):
    nseq, groups, full, _ = qkv.shape
    nh, _, seg, _ = d_head.shape
    cq, sq, ckv, skv = tables
    tab = pl.BlockSpec((full, 128), lambda s, g: (0, 0))
    return pl.pallas_call(
        bwd_kernel,
        grid=(nseq, groups),
        in_specs=[
            pl.BlockSpec(memory_space=pltpu.SMEM),
            pl.BlockSpec((1, 1, full, 256), lambda s, g: (s, g, 0, 0)),
            pl.BlockSpec((nh, 1, seg, 128), lambda s, g: (0, s, 0, g)),
            pl.BlockSpec((1, 1, nh, 2 * seg), lambda s, g: (s, g, 0, 0)),
            tab,
            tab,
            tab,
            tab,
        ],
        out_specs=pl.BlockSpec((nh, 1, seg, 256), lambda s, g: (0, s, 0, g)),
        out_shape=jax.ShapeDtypeStruct((nh, nseq, seg, groups * 256), BF),
        scratch_shapes=[pltpu.VMEM((full, 128), F32)],
        compiler_params=params(2),
        cost_estimate=pl.CostEstimate(flops=12 * 10**9, bytes_accessed=8 * 2**20, transcendentals=10**7),
        name="attn_backward",
    )(lengths, qkv, d_head, lse, cq, sq, ckv, skv)


def rotary_tables(length):
    half = HEAD // 2
    frequency = jnp.exp(jnp.arange(half, dtype=F32) * (-2.0 * math.log(10000.0) / HEAD))
    angles = jnp.arange(length, dtype=F32)[:, None] * frequency[None, :]
    cos, sin = jnp.cos(angles), jnp.sin(angles)
    c1 = jnp.concatenate([cos, cos], axis=1)
    s1 = jnp.concatenate([-sin, sin], axis=1)
    cq = jnp.concatenate([c1, c1], axis=1)
    sq = jnp.concatenate([s1, s1], axis=1)
    ckv = jnp.concatenate([c1, jnp.ones_like(c1)], axis=1)
    skv = jnp.concatenate([s1, jnp.zeros_like(s1)], axis=1)
    return cq, sq, ckv, skv


def pick_rows(slots, cap):
    tokens = slots.shape[1]
    index = lax.broadcasted_iota(jnp.int32, (cap, tokens), 0)
    return [index == slots[j : j + 1, :] for j in range(slots.shape[0])]


def gather_kernel(weighted, slot_ref, *refs):
    if weighted:
        weight_ref, tok_ref, out_ref = refs
    else:
        tok_ref, out_ref = refs[0], refs[-1]
    cap = out_ref.shape[2]
    hits = pick_rows(slot_ref[0], cap)
    rows = dot(jnp.concatenate([h.astype(F32) for h in hits], axis=0).astype(BF), tok_ref[0])
    for j, hit in enumerate(hits):
        part = rows[j * cap : (j + 1) * cap]
        if weighted:
            part = part * jnp.sum(jnp.where(hit, weight_ref[0, j : j + 1, :], 0.0), axis=1, keepdims=True)
        out_ref[j, 0] = part.astype(BF)


def gather_rows(slots, weights, tokens, cap):
    sources, here, count = slots.shape
    width = tokens.shape[-1]
    small = pl.BlockSpec((1, here, count), lambda s: (s, 0, 0))
    weighted = weights is not None
    return pl.pallas_call(
        functools.partial(gather_kernel, weighted),
        grid=(sources,),
        in_specs=[small] + [small] * weighted + [pl.BlockSpec((1, count, width), lambda s: (s, 0, 0))],
        out_specs=pl.BlockSpec((here, 1, cap, width), lambda s: (0, s, 0, 0)),
        out_shape=jax.ShapeDtypeStruct((here, sources, cap, width), BF),
        compiler_params=params(1),
        cost_estimate=pl.CostEstimate(
            flops=2 * sources * here * cap * count * width,
            bytes_accessed=2 * sources * width * (count + here * cap),
            transcendentals=0,
        ),
        name="gather_rows",
    )(*([slots] + [weights] * weighted + [tokens]))


def expert_kernel(steps, slot_ref, weight_ref, x_ref, d_ref, win_ref, wdown_ref,
                  out_ref, drow_ref, gin_ref, gdown_ref, hid_ref, dgu_ref, *acc):
    _, sources, cap, width = x_ref.shape
    ff = wdown_ref.shape[1]
    per = 2 if sources % 2 == 0 else 1
    win, wdown = win_ref[0], wdown_ref[0]
    for c in range(sources // per):
        rows = slice(c * per * cap, (c + 1) * per * cap)
        x = x_ref[0, c * per : (c + 1) * per].reshape(per * cap, width)
        d = d_ref[0, c * per : (c + 1) * per].reshape(per * cap, width)
        gu = dot(x, win)
        gate, up = gu[:, :ff], gu[:, ff:]
        sig = 1.0 / (1.0 + jnp.exp(-gate))
        act = gate * sig
        hidden = (act * up).astype(BF)
        hid_ref[rows, :] = hidden
        result = dot(hidden, wdown).astype(BF).astype(F32)
        for b in range(per):
            hit = pick_rows(slot_ref[c * per + b, 0], cap)[0]
            w = jnp.sum(jnp.where(hit, weight_ref[c * per + b, 0], 0.0), axis=1, keepdims=True)
            out_ref[0, c * per + b] = (result[b * cap : (b + 1) * cap] * w).astype(BF)
        dh = dot_nt(d, wdown)
        dgu_ref[rows, :ff] = (dh * up * (sig * (1.0 + gate * (1.0 - sig)))).astype(BF)
        dgu_ref[rows, ff:] = (dh * act).astype(BF)
        drow = dot_nt(dgu_ref[rows, :], win).astype(BF)
        for b in range(per):
            drow_ref[0, c * per + b] = drow[b * cap : (b + 1) * cap]
    x = x_ref[0].reshape(sources * cap, width)
    d = d_ref[0].reshape(sources * cap, width)
    gin = dot_tn(x, dgu_ref[...])
    gdown = dot_tn(hid_ref[...], d)
    if steps == 1:
        gin_ref[0] = gin.astype(BF)
        gdown_ref[0] = gdown.astype(BF)
    else:
        ain, adown = acc
        step = pl.program_id(1)

        @pl.when(step == 0)
        def _():
            ain[...] = jnp.zeros_like(ain)
            adown[...] = jnp.zeros_like(adown)

        ain[...] += gin
        adown[...] += gdown

        @pl.when(step == steps - 1)
        def _():
            gin_ref[0] = ain[...].astype(BF)
            gdown_ref[0] = adown[...].astype(BF)


def experts_call(first, count, slots, weights, x, d, win, wdown):
    _, sources, cap, width = x.shape
    tokens = slots.shape[-1]
    ff = wdown.shape[1]
    chunk = min(sources, 8)
    steps = sources // chunk
    small = pl.BlockSpec((chunk, 1, 1, tokens), lambda j, r: (r, first + j, 0, 0))
    rows = pl.BlockSpec((1, chunk, cap, width), lambda j, r: (first + j, r, 0, 0))
    rows_out = pl.BlockSpec((1, chunk, cap, width), lambda j, r: (j, r, 0, 0))
    scratch = [pltpu.VMEM((chunk * cap, ff), BF), pltpu.VMEM((chunk * cap, 2 * ff), BF)]
    if steps > 1:
        scratch += [pltpu.VMEM((width, 2 * ff), F32), pltpu.VMEM((ff, width), F32)]
    shape = jax.ShapeDtypeStruct((count, sources, cap, width), BF)
    return pl.pallas_call(
        functools.partial(expert_kernel, steps),
        grid=(count, steps),
        in_specs=[
            small,
            small,
            rows,
            rows,
            pl.BlockSpec((1, width, 2 * ff), lambda j, r: (first + j, 0, 0)),
            pl.BlockSpec((1, ff, width), lambda j, r: (first + j, 0, 0)),
        ],
        out_specs=[
            rows_out,
            rows_out,
            pl.BlockSpec((1, width, 2 * ff), lambda j, r: (j, 0, 0)),
            pl.BlockSpec((1, ff, width), lambda j, r: (j, 0, 0)),
        ],
        out_shape=[
            shape,
            shape,
            jax.ShapeDtypeStruct((count, width, 2 * ff), BF),
            jax.ShapeDtypeStruct((count, ff, width), BF),
        ],
        scratch_shapes=scratch,
        compiler_params=params(2),
        cost_estimate=pl.CostEstimate(
            flops=2 * count * sources * cap * width * ff * 9,
            bytes_accessed=8 * count * sources * cap * width + 12 * count * width * ff,
            transcendentals=count * sources * cap * ff,
        ),
        name="experts",
    )(slots[:, :, None, :], weights[:, :, None, :], x, d, win, wdown)


def combine_kernel(parts, slot_ref, *refs):
    row_refs, out_refs = refs[: 2 * parts], refs[2 * parts :]
    slots = slot_ref[0]
    count, here = slots.shape
    cap = row_refs[0].shape[2]
    lane = lax.broadcasted_iota(jnp.int32, (count, here * cap), 1)
    hot = None
    for j in range(here):
        col = slots[:, j : j + 1]
        hit = lane == jnp.where(col >= 0, col + j * cap, -1)
        hot = hit if hot is None else hot | hit
    hot = hot.astype(F32).astype(BF)
    for group, out_ref in zip((row_refs[:parts], row_refs[parts:]), out_refs):
        rows = jnp.concatenate([r[j, 0] for r in group for j in range(r.shape[0])], axis=0)
        out_ref[0] = dot(hot, rows).astype(BF)


def combine(slots_t, outs, drows):
    sources, count, here = slots_t.shape
    _, _, cap, width = outs[0].shape
    blocks = [pl.BlockSpec((o.shape[0], 1, cap, width), lambda s: (0, s, 0, 0)) for o in outs]
    shape = jax.ShapeDtypeStruct((sources, count, width), BF)
    spec = pl.BlockSpec((1, count, width), lambda s: (s, 0, 0))
    return pl.pallas_call(
        functools.partial(combine_kernel, len(outs)),
        grid=(sources,),
        in_specs=[pl.BlockSpec((1, count, here), lambda s: (s, 0, 0))] + blocks + blocks,
        out_specs=[spec, spec],
        out_shape=[shape, shape],
        compiler_params=params(1),
        cost_estimate=pl.CostEstimate(
            flops=4 * sources * here * cap * count * width,
            bytes_accessed=4 * sources * width * (count + here * cap),
            transcendentals=0,
        ),
        name="combine",
    )(slots_t, *outs, *drows)


def swap(x, bit, n):
    return lax.ppermute(x, "experts", [(i, i ^ bit) for i in range(n)])


def plane_gather(x, n):
    if n != 8:
        whole = lax.all_gather(x, "experts", axis=0)
        order = lax.axis_index("experts") ^ jnp.arange(n, dtype=jnp.int32)
        return whole[order]
    got = {0: x}
    for r in (2, 4, 6):
        got[r] = swap(x, r, n)
    for r in (0, 2, 4, 6):
        got[r + 1] = swap(got[r], 1, n)
    return jnp.stack([got[r] for r in range(n)], axis=0)


def plane_scatter(parts, n):
    if n != 8:
        order = lax.axis_index("experts") ^ jnp.arange(n, dtype=jnp.int32)
        return lax.psum_scatter(parts[order].astype(F32), "experts", scatter_dimension=0)
    odd = swap(parts[1::2], 1, n)
    both = [parts[2 * i].astype(F32) + odd[i].astype(F32) for i in range(4)]
    total = both[0]
    for i in (1, 2, 3):
        total = total + swap(both[i].astype(BF), 2 * i, n).astype(F32)
    return total


def heads_sum(x, z, nh):
    if nh != 4:
        return lax.psum(x.astype(F32), "heads")
    first = lax.ppermute(x, "heads", [(0, 1), (3, 2)])
    pair = (x.astype(F32) + first.astype(F32)).astype(BF)
    second = lax.ppermute(pair, "heads", [(1, 2), (2, 1)])
    total = (pair.astype(F32) + second.astype(F32)).astype(BF)
    third = lax.ppermute(total, "heads", [(1, 0), (2, 3)])
    return jnp.where((z == 1) | (z == 2), total, third).astype(F32)


def body(layer_input, seq_lengths, expert_ids, route_weight, priority, attn_gain, moe_gain,
         query_matrix, key_matrix, value_matrix, output_matrix, expert_in, expert_down, out_grad):
    seg, nseq, width = layer_input.shape
    nh, ne = lax.axis_size("heads"), lax.axis_size("experts")
    z, me = lax.axis_index("heads"), lax.axis_index("experts")
    top = expert_ids.shape[-1]
    tokens = seg * nseq
    groups = key_matrix.shape[1] // HEAD
    here = expert_in.shape[0]
    cap = (5 * tokens * top + 4 * EXPERTS - 1) // (4 * EXPERTS)

    def local(v):
        return jnp.swapaxes(v, 0, 1).reshape((tokens,) + v.shape[2:])

    def unlocal(v):
        return jnp.swapaxes(v.reshape((nseq, seg) + v.shape[1:]), 0, 1)

    ids = local(expert_ids)
    order = local(priority)
    weight = local(route_weight)
    position = z * seg + jnp.arange(seg, dtype=jnp.int32)
    live = (position[None, :] < seq_lengths[:, None]).reshape(tokens)
    match = ids.T[:, None, :] == jnp.arange(EXPERTS, dtype=jnp.int32)[None, :, None]
    weight_e = jnp.sum(jnp.where(match, weight.T[:, None, :], 0.0), axis=0)
    chosen = jnp.any(match, axis=0) & live[None, :]
    earlier = (order[:, None] < order[None, :]).astype(BF)
    before = dot(chosen.astype(BF), earlier)
    slot = jnp.where(chosen & (before < cap), before, -1.0)
    packed = jnp.stack([slot.reshape(ne, here, tokens), weight_e.reshape(ne, here, tokens)], axis=1)
    packed = lax.all_to_all(packed, "experts", split_axis=0, concat_axis=0, tiled=True)
    packed = packed[me ^ jnp.arange(ne, dtype=jnp.int32)]
    slots = packed[:, 0].astype(jnp.int32)
    weights = packed[:, 1]

    xf = local(layer_input).astype(F32)
    inv_one = lax.rsqrt(jnp.mean(xf * xf, axis=-1, keepdims=True) + EPS)
    attn_in = (xf * inv_one * attn_gain).astype(BF)
    gathered = lax.all_gather(attn_in.reshape(nseq, seg, width), "heads", axis=0)

    wq = query_matrix.reshape(width, groups, 128)
    wk = key_matrix.reshape(width, groups, HEAD)
    wv = value_matrix.reshape(width, groups, HEAD)
    w_local = jnp.concatenate([wq, wk, wv], axis=2)
    w_groups = jnp.transpose(w_local, (1, 0, 2))
    rows_in = width // ne
    rows_out = output_matrix.shape[0] // ne
    w_piece = lax.dynamic_slice_in_dim(w_local.reshape(width, groups * 256), me * rows_in, rows_in, 0)
    o_piece = lax.dynamic_slice_in_dim(output_matrix, me * rows_out, rows_out, 0)
    o_full = lax.all_gather(o_piece, ("heads", "experts"), axis=0, tiled=True)
    w_full = lax.all_gather(w_piece, ("heads", "experts"), axis=0, tiled=True)
    w_full = w_full.reshape(nh, width, groups * 256)

    tables = rotary_tables(nh * seg)
    qkv, heads_out, lse = attn_forward(gathered, w_groups, seq_lengths, tables)
    heads_in = lax.all_to_all(heads_out, "heads", split_axis=0, concat_axis=0, tiled=True)
    heads_in = heads_in.reshape(nh, tokens, groups * 128)
    o_parts = o_full.reshape(nh, groups * 128, width)
    branch = jnp.einsum("ztm,zmw->tw", heads_in, o_parts, preferred_element_type=F32)
    mid = xf + branch
    inv_two = lax.rsqrt(jnp.mean(mid * mid, axis=-1, keepdims=True) + EPS)
    moe_in = (mid * inv_two * moe_gain).astype(BF)

    grad = local(out_grad)
    grads_all = plane_gather(grad, ne)
    d_rows = gather_rows(slots, weights, grads_all, cap)
    tokens_all = plane_gather(moe_in, ne)
    x_rows = gather_rows(slots, None, tokens_all, cap)
    outs, drows, gins, gdowns = [], [], [], []
    for j in range(here):
        o, dr, gi, gd = experts_call(j, 1, slots, weights, x_rows, d_rows, expert_in, expert_down)
        outs.append(o)
        drows.append(dr)
        gins.append(heads_sum(gi, z, nh))
        gdowns.append(heads_sum(gd, z, nh))
    grad_in = jnp.concatenate(gins, axis=0)
    grad_down = jnp.concatenate(gdowns, axis=0)
    moe_parts, d_parts = combine(jnp.swapaxes(slots, 1, 2), outs, drows)
    d_moe = plane_scatter(d_parts, ne)
    moe_sum = plane_scatter(moe_parts, ne)
    out = (mid + moe_sum).astype(BF)

    gf = grad.astype(F32)
    zed = moe_gain * d_moe
    d_mid = gf + inv_two * zed - mid * (inv_two ** 3 * jnp.mean(zed * mid, axis=-1, keepdims=True))
    gain_two = jnp.sum(d_moe * mid * inv_two, axis=0)
    d_branch = d_mid.astype(BF)
    d_heads = jnp.einsum("tw,zmw->ztm", d_branch, o_parts, preferred_element_type=F32).astype(BF)
    d_heads = d_heads.reshape(nh, nseq, seg, groups * 128)
    d_heads = lax.all_to_all(d_heads, "heads", split_axis=0, concat_axis=0, tiled=True)
    o_partial = jnp.einsum("ztm,tw->zmw", heads_in, d_branch, preferred_element_type=F32)
    o_grad = lax.psum_scatter(o_partial, "heads", scatter_dimension=0)
    o_grad = lax.psum(o_grad, "experts")

    dqkv = attn_backward(qkv, d_heads, lse, seq_lengths, tables)
    w_partial = jnp.einsum("zsrm,zsrc->mc", gathered, dqkv, preferred_element_type=F32)
    back = lax.all_to_all(dqkv, "heads", split_axis=0, concat_axis=0, tiled=True)
    back = back.reshape(nh, tokens, groups * 256)
    d_attn = jnp.einsum("ztc,zmc->tm", back, w_full, preferred_element_type=F32)
    w_grad = lax.psum(w_partial, "experts").reshape(width, groups, 256)
    wed = attn_gain * d_attn
    x_grad = d_mid + inv_one * wed - xf * (inv_one ** 3 * jnp.mean(wed * xf, axis=-1, keepdims=True))
    gain_one = jnp.sum(d_attn * xf * inv_one, axis=0)
    gain_one, gain_two = lax.psum((gain_one, gain_two), ("heads", "experts"))
    return (
        unlocal(out),
        unlocal(x_grad),
        gain_one,
        gain_two,
        w_grad[:, :, :128].reshape(query_matrix.shape),
        w_grad[:, :, 128:192].reshape(key_matrix.shape),
        w_grad[:, :, 192:].reshape(value_matrix.shape),
        o_grad,
        grad_in,
        grad_down,
    )


def solution(mesh):
    rows = P("heads", "experts", None)
    in_specs = (
        rows,
        P("experts"),
        rows,
        rows,
        P("heads", "experts"),
        P(),
        P(),
        P(None, "heads"),
        P(None, "heads"),
        P(None, "heads"),
        P("heads", None),
        P("experts", None, None),
        P("experts", None, None),
        rows,
    )
    out_specs = (
        rows,
        rows,
        P(),
        P(),
        P(None, "heads"),
        P(None, "heads"),
        P(None, "heads"),
        P("heads", None),
        P("experts", None, None),
        P("experts", None, None),
    )
    return jax.shard_map(body, mesh=mesh, in_specs=in_specs, out_specs=out_specs, check_vma=False)
```

time: 2150 us -> 1130 us (0.53)
  waiting for transfers between devices: 1340 us -> 573 us
  matrix products: 305 us -> 20.1 us
  Pallas kernels: 0 us -> 171 us
  local copies, waits for them, and re-layouts: 232 us -> 79.8 us
  blocking collectives: 157 us -> 37.7 us
  starting transfers between devices: 16.4 us -> 97.7 us
  other arithmetic: 83.1 us -> 121 us
    psum x2 -> x1, waiting for transfers between devices: 801 us -> 9.54 us  [body(): w_grad = lax.psum(w_partial, 'experts').reshape(width, groups, 256)]
    ppermute x0 -> x46, waiting for transfers between devices: none -> 335 us  [the longest x8 236 us: heads_sum(): first = lax.ppermute(x, 'heads', [(0, 1), (3, 2)])]
    dot_general x42 -> x6, matrix products: 305 us -> 20.1 us  [the longest x1 5.63 us: body(): d_attn = jnp.einsum('ztc,zmc->tm', back, w_full, preferred_element_type=F32)]
    pallas_call x0 -> x9, Pallas kernels: none -> 171 us  [the longest x4 81.2 us: experts_call(): pl.pallas_call(functools.partial(expert_kernel, steps), grid=(count, step...]
    all_to_all x1 -> x0, blocking collectives: 133 us -> none  [body(): lax.all_to_all(result_rows, 'experts', split_axis=0, concat_axis=0, tiled...]
    all_to_all x3 -> x4, waiting for transfers between devices: 272 us -> 150 us  [the longest x1 146 us: body(): lax.all_to_all(d_heads, 'heads', split_axis=0, concat_axis=0, tiled=True)]
    reduce_scatter x2 -> x1, waiting for transfers between devices: 106 us -> 0.01 us  [body(): o_grad = lax.psum_scatter(o_partial, 'heads', scatter_dimension=0)]
    gather x7 -> x1, local copies, waits for them, and re-layouts: 103 us -> 0.62 us  [body(): packed = packed[me ^ jnp.arange(ne, dtype=jnp.int32)]]
  transfers between devices with their start and end apart: 9 -> 55, of which waited for: 7 -> 19; matrix products, arithmetic and copies ran while one was open for 11% -> 18% of each run, Pallas kernels for 0% -> 15%
where the time goes in v1:
time: 1130 us; the launch traced here: 1110 us
  waiting for transfers between devices  573 us (51%)
  Pallas kernels  171 us (15%)
  other arithmetic  121 us (11%)
  starting transfers between devices  97.7 us (9%)
  local copies, waits for them, and re-layouts  79.8 us (7%)
  blocking collectives  37.7 us (3%)
  matrix products  20.1 us (2%)
  between operations  14.9 us (1%)
    ppermute x8, waiting for transfers between devices, heads_sum(): first = lax.ppermute(x, 'heads', [(0, 1), (3, 2)])  236 us
    all_to_all x1, waiting for transfers between devices, body(): lax.all_to_all(d_heads, 'heads', split_axis=0, concat_axis=0, tiled=True)  146 us
    pallas_call x4, Pallas kernels, experts_call(): pl.pallas_call(functools.partial(expert_kernel, steps), grid=(count, step...  81.2 us
    ppermute x22, waiting for transfers between devices, swap(): return lax.ppermute(x, 'experts', [(i, i ^ bit) for i in range(n)])  77.4 us
    all_gather x1, waiting for transfers between devices, body(): lax.all_gather(attn_in.reshape(nseq, seg, width), 'heads', axis=0)  55.9 us
    unnamed x93, local copies, waits for them, and re-layouts  43.1 us
    psum x1, blocking collectives, body(): gain_one, gain_two = lax.psum((gain_one, gain_two), ('heads', 'experts'))  37.7 us
    ppermute x8, starting transfers between devices, heads_sum(): first = lax.ppermute(x, 'heads', [(0, 1), (3, 2)])  32.4 us
  transfers between devices with their start and end apart: 55, of which 19 were waited for; matrix products, arithmetic and copies ran while one was open for 18% of the time, Pallas kernels for 15%

profile of v1, /device:TPU:0, one launch (start us, length us, event | category | flops | bytes accessed | tf_op | source)
XLA Modules:
  0.0 1114.7 jit_solution(12544483706897851932)
XLA Ops:
  39.2 55.9 %all-gather.9.cloned.1.call-done = bf16[8,256,1024]{2,1,0:T(8,128)(2,1)} async-done(((bf16[2,256,1024]{2,1,0:T(8,128)(2,1)}), bf16[8,256,1024]{2,1,0:T(8,128)(2,1)}) %all-gather.9.cloned.1.call-update) | async-done | bytes 4194320 | tf_op jit(solution)/shard_map/all_gather | solution.py:455
  95.2 20.5 %attn_forward.1 = (bf16[2,2,1024,256]{3,2,1,0:T(8,128)(2,1)}, bf16[4,2,256,256]{3,2,1,0:T(8,128)(2,1)}, f32[2,2,4,512]{3,2,1,0:T(4,128)}) custom-call(s32[2]{0:T(128)} %len_ref.3, bf16[4,2,256,1024]{3,2,1,0:T(8,128)(2,1)} %bitcast.208, bf16[2,1024,256]{2,1,0:T(8,128)(2,1)} %fusion.56.w_ref, f32[1024,128]{1,0:T(8,128)} %get-tuple-element.119.cq, ...), custom_call_target="tpu_custom_call" | custom-call | flops 6000000000 | bytes 12582912 | tf_op jit(solution)/shard_map/attn_forward/pallas_call | solution.py:92
  141.1 22.1 %all-gather.5.cloned.1.call-done = bf16[1024,1024]{1,0:T(8,128)(2,1)} async-done(((bf16[32,1024]{1,0:T(8,128)(2,1)}), bf16[1024,1024]{1,0:T(8,128)(2,1)}) %all-gather.5.cloned.1.call-update) | async-done | bytes 2097168 | tf_op jit(solution)/shard_map/all_gather | solution.py:466
  180.9 15.2 %collective-permute-done.1 = bf16[512,1024]{1,0:T(8,128)(2,1)} collective-permute-done((bf16[512,1024]{1,0:T(8,128)(2,1)}, bf16[512,1024]{1,0:T(8,128)(2,1)}, u32[]{:S(2)}, u32[]{:S(2)}) %collective-permute-start.1) | collective-permute-done | bytes 1048608 | tf_op jit(solution)/shard_map/ppermute | solution.py:379
  196.0 12.4 %gather_rows.3.d_ref = bf16[4,8,160,1024]{3,2,1,0:T(8,128)(2,1)} custom-call(s32[8,4,512]{2,1,0:T(4,128)} %copy.156.slot_ref, f32[8,4,512]{2,1,0:T(4,128)} %get-tuple-element.120.refs_0_, bf16[8,512,1024]{2,1,0:T(8,128)(2,1)} %bitcast_dynamic-update-slice_fusion.refs_1_), custom_call_target="tpu_custom_call" | custom-call | flops 5368709120 | bytes 18874368 | tf_op jit(solution)/shard_map/gather_rows/pallas_call | solution.py:224
  208.5 17.0 %collective-permute-done.3 = bf16[512,1024]{1,0:T(8,128)(2,1)} collective-permute-done((bf16[512,1024]{1,0:T(8,128)(2,1)}, bf16[512,1024]{1,0:T(8,128)(2,1)}, u32[]{:S(2)}, u32[]{:S(2)}) %collective-permute-start.3) | collective-permute-done | bytes 1048608 | tf_op jit(solution)/shard_map/ppermute | solution.py:379
  239.4 12.0 %gather_rows.2.x_ref = bf16[4,8,160,1024]{3,2,1,0:T(8,128)(2,1)} custom-call(s32[8,4,512]{2,1,0:T(4,128)} %copy.156.slot_ref, bf16[8,512,1024]{2,1,0:T(8,128)(2,1)} %bitcast_dynamic-update-slice_fusion.8.refs_0_), custom_call_target="tpu_custom_call" | custom-call | flops 5368709120 | bytes 18874368 | tf_op jit(solution)/shard_map/gather_rows/pallas_call | solution.py:224
  251.4 18.0 %experts.4 = (bf16[1,8,160,1024]{3,2,1,0:T(8,128)(2,1)}, bf16[1,8,160,1024]{3,2,1,0:T(8,128)(2,1)}, bf16[1,1024,1024]{2,1,0:T(8,128)(2,1)}, bf16[1,512,1024]{2,1,0:T(8,128)(2,1)}) custom-call(s32[8,4,1,512]{3,2,1,0:T(1,128)} %copy.160.slot_ref, f32[8,4,1,512]{3,2,1,0:T(1,128)} %bitcast.196, bf16[4,8,160,1024]{3,2,1,0:T(8,128)(2,1)} %gather_rows.2.x_ref, ...), custom_call_target="tpu_custom_call" | custom-call | flops 12079595520 | bytes 16777216 | tf_op jit(solution)/shard_map/experts/pallas_call | solution.py:305
  269.4 26.7 %experts.5 = (bf16[1,8,160,1024]{3,2,1,0:T(8,128)(2,1)}, bf16[1,8,160,1024]{3,2,1,0:T(8,128)(2,1)}, bf16[1,1024,1024]{2,1,0:T(8,128)(2,1)}, bf16[1,512,1024]{2,1,0:T(8,128)(2,1)}) custom-call(s32[8,4,1,512]{3,2,1,0:T(1,128)} %copy.160.slot_ref, f32[8,4,1,512]{3,2,1,0:T(1,128)} %bitcast.197, bf16[4,8,160,1024]{3,2,1,0:T(8,128)(2,1)} %gather_rows.2.x_ref, ...), custom_call_target="tpu_custom_call" | custom-call | flops 12079595520 | bytes 16777216 | tf_op jit(solution)/shard_map/experts/pallas_call | solution.py:305
  296.1 18.2 %experts.6 = (bf16[1,8,160,1024]{3,2,1,0:T(8,128)(2,1)}, bf16[1,8,160,1024]{3,2,1,0:T(8,128)(2,1)}, bf16[1,1024,1024]{2,1,0:T(8,128)(2,1)}, bf16[1,512,1024]{2,1,0:T(8,128)(2,1)}) custom-call(s32[8,4,1,512]{3,2,1,0:T(1,128)} %copy.160.slot_ref, f32[8,4,1,512]{3,2,1,0:T(1,128)} %bitcast.198, bf16[4,8,160,1024]{3,2,1,0:T(8,128)(2,1)} %gather_rows.2.x_ref, ...), custom_call_target="tpu_custom_call" | custom-call | flops 12079595520 | bytes 16777216 | tf_op jit(solution)/shard_map/experts/pallas_call | solution.py:305
  314.2 18.4 %experts.7 = (bf16[1,8,160,1024]{3,2,1,0:T(8,128)(2,1)}, bf16[1,8,160,1024]{3,2,1,0:T(8,128)(2,1)}, bf16[1,1024,1024]{2,1,0:T(8,128)(2,1)}, bf16[1,512,1024]{2,1,0:T(8,128)(2,1)}) custom-call(s32[8,4,1,512]{3,2,1,0:T(1,128)} %copy.160.slot_ref, f32[8,4,1,512]{3,2,1,0:T(1,128)} %bitcast.199, bf16[4,8,160,1024]{3,2,1,0:T(8,128)(2,1)} %gather_rows.2.x_ref, ...), custom_call_target="tpu_custom_call" | custom-call | flops 12079595520 | bytes 16777216 | tf_op jit(solution)/shard_map/experts/pallas_call | solution.py:305
  332.6 22.1 %combine.1 = (bf16[8,512,1024]{2,1,0:T(8,128)(2,1)}, bf16[8,512,1024]{2,1,0:T(8,128)(2,1)}) custom-call(s32[8,512,4]{2,1,0:T(8,128)} %get-tuple-element.115.slot_ref, bf16[1,8,160,1024]{3,2,1,0:T(8,128)(2,1)} %get-tuple-element.32.refs_0_, bf16[1,8,160,1024]{3,2,1,0:T(8,128)(2,1)} %get-tuple-element.33.refs_1_, ...), custom_call_target="tpu_custom_call" | custom-call | flops 10737418240 | bytes 37748736 | tf_op jit(solution)/shard_map/combine/pallas_call | solution.py:362
  368.5 20.7 %collective-permute-done.43 = bf16[1,512,1024]{2,1,0:T(8,128)(2,1)S(1)} collective-permute-done((bf16[1,512,1024]{2,1,0:T(8,128)(2,1)S(1)}, bf16[1,512,1024]{2,1,0:T(8,128)(2,1)S(1)}, u32[]{:S(2)}, u32[]{:S(2)}) %collective-permute-start.43) | collective-permute-done | bytes 1048608 | tf_op jit(solution)/shard_map/ppermute | solution.py:410
  395.0 16.6 %collective-permute-done.40 = bf16[1,512,1024]{2,1,0:T(8,128)(2,1)S(1)} collective-permute-done((bf16[1,512,1024]{2,1,0:T(8,128)(2,1)S(1)}, bf16[1,512,1024]{2,1,0:T(8,128)(2,1)S(1)}, u32[]{:S(2)}, u32[]{:S(2)}) %collective-permute-start.40) | collective-permute-done | bytes 1048608 | tf_op jit(solution)/shard_map/ppermute | solution.py:410
  414.7 19.4 %collective-permute-done.37 = bf16[1,512,1024]{2,1,0:T(8,128)(2,1)S(1)} collective-permute-done((bf16[1,512,1024]{2,1,0:T(8,128)(2,1)S(1)}, bf16[1,512,1024]{2,1,0:T(8,128)(2,1)S(1)}, u32[]{:S(2)}, u32[]{:S(2)}) %collective-permute-start.37) | collective-permute-done | bytes 1048608 | tf_op jit(solution)/shard_map/ppermute | solution.py:410
  443.8 12.1 %collective-permute-done.34 = bf16[1,512,1024]{2,1,0:T(8,128)(2,1)S(1)} collective-permute-done((bf16[1,512,1024]{2,1,0:T(8,128)(2,1)S(1)}, bf16[1,512,1024]{2,1,0:T(8,128)(2,1)S(1)}, u32[]{:S(2)}, u32[]{:S(2)}) %collective-permute-start.34) | collective-permute-done | bytes 1048608 | tf_op jit(solution)/shard_map/ppermute | solution.py:410
  458.2 6.6 copy.167
  488.6 18.0 %collective-permute-done.20 = bf16[512,1024]{1,0:T(8,128)(2,1)S(1)} collective-permute-done((bf16[512,1024]{1,0:T(8,128)(2,1)}, bf16[512,1024]{1,0:T(8,128)(2,1)S(1)}, u32[]{:S(2)}, u32[]{:S(2)}) %collective-permute-start.20) | collective-permute-done | bytes 1048608 | tf_op jit(solution)/shard_map/ppermute | solution.py:379
  521.1 8.1 collective-permute-done.17
  529.1 5.7 collective-permute-start.25
  534.9 15.1 %collective-permute-done.16 = bf16[512,1024]{1,0:T(8,128)(2,1)S(1)} collective-permute-done((bf16[512,1024]{1,0:T(8,128)(2,1)S(1)}, bf16[512,1024]{1,0:T(8,128)(2,1)S(1)}, u32[]{:S(2)}, u32[]{:S(2)}) %collective-permute-start.16) | collective-permute-done | bytes 1048608 | tf_op jit(solution)/shard_map/ppermute | solution.py:379
  551.6 7.4 collective-permute-start.22
  579.1 52.3 %collective-permute-done.28 = bf16[1,1024,1024]{2,1,0:T(8,128)(2,1)} collective-permute-done((bf16[1,1024,1024]{2,1,0:T(8,128)(2,1)}, bf16[1,1024,1024]{2,1,0:T(8,128)(2,1)}, u32[]{:S(2)}, u32[]{:S(2)}) %collective-permute-start.28) | collective-permute-done | bytes 2097184 | tf_op jit(solution)/shard_map/ppermute | solution.py:410
  637.2 77.5 %collective-permute-done.25 = bf16[1,1024,1024]{2,1,0:T(8,128)(2,1)} collective-permute-done((bf16[1,1024,1024]{2,1,0:T(8,128)(2,1)}, bf16[1,1024,1024]{2,1,0:T(8,128)(2,1)}, u32[]{:S(2)}, u32[]{:S(2)}) %collective-permute-start.25) | collective-permute-done | bytes 2097184 | tf_op jit(solution)/shard_map/ppermute | solution.py:410
  720.7 37.7 %collective-permute-done.22 = bf16[1,1024,1024]{2,1,0:T(8,128)(2,1)} collective-permute-done((bf16[1,1024,1024]{2,1,0:T(8,128)(2,1)}, bf16[1,1024,1024]{2,1,0:T(8,128)(2,1)}, u32[]{:S(2)}, u32[]{:S(2)}) %collective-permute-start.22) | collective-permute-done | bytes 2097184 | tf_op jit(solution)/shard_map/ppermute | solution.py:410
  781.1 8.1 all-to-all-start.2
  820.1 146.3 %all-to-all-done.2.do_ref = bf16[4,2,256,256]{3,2,1,0:T(8,128)(2,1)} async-done(((bf16[4,2,256,256]{3,2,1,0:T(8,128)(2,1)}), bf16[4,2,256,256]{3,2,1,0:T(8,128)(2,1)}, u32[]{:S(2)}, u32[]{:S(2)}) %all-to-all-start.2) | async-done | bytes 1048608 | tf_op jit(solution)/shard_map/all_to_all | solution.py:506
  966.4 22.4 %attn_backward.1 = bf16[4,2,256,512]{3,2,1,0:T(8,128)(2,1)} custom-call(s32[2]{0:T(128)} %len_ref.3, bf16[2,2,1024,256]{3,2,1,0:T(8,128)(2,1)} %get-tuple-element.42.qkv_ref, bf16[4,2,256,256]{3,2,1,0:T(8,128)(2,1)} %all-to-all-done.2.do_ref, f32[2,2,4,512]{3,2,1,0:T(4,128)} %get-tuple-element.43.lse_ref, f32[1024,128]{1,0:T(8,128)} %get-tuple-element.119.cq, ...), custom_call_target="tpu_custom_call" | custom-call | flops 12000000000 | bytes 8388608 | tf_op jit(solution)/shard_map/attn_backward/pallas_call | solution.py:162
  1003.0 21.5 %collective-permute-done.24 = bf16[1,1024,1024]{2,1,0:T(8,128)(2,1)} collective-permute-done((bf16[1,1024,1024]{2,1,0:T(8,128)(2,1)}, bf16[1,1024,1024]{2,1,0:T(8,128)(2,1)}, u32[]{:S(2)}, u32[]{:S(2)}) %collective-permute-start.24) | collective-permute-done | bytes 2097184 | tf_op jit(solution)/shard_map/ppermute | solution.py:414
  1031.6 9.6 maximum_convert_fusion
  1054.1 37.7 %all-reduce = (f32[1024]{0:T(1024)}, f32[1024]{0:T(1024)}) all-reduce(f32[1024]{0:T(1024)S(1)} %get-tuple-element.94, f32[1024]{0:T(1024)S(1)} %get-tuple-element.92), channel_id=1, replica_groups=mesh['heads'=4,'experts'=8] {'heads','experts'}, use_global_device_ids=true, to_apply=%region_7.8 | all-reduce | flops 2048 | bytes 16384 | tf_op jit(solution)/shard_map/psum | solution.py:520
  1091.8 9.5 all-reduce.4.cloned.1.call-done
  (271 shorter events, 289.0 us)
Async XLA Ops:
  7.2 87.9 %all-gather.9.cloned.1.call-start = ((), (), s32[]{:S(2)}) async-start(), calls=%async_computation.8 | async-start | bytes 5242880 | tf_op jit(solution)/shard_map/all_gather | solution.py:455
  11.5 151.6 %all-gather.5.cloned.1.call-start = ((), (), s32[]{:S(2)}) async-start(), calls=%async_computation.5 | async-start | bytes 2162688 | tf_op jit(solution)/shard_map/all_gather | solution.py:466
  12.6 121.7 %collective-permute-start.7 = (bf16[512,1024]{1,0:T(8,128)(2,1)S(1)}, bf16[512,1024]{1,0:T(8,128)(2,1)}, u32[]{:S(2)}, u32[]{:S(2)}) collective-permute-start(bf16[512,1024]{1,0:T(8,128)(2,1)S(1)} %bitcast.174), channel_id=1, source_target_pairs={{0,1},{1,0},{2,3},{3,2},{4,5},{5,4},{6,7},{7,6},{8,9},{9,8},{10,11... | collective-permute-start | bytes 3145736 | tf_op jit(solution)/shard_map/ppermute | solution.py:379
  13.1 108.8 %collective-permute-start.8 = (bf16[512,1024]{1,0:T(8,128)(2,1)S(1)}, bf16[512,1024]{1,0:T(8,128)(2,1)}, u32[]{:S(2)}, u32[]{:S(2)}) collective-permute-start(bf16[512,1024]{1,0:T(8,128)(2,1)S(1)} %bitcast.175), channel_id=1, source_target_pairs={{0,2},{1,3},{2,0},{3,1},{4,6},{5,7},{6,4},{7,5},{8,10},{9,11},{10,... | collective-permute-start | bytes 3145736 | tf_op jit(solution)/shard_map/ppermute | solution.py:379
  15.7 118.0 %collective-permute-start.10 = (bf16[512,1024]{1,0:T(8,128)(2,1)S(1)}, bf16[512,1024]{1,0:T(8,128)(2,1)}, u32[]{:S(2)}, u32[]{:S(2)}) collective-permute-start(bf16[512,1024]{1,0:T(8,128)(2,1)S(1)} %bitcast.176), channel_id=1, source_target_pairs={{0,4},{1,5},{2,6},{3,7},{4,0},{5,1},{6,2},{7,3},{8,12},{9,13},{10,... | collective-permute-start | bytes 3145736 | tf_op jit(solution)/shard_map/ppermute | solution.py:379
  17.2 117.0 %collective-permute-start.12 = (bf16[512,1024]{1,0:T(8,128)(2,1)S(1)}, bf16[512,1024]{1,0:T(8,128)(2,1)}, u32[]{:S(2)}, u32[]{:S(2)}) collective-permute-start(bf16[512,1024]{1,0:T(8,128)(2,1)S(1)} %bitcast.177), channel_id=1, source_target_pairs={{0,6},{1,7},{2,4},{3,5},{4,2},{5,3},{6,0},{7,1},{8,14},{9,15},{10,... | collective-permute-start | bytes 3145736 | tf_op jit(solution)/shard_map/ppermute | solution.py:379
  18.6 97.0 %all-to-all-start.1 = ((f32[8,2,4,512]{3,2,1,0:T(4,128)}), f32[8,2,4,512]{3,2,1,0:T(4,128)S(1)}, u32[]{:S(2)}, u32[]{:S(2)}) async-start(f32[8,2,4,512]{3,2,1,0:T(4,128)} %pad_maximum_fusion.5), calls=%async_computation.1 | async-start | bytes 262144 | tf_op jit(solution)/shard_map/all_to_all | solution.py:447
  22.8 435.4 %all-gather.7.cloned.1.call-start = ((), (), s32[]{:S(2)}) async-start(), calls=%async_computation.6 | async-start | bytes 4325376 | tf_op jit(solution)/shard_map/all_gather | solution.py:467
  119.9 911.6 %reduce-scatter.2.cloned.1.call-start = ((), (), s32[]{:S(2)}) async-start(), calls=%async_computation.7 | async-start | bytes 5242880 | tf_op jit(solution)/shard_map/reduce_scatter | solution.py:508
  357.5 79.6 %collective-permute-start.18 = (bf16[4,512,1024]{2,1,0:T(8,128)(2,1)S(1)}, bf16[4,512,1024]{2,1,0:T(8,128)(2,1)S(1)}, u32[]{:S(2)}, u32[]{:S(2)}) collective-permute-start(bf16[4,512,1024]{2,1,0:T(8,128)(2,1)S(1)} %slice.81), channel_id=1, source_target_pairs={{0,1},{1,0},{2,3},{3,2},{4,5},{5,4},{6,7},{7,6},{8,9},{9,8},{10,11... | collective-permute-start | bytes 12582920 | tf_op jit(solution)/shard_map/ppermute | solution.py:379
  361.9 107.5 %collective-permute-start.14 = (bf16[4,512,1024]{2,1,0:T(8,128)(2,1)}, bf16[4,512,1024]{2,1,0:T(8,128)(2,1)}, u32[]{:S(2)}, u32[]{:S(2)}) collective-permute-start(bf16[4,512,1024]{2,1,0:T(8,128)(2,1)} %slice.72), channel_id=1, source_target_pairs={{0,1},{1,0},{2,3},{3,2},{4,5},{5,4},{6,7},{7,6},{8,9},{9,8},{10,11... | collective-permute-start | bytes 12582920 | tf_op jit(solution)/shard_map/ppermute | solution.py:379
  367.1 67.0 %collective-permute-start.37 = (bf16[1,512,1024]{2,1,0:T(8,128)(2,1)S(1)}, bf16[1,512,1024]{2,1,0:T(8,128)(2,1)S(1)}, u32[]{:S(2)}, u32[]{:S(2)}) collective-permute-start(bf16[1,512,1024]{2,1,0:T(8,128)(2,1)S(1)} %copy-done.18), channel_id=1, source_target_pairs={{0,8},{24,16},{1,9},{25,17},{2,10},{26,18},{3,11},{27,19},{4,12},{... | collective-permute-start | bytes 3145736 | tf_op jit(solution)/shard_map/ppermute | solution.py:410
  389.1 66.8 %collective-permute-start.34 = (bf16[1,512,1024]{2,1,0:T(8,128)(2,1)S(1)}, bf16[1,512,1024]{2,1,0:T(8,128)(2,1)S(1)}, u32[]{:S(2)}, u32[]{:S(2)}) collective-permute-start(bf16[1,512,1024]{2,1,0:T(8,128)(2,1)S(1)} %copy-done.16), channel_id=1, source_target_pairs={{0,8},{24,16},{1,9},{25,17},{2,10},{26,18},{3,11},{27,19},{4,12},{... | collective-permute-start | bytes 3145736 | tf_op jit(solution)/shard_map/ppermute | solution.py:410
  411.6 53.2 %collective-permute-start.44 = (bf16[1,512,1024]{2,1,0:T(8,128)(2,1)}, bf16[1,512,1024]{2,1,0:T(8,128)(2,1)}, u32[]{:S(2)}, u32[]{:S(2)}) collective-permute-start(bf16[1,512,1024]{2,1,0:T(8,128)(2,1)} %add_convert_fusion.9), channel_id=1, source_target_pairs={{8,16},{16,8},{9,17},{17,9},{10,18},{18,10},{11,19},{19,11},{12,20... | collective-permute-start | bytes 3145736 | tf_op jit(solution)/shard_map/ppermute | solution.py:412
  477.2 51.9 %collective-permute-start.17 = (bf16[512,1024]{1,0:T(8,128)(2,1)S(1)}, bf16[512,1024]{1,0:T(8,128)(2,1)S(1)}, u32[]{:S(2)}, u32[]{:S(2)}) collective-permute-start(bf16[512,1024]{1,0:T(8,128)(2,1)S(1)} %get-tuple-element.107), channel_id=1, source_target_pairs={{0,6},{1,7},{2,4},{3,5},{4,2},{5,3},{6,0},{7,1},{8,14},{9,15},{10,... | collective-permute-start | bytes 3145736 | tf_op jit(solution)/shard_map/ppermute | solution.py:379
  478.6 71.4 %collective-permute-start.16 = (bf16[512,1024]{1,0:T(8,128)(2,1)S(1)}, bf16[512,1024]{1,0:T(8,128)(2,1)S(1)}, u32[]{:S(2)}, u32[]{:S(2)}) collective-permute-start(bf16[512,1024]{1,0:T(8,128)(2,1)S(1)} %get-tuple-element.108), channel_id=1, source_target_pairs={{0,4},{1,5},{2,6},{3,7},{4,0},{5,1},{6,2},{7,3},{8,12},{9,13},{10,... | collective-permute-start | bytes 3145736 | tf_op jit(solution)/shard_map/ppermute | solution.py:379
  484.3 67.3 %collective-permute-start.15 = (bf16[512,1024]{1,0:T(8,128)(2,1)S(1)}, bf16[512,1024]{1,0:T(8,128)(2,1)S(1)}, u32[]{:S(2)}, u32[]{:S(2)}) collective-permute-start(bf16[512,1024]{1,0:T(8,128)(2,1)S(1)} %get-tuple-element.106), channel_id=1, source_target_pairs={{0,2},{1,3},{2,0},{3,1},{4,6},{5,7},{6,4},{7,5},{8,10},{9,11},{10,... | collective-permute-start | bytes 3145736 | tf_op jit(solution)/shard_map/ppermute | solution.py:379
  506.7 66.5 %collective-permute-start.31 = (bf16[1,1024,1024]{2,1,0:T(8,128)(2,1)}, bf16[1,1024,1024]{2,1,0:T(8,128)(2,1)}, u32[]{:S(2)}, u32[]{:S(2)}) collective-permute-start(bf16[1,1024,1024]{2,1,0:T(8,128)(2,1)} %get-tuple-element.47), channel_id=1, source_target_pairs={{0,8},{24,16},{1,9},{25,17},{2,10},{26,18},{3,11},{27,19},{4,12},{... | collective-permute-start | bytes 6291464 | tf_op jit(solution)/shard_map/ppermute | solution.py:410
  515.3 116.0 %collective-permute-start.28 = (bf16[1,1024,1024]{2,1,0:T(8,128)(2,1)}, bf16[1,1024,1024]{2,1,0:T(8,128)(2,1)}, u32[]{:S(2)}, u32[]{:S(2)}) collective-permute-start(bf16[1,1024,1024]{2,1,0:T(8,128)(2,1)} %get-tuple-element.46), channel_id=1, source_target_pairs={{0,8},{24,16},{1,9},{25,17},{2,10},{26,18},{3,11},{27,19},{4,12},{... | collective-permute-start | bytes 6291464 | tf_op jit(solution)/shard_map/ppermute | solution.py:410
  529.1 185.6 %collective-permute-start.25 = (bf16[1,1024,1024]{2,1,0:T(8,128)(2,1)}, bf16[1,1024,1024]{2,1,0:T(8,128)(2,1)}, u32[]{:S(2)}, u32[]{:S(2)}) collective-permute-start(bf16[1,1024,1024]{2,1,0:T(8,128)(2,1)} %get-tuple-element.45), channel_id=1, source_target_pairs={{0,8},{24,16},{1,9},{25,17},{2,10},{26,18},{3,11},{27,19},{4,12},{... | collective-permute-start | bytes 6291464 | tf_op jit(solution)/shard_map/ppermute | solution.py:410
  551.6 206.8 %collective-permute-start.22 = (bf16[1,1024,1024]{2,1,0:T(8,128)(2,1)}, bf16[1,1024,1024]{2,1,0:T(8,128)(2,1)}, u32[]{:S(2)}, u32[]{:S(2)}) collective-permute-start(bf16[1,1024,1024]{2,1,0:T(8,128)(2,1)} %get-tuple-element.44), channel_id=1, source_target_pairs={{0,8},{24,16},{1,9},{25,17},{2,10},{26,18},{3,11},{27,19},{4,12},{... | collective-permute-start | bytes 6291464 | tf_op jit(solution)/shard_map/ppermute | solution.py:410
  569.9 195.1 %collective-permute-start.45 = (bf16[1,512,1024]{2,1,0:T(8,128)(2,1)S(1)}, bf16[1,512,1024]{2,1,0:T(8,128)(2,1)S(1)}, u32[]{:S(2)}, u32[]{:S(2)}) collective-permute-start(bf16[1,512,1024]{2,1,0:T(8,128)(2,1)S(1)} %copy-done.8), channel_id=1, source_target_pairs={{8,0},{16,24},{9,1},{17,25},{10,2},{18,26},{11,3},{19,27},{12,4},{... | collective-permute-start | bytes 3145736 | tf_op jit(solution)/shard_map/ppermute | solution.py:414
  573.2 195.0 %collective-permute-start.42 = (bf16[1,512,1024]{2,1,0:T(8,128)(2,1)S(1)}, bf16[1,512,1024]{2,1,0:T(8,128)(2,1)S(1)}, u32[]{:S(2)}, u32[]{:S(2)}) collective-permute-start(bf16[1,512,1024]{2,1,0:T(8,128)(2,1)S(1)} %copy-done.10), channel_id=1, source_target_pairs={{8,0},{16,24},{9,1},{17,25},{10,2},{18,26},{11,3},{19,27},{12,4},{... | collective-permute-start | bytes 3145736 | tf_op jit(solution)/shard_map/ppermute | solution.py:414
  631.4 139.9 %collective-permute-start.39 = (bf16[1,512,1024]{2,1,0:T(8,128)(2,1)S(1)}, bf16[1,512,1024]{2,1,0:T(8,128)(2,1)S(1)}, u32[]{:S(2)}, u32[]{:S(2)}) collective-permute-start(bf16[1,512,1024]{2,1,0:T(8,128)(2,1)S(1)} %copy-done.11), channel_id=1, source_target_pairs={{8,0},{16,24},{9,1},{17,25},{10,2},{18,26},{11,3},{19,27},{12,4},{... | collective-permute-start | bytes 3145736 | tf_op jit(solution)/shard_map/ppermute | solution.py:414
  714.7 59.7 %collective-permute-start.36 = (bf16[1,512,1024]{2,1,0:T(8,128)(2,1)S(1)}, bf16[1,512,1024]{2,1,0:T(8,128)(2,1)S(1)}, u32[]{:S(2)}, u32[]{:S(2)}) collective-permute-start(bf16[1,512,1024]{2,1,0:T(8,128)(2,1)S(1)} %add_convert_fusion.14), channel_id=1, source_target_pairs={{8,0},{16,24},{9,1},{17,25},{10,2},{18,26},{11,3},{19,27},{12,4},{... | collective-permute-start | bytes 3145736 | tf_op jit(solution)/shard_map/ppermute | solution.py:414
  781.1 185.2 %all-to-all-start.2 = ((bf16[4,2,256,256]{3,2,1,0:T(8,128)(2,1)}), bf16[4,2,256,256]{3,2,1,0:T(8,128)(2,1)}, u32[]{:S(2)}, u32[]{:S(2)}) async-start(bf16[4,2,256,256]{3,2,1,0:T(8,128)(2,1)} %bitcast.182), calls=%async_computation.2 | async-start | bytes 2097152 | tf_op jit(solution)/shard_map/all_to_all | solution.py:506
  798.8 194.7 %collective-permute-start.33 = (bf16[1,1024,1024]{2,1,0:T(8,128)(2,1)}, bf16[1,1024,1024]{2,1,0:T(8,128)(2,1)}, u32[]{:S(2)}, u32[]{:S(2)}) collective-permute-start(bf16[1,1024,1024]{2,1,0:T(8,128)(2,1)} %add_convert_fusion), channel_id=1, source_target_pairs={{8,0},{16,24},{9,1},{17,25},{10,2},{18,26},{11,3},{19,27},{12,4},{... | collective-permute-start | bytes 6291464 | tf_op jit(solution)/shard_map/ppermute | solution.py:414
  804.6 192.1 %collective-permute-start.30 = (bf16[1,1024,1024]{2,1,0:T(8,128)(2,1)}, bf16[1,1024,1024]{2,1,0:T(8,128)(2,1)}, u32[]{:S(2)}, u32[]{:S(2)}) collective-permute-start(bf16[1,1024,1024]{2,1,0:T(8,128)(2,1)} %add_convert_fusion.2), channel_id=1, source_target_pairs={{8,0},{16,24},{9,1},{17,25},{10,2},{18,26},{11,3},{19,27},{12,4},{... | collective-permute-start | bytes 6291464 | tf_op jit(solution)/shard_map/ppermute | solution.py:414
  810.4 189.4 %collective-permute-start.27 = (bf16[1,1024,1024]{2,1,0:T(8,128)(2,1)}, bf16[1,1024,1024]{2,1,0:T(8,128)(2,1)}, u32[]{:S(2)}, u32[]{:S(2)}) collective-permute-start(bf16[1,1024,1024]{2,1,0:T(8,128)(2,1)} %add_convert_fusion.4), channel_id=1, source_target_pairs={{8,0},{16,24},{9,1},{17,25},{10,2},{18,26},{11,3},{19,27},{12,4},{... | collective-permute-start | bytes 6291464 | tf_op jit(solution)/shard_map/ppermute | solution.py:414
  816.5 208.0 %collective-permute-start.24 = (bf16[1,1024,1024]{2,1,0:T(8,128)(2,1)}, bf16[1,1024,1024]{2,1,0:T(8,128)(2,1)}, u32[]{:S(2)}, u32[]{:S(2)}) collective-permute-start(bf16[1,1024,1024]{2,1,0:T(8,128)(2,1)} %add_convert_fusion.6), channel_id=1, source_target_pairs={{8,0},{16,24},{9,1},{17,25},{10,2},{18,26},{11,3},{19,27},{12,4},{... | collective-permute-start | bytes 6291464 | tf_op jit(solution)/shard_map/ppermute | solution.py:414
  988.7 56.2 %all-to-all-start.3 = ((bf16[4,2,256,512]{3,2,1,0:T(8,128)(2,1)}), bf16[4,2,256,512]{3,2,1,0:T(8,128)(2,1)}, u32[]{:S(2)}, u32[]{:S(2)}) async-start(bf16[4,2,256,512]{3,2,1,0:T(8,128)(2,1)} %attn_backward.1), calls=%async_computation.3 | async-start | bytes 4194304 | tf_op jit(solution)/shard_map/all_to_all | solution.py:513
  993.2 108.2 %all-reduce.4.cloned.1.call-start = ((), (), s32[]{:S(2)}) async-start(), calls=%async_computation.9 | async-start | bytes 6291456 | tf_op jit(solution)/shard_map/psum | solution.py:516
  (57 other events, 1127.1 us)
Sparse Core Ops, SparseCore 0:
  11.7 83.4 all-gather.8
  98.0 65.1 all-gather.4
  166.0 91.8 all-gather.6
  568.8 140.5 reduce-scatter.1
  1031.7 69.6 all-reduce.3

commit v2 on v1

--- a/solution.py
+++ b/solution.py
@@ -16,6 +16,8 @@
 SCALE = HEAD ** (-0.5)
 NEG = -1e30
 VMEM = 60 * 1024 * 1024
+MESH = pl.DeviceIdType.MESH
+DMA = pltpu.SemaphoreType.DMA
 
 
 def dot(a, b):
@@ -117,29 +119,19 @@
     )(lengths, x, w, cq, sq, ckv, skv)
 
 
-def bwd_kernel(len_ref, qkv_ref, do_ref, lse_ref, cq, sq, ckv, skv, out_ref, dkv_ref):
-    nh, _, seg, _ = do_ref.shape
-    full = nh * seg
-    block = seg
-    length = len_ref[pl.program_id(0)]
-    q = qkv_ref[0, 0, :, :128]
-    kv = qkv_ref[0, 0, :, 128:]
+def bwd_piece(q, kv, heads, lses, length, tables, dkv_ref, put):
+    cq, sq, ckv, skv = tables
+    full, block = q.shape[0], lses(0).shape[1] // 2
     k, v = kv[:, :HEAD], kv[:, HEAD:]
     kt = kv.astype(F32).T[:HEAD].astype(BF)
     dkv_ref[...] = jnp.zeros_like(dkv_ref)
-    for i in range(nh):
+    for i in range(full // block):
         n = (i + 1) * block
         rows = pl.ds(i * block, block)
         q2 = two_heads(q[i * block : n])
-        do2 = two_heads(do_ref[i, 0])
+        do2 = two_heads(heads(i))
         s = dot_nt(k[:n], q2)
-        p = jnp.exp(
-            jnp.where(
-                attn_mask(i * block, n, block, length),
-                s * SCALE - lse_ref[0, 0, i : i + 1, :],
-                NEG,
-            )
-        )
+        p = jnp.exp(jnp.where(attn_mask(i * block, n, block, length), s * SCALE - lses(i), NEG))
         dp = dot_nt(v[:n], do2)
         delta = jnp.sum(p * dp, axis=0, keepdims=True)
         ds = (p * (dp - delta) * SCALE).astype(BF)
@@ -147,11 +139,27 @@
         dkv_ref[:n, HEAD:] += dot(p.astype(BF), do2)
         dq = untwo(dot(kt[:, :n], ds), block)
         dq = dq * cq[rows, :] - swap_halves(dq) * sq[rows, :]
-        out_ref[i, 0, :, :128] = dq.astype(BF)
+        put(i, 0, dq.astype(BF))
     dkv = dkv_ref[...]
     dkv = (dkv * ckv[...] - swap_halves(dkv) * skv[...]).astype(BF)
-    for i in range(nh):
-        out_ref[i, 0, :, 128:] = dkv[i * block : (i + 1) * block]
+    for i in range(full // block):
+        put(i, 128, dkv[i * block : (i + 1) * block])
+
+
+def bwd_kernel(len_ref, qkv_ref, do_ref, lse_ref, cq, sq, ckv, skv, out_ref, dkv_ref):
+    def put(i, lo, v):
+        out_ref[i, 0, :, lo : lo + 128] = v
+
+    bwd_piece(
+        qkv_ref[0, 0, :, :128],
+        qkv_ref[0, 0, :, 128:],
+        lambda i: do_ref[i, 0],
+        lambda i: lse_ref[0, 0, i : i + 1, :],
+        len_ref[pl.program_id(0)],
+        (cq, sq, ckv, skv),
+        dkv_ref,
+        put,
+    )
 
 
 def attn_backward(qkv, d_head, lse, lengths, tables):
@@ -238,7 +246,7 @@
 
 
 def expert_kernel(steps, slot_ref, weight_ref, x_ref, d_ref, win_ref, wdown_ref,
-                  out_ref, drow_ref, gin_ref, gdown_ref, hid_ref, dgu_ref, *acc):
+                  out_ref, drow_ref, grad_ref, hid_ref, dgu_ref, *acc):
     _, sources, cap, width = x_ref.shape
     ff = wdown_ref.shape[1]
     per = 2 if sources % 2 == 0 else 1
@@ -269,8 +277,8 @@
     gin = dot_tn(x, dgu_ref[...])
     gdown = dot_tn(hid_ref[...], d)
     if steps == 1:
-        gin_ref[0] = gin.astype(BF)
-        gdown_ref[0] = gdown.astype(BF)
+        grad_ref[0, :width] = gin.astype(BF)
+        grad_ref[0, width:] = gdown.astype(BF)
     else:
         ain, adown = acc
         step = pl.program_id(1)
@@ -285,18 +293,18 @@
 
         @pl.when(step == steps - 1)
         def _():
-            gin_ref[0] = ain[...].astype(BF)
-            gdown_ref[0] = adown[...].astype(BF)
-
-
-def experts_call(first, count, slots, weights, x, d, win, wdown):
-    _, sources, cap, width = x.shape
+            grad_ref[0, :width] = ain[...].astype(BF)
+            grad_ref[0, width:] = adown[...].astype(BF)
+
+
+def experts_call(slots, weights, x, d, win, wdown):
+    count, sources, cap, width = x.shape
     tokens = slots.shape[-1]
     ff = wdown.shape[1]
     chunk = min(sources, 8)
     steps = sources // chunk
-    small = pl.BlockSpec((chunk, 1, 1, tokens), lambda j, r: (r, first + j, 0, 0))
-    rows = pl.BlockSpec((1, chunk, cap, width), lambda j, r: (first + j, r, 0, 0))
+    small = pl.BlockSpec((chunk, 1, 1, tokens), lambda j, r: (r, j, 0, 0))
+    rows = pl.BlockSpec((1, chunk, cap, width), lambda j, r: (j, r, 0, 0))
     rows_out = pl.BlockSpec((1, chunk, cap, width), lambda j, r: (j, r, 0, 0))
     scratch = [pltpu.VMEM((chunk * cap, ff), BF), pltpu.VMEM((chunk * cap, 2 * ff), BF)]
     if steps > 1:
@@ -310,20 +318,18 @@
             small,
             rows,
             rows,
-            pl.BlockSpec((1, width, 2 * ff), lambda j, r: (first + j, 0, 0)),
-            pl.BlockSpec((1, ff, width), lambda j, r: (first + j, 0, 0)),
+            pl.BlockSpec((1, width, 2 * ff), lambda j, r: (j, 0, 0)),
+            pl.BlockSpec((1, ff, width), lambda j, r: (j, 0, 0)),
         ],
         out_specs=[
             rows_out,
             rows_out,
-            pl.BlockSpec((1, width, 2 * ff), lambda j, r: (j, 0, 0)),
-            pl.BlockSpec((1, ff, width), lambda j, r: (j, 0, 0)),
+            pl.BlockSpec((1, width + ff, width), lambda j, r: (j, 0, 0)),
         ],
         out_shape=[
             shape,
             shape,
-            jax.ShapeDtypeStruct((count, width, 2 * ff), BF),
-            jax.ShapeDtypeStruct((count, ff, width), BF),
+            jax.ShapeDtypeStruct((count, width + ff, width), BF),
         ],
         scratch_shapes=scratch,
         compiler_params=params(2),
@@ -336,11 +342,10 @@
     )(slots[:, :, None, :], weights[:, :, None, :], x, d, win, wdown)
 
 
-def combine_kernel(parts, slot_ref, *refs):
-    row_refs, out_refs = refs[: 2 * parts], refs[2 * parts :]
+def combine_kernel(slot_ref, row_ref, out_ref):
     slots = slot_ref[0]
     count, here = slots.shape
-    cap = row_refs[0].shape[2]
+    cap = row_ref.shape[2]
     lane = lax.broadcasted_iota(jnp.int32, (count, here * cap), 1)
     hot = None
     for j in range(here):
@@ -348,31 +353,29 @@
         hit = lane == jnp.where(col >= 0, col + j * cap, -1)
         hot = hit if hot is None else hot | hit
     hot = hot.astype(F32).astype(BF)
-    for group, out_ref in zip((row_refs[:parts], row_refs[parts:]), out_refs):
-        rows = jnp.concatenate([r[j, 0] for r in group for j in range(r.shape[0])], axis=0)
-        out_ref[0] = dot(hot, rows).astype(BF)
-
-
-def combine(slots_t, outs, drows):
+    out_ref[0] = dot(hot, row_ref[...].reshape(here * cap, row_ref.shape[3])).astype(BF)
+
+
+def combine(slots_t, rows):
     sources, count, here = slots_t.shape
-    _, _, cap, width = outs[0].shape
-    blocks = [pl.BlockSpec((o.shape[0], 1, cap, width), lambda s: (0, s, 0, 0)) for o in outs]
-    shape = jax.ShapeDtypeStruct((sources, count, width), BF)
-    spec = pl.BlockSpec((1, count, width), lambda s: (s, 0, 0))
+    _, _, cap, width = rows.shape
     return pl.pallas_call(
-        functools.partial(combine_kernel, len(outs)),
+        combine_kernel,
         grid=(sources,),
-        in_specs=[pl.BlockSpec((1, count, here), lambda s: (s, 0, 0))] + blocks + blocks,
-        out_specs=[spec, spec],
-        out_shape=[shape, shape],
+        in_specs=[
+            pl.BlockSpec((1, count, here), lambda s: (s, 0, 0)),
+            pl.BlockSpec((here, 1, cap, width), lambda s: (0, s, 0, 0)),
+        ],
+        out_specs=pl.BlockSpec((1, count, width), lambda s: (s, 0, 0)),
+        out_shape=jax.ShapeDtypeStruct((sources, count, width), BF),
         compiler_params=params(1),
         cost_estimate=pl.CostEstimate(
-            flops=4 * sources * here * cap * count * width,
-            bytes_accessed=4 * sources * width * (count + here * cap),
+            flops=2 * sources * here * cap * count * width,
+            bytes_accessed=2 * sources * width * (count + here * cap),
             transcendentals=0,
         ),
         name="combine",
-    )(slots_t, *outs, *drows)
+    )(slots_t, rows)
 
 
 def swap(x, bit, n):
@@ -413,6 +416,321 @@
     total = (pair.astype(F32) + second.astype(F32)).astype(BF)
     third = lax.ppermute(total, "heads", [(1, 0), (2, 3)])
     return jnp.where((z == 1) | (z == 2), total, third).astype(F32)
+
+
+CHUNK = 256
+LAG = 3
+
+
+def remote(src, dst, send, recv, axis, index):
+    return pltpu.make_async_remote_copy(
+        src_ref=src, dst_ref=dst, send_sem=send, recv_sem=recv,
+        device_id={axis: index}, device_id_type=MESH,
+    )
+
+
+def greet(nh, masks):
+    z, me = lax.axis_index("heads"), lax.axis_index("experts")
+    bar = pltpu.get_barrier_semaphore()
+    for d in range(1, nh):
+        pl.semaphore_signal(bar, inc=1, device_id={"heads": lax.rem(z + d, nh)}, device_id_type=MESH)
+    for r in masks:
+        pl.semaphore_signal(bar, inc=1, device_id={"experts": me ^ r}, device_id_type=MESH)
+    pl.semaphore_wait(bar, nh - 1 + len(masks))
+
+
+class Chain:
+    def __init__(self, src, out, scratch, first, count):
+        self.src, self.out, self.first, self.count = src, out, first, count
+        self.a, self.b, self.buf, self.s1, self.r1, self.s2, self.r2, self.ls, self.os = scratch
+        z = lax.axis_index("heads")
+        self.mid = (z == 1) | (z == 2)
+        self.outer = jnp.where(z == 0, 1, jnp.where(z == 1, 0, jnp.where(z == 2, 3, 2)))
+        self.inner = jnp.where(z == 1, 2, jnp.where(z == 2, 1, z))
+
+    def piece(self, k):
+        return self.src.at[pl.ds((self.first + k) * CHUNK, CHUNK)]
+
+    def load(self, k):
+        return pltpu.make_async_copy(self.piece(k), self.buf.at[lax.rem(k, 2)], self.ls.at[lax.rem(k, 2)])
+
+    def store(self, ref, k):
+        return pltpu.make_async_copy(ref.at[k], self.out.at[pl.ds(k * CHUNK, CHUNK)], self.os.at[k])
+
+    def up(self, k):
+        return remote(self.piece(k), self.a.at[k], self.s1.at[k], self.r1.at[k], "heads", self.outer)
+
+    def across(self, k):
+        return remote(self.a.at[k], self.b.at[k], self.s2.at[k], self.r2.at[k], "heads", self.inner)
+
+    def down(self, k):
+        return remote(self.b.at[k], self.a.at[k], self.s1.at[k], self.r1.at[k], "heads", self.outer)
+
+    def begin(self):
+        @pl.when(self.mid)
+        def _():
+            self.load(0).start()
+
+    def steps(self):
+        return self.count + LAG
+
+    def step(self, k):
+        n = self.count
+
+        @pl.when(self.mid)
+        def _():
+            @pl.when(k < n)
+            def _():
+                @pl.when(k + 1 < n)
+                def _():
+                    self.load(k + 1).start()
+
+                self.load(k).wait()
+                self.up(k).wait_recv()
+                own = self.buf[lax.rem(k, 2)].astype(F32)
+                self.a[k] = (self.a[k].astype(F32) + own).astype(BF)
+                self.across(k).start()
+
+            @pl.when((k >= 1) & (k <= n))
+            def _():
+                j = k - 1
+                self.across(j).wait_recv()
+                self.b[j] = (self.a[j].astype(F32) + self.b[j].astype(F32)).astype(BF)
+                self.down(j).start()
+                self.store(self.b, j).start()
+
+        @pl.when(jnp.logical_not(self.mid))
+        def _():
+            @pl.when(k < n)
+            def _():
+                @pl.when(k >= LAG)
+                def _():
+                    self.up(k - LAG).wait_send()
+
+                self.up(k).start()
+
+            @pl.when(k >= LAG)
+            def _():
+                j = k - LAG
+                self.down(j).wait_recv()
+                self.store(self.a, j).start()
+
+    def run(self, first, last):
+        @pl.loop(first, last)
+        def _(k):
+            self.step(k)
+
+    def finish(self):
+        n = self.count
+
+        @pl.when(self.mid)
+        def _():
+            @pl.loop(0, n)
+            def _(k):
+                self.across(k).wait_send()
+                self.down(k).wait_send()
+                self.store(self.b, k).wait()
+
+        @pl.when(jnp.logical_not(self.mid))
+        def _():
+            @pl.loop(n - LAG, n)
+            def _(k):
+                self.up(k).wait_send()
+
+            @pl.loop(0, n)
+            def _(k):
+                self.store(self.a, k).wait()
+
+
+def chain_scratch(count, width):
+    return [
+        pltpu.VMEM((count, CHUNK, width), BF),
+        pltpu.VMEM((count, CHUNK, width), BF),
+        pltpu.VMEM((2, CHUNK, width), BF),
+        DMA((count,)),
+        DMA((count,)),
+        DMA((count,)),
+        DMA((count,)),
+        DMA((2,)),
+        DMA((count,)),
+    ]
+
+
+def middle_kernel(count, len_ref, sum_ref, parts_ref, mid_ref, grad_ref, gain_ref, o_ref, qkv_ref, lse_ref,
+                  cq, sq, ckv, skv, total_ref, dmid_ref, dbranch_ref, gtwo_ref, dqkv_ref,
+                  c_buf, e_buf, f_buf, hs, hr, dmoe, dkv, cs, cr, fs, fr, hss, hrs, *chain):
+    nh, nseq, seg, _ = dqkv_ref.shape
+    groups = qkv_ref.shape[1]
+    tokens = nseq * seg
+    z, me = lax.axis_index("heads"), lax.axis_index("experts")
+    chain = Chain(sum_ref, total_ref, chain, 0, count)
+    greet(nh, (1, 2, 4, 6))
+
+    def core(i):
+        return remote(parts_ref.at[2 * i + 1], c_buf.at[i], cs.at[i], cr.at[i], "experts", me ^ 1)
+
+    def chip(i):
+        return remote(e_buf.at[i - 1], f_buf.at[i - 1], fs.at[i - 1], fr.at[i - 1], "experts", me ^ (2 * i))
+
+    order = (3, 1, 2)
+    for i in order + (0,):
+        core(i).start()
+    chain.begin()
+    chain.run(0, 1)
+    for i in order:
+        core(i).wait_recv()
+        e_buf[i - 1] = (parts_ref[2 * i].astype(F32) + c_buf[i].astype(F32)).astype(BF)
+        chip(i).start()
+    chain.run(1, 2)
+    core(0).wait_recv()
+    dmoe[...] = parts_ref[0].astype(F32) + c_buf[0].astype(F32)
+    chain.run(2, 5)
+    for i in order:
+        chip(i).wait_recv()
+
+    gtwo_ref[...] = jnp.zeros_like(gtwo_ref)
+    rows_at = 128
+
+    @pl.loop(0, tokens // rows_at)
+    def _(i):
+        rows = pl.ds(i * rows_at, rows_at)
+        d = dmoe[rows]
+        for r in range(3):
+            d = d + f_buf[r, rows].astype(F32)
+        m = mid_ref[rows]
+        inv = lax.rsqrt(jnp.mean(m * m, axis=-1, keepdims=True) + EPS)
+        zed = gain_ref[...] * d
+        dm = grad_ref[rows].astype(F32) + inv * zed - m * (inv * inv * inv * jnp.mean(zed * m, axis=-1, keepdims=True))
+        gtwo_ref[...] += jnp.sum(d * m * inv, axis=0, keepdims=True)
+        dmid_ref[rows] = dm
+        db = dm.astype(BF)
+        dbranch_ref[rows] = db
+        for h in range(nh):
+            hs[h, rows] = dot_nt(db, o_ref[h]).astype(BF)
+
+    def send(d):
+        to = lax.rem(z + d, nh)
+        return remote(hs.at[to], hr.at[z], hss.at[d], hrs.at[d], "heads", to)
+
+    def arrive(d):
+        src = lax.rem(z + nh - d, nh)
+        return remote(hs.at[src], hr.at[src], hss.at[d], hrs.at[d], "heads", src)
+
+    for d in range(1, nh):
+        send(d).start()
+    hr[pl.ds(z, 1)] = hs[pl.ds(z, 1)]
+    chain.run(5, 8)
+    for d in range(1, nh):
+        arrive(d).wait_recv()
+
+    @pl.loop(0, nseq)
+    def _(s):
+        length = len_ref[s]
+        for g in range(groups):
+            def put(i, lo, v):
+                dqkv_ref[i, s, :, g * 256 + lo : g * 256 + lo + 128] = v
+
+            bwd_piece(
+                qkv_ref[s, g, :, :128],
+                qkv_ref[s, g, :, 128:],
+                lambda i: hr[i, pl.ds(s * seg, seg), g * 128 : (g + 1) * 128],
+                lambda i: lse_ref[s, g, i : i + 1, :],
+                length,
+                (cq, sq, ckv, skv),
+                dkv,
+                put,
+            )
+        chain.step(8 + s)
+
+    chain.run(8 + nseq, chain.steps())
+    chain.finish()
+    for i in range(4):
+        core(i).wait_send()
+    for i in order:
+        chip(i).wait_send()
+    for d in range(1, nh):
+        send(d).wait_send()
+
+
+def middle(count, lengths, sums, parts, mid, grad, gain, o_parts, qkv, lse, tables):
+    nseq, groups, full, _ = qkv.shape
+    nh = o_parts.shape[0]
+    tokens, width = mid.shape
+    seg = tokens // nseq
+    vmem = pl.BlockSpec(memory_space=pltpu.VMEM)
+    hbm = pl.BlockSpec(memory_space=pl.ANY)
+    heads = (nh, tokens, groups * 128)
+    return pl.pallas_call(
+        functools.partial(middle_kernel, count),
+        in_specs=[pl.BlockSpec(memory_space=pltpu.SMEM), hbm] + [vmem] * 11,
+        out_specs=[hbm] + [vmem] * 4,
+        out_shape=[
+            jax.ShapeDtypeStruct((count * CHUNK, width), BF),
+            jax.ShapeDtypeStruct((tokens, width), F32),
+            jax.ShapeDtypeStruct((tokens, width), BF),
+            jax.ShapeDtypeStruct((1, width), F32),
+            jax.ShapeDtypeStruct((nh, nseq, seg, groups * 256), BF),
+        ],
+        scratch_shapes=[
+            pltpu.VMEM((4, tokens, width), BF),
+            pltpu.VMEM((3, tokens, width), BF),
+            pltpu.VMEM((3, tokens, width), BF),
+            pltpu.VMEM(heads, BF),
+            pltpu.VMEM(heads, BF),
+            pltpu.VMEM((tokens, width), F32),
+            pltpu.VMEM((full, 128), F32),
+            DMA((4,)),
+            DMA((4,)),
+            DMA((3,)),
+            DMA((3,)),
+            DMA((nh,)),
+            DMA((nh,)),
+        ]
+        + chain_scratch(count, width),
+        compiler_params=pltpu.CompilerParams(
+            collective_id=1, has_side_effects=True, vmem_limit_bytes=VMEM
+        ),
+        cost_estimate=pl.CostEstimate(flops=10**11, bytes_accessed=30 * 2**20, transcendentals=10**7),
+        name="middle",
+    )(lengths, sums, parts, mid, grad, gain, o_parts, qkv, lse, *tables)
+
+
+def last_kernel(first, count, sum_ref, parts_ref, total_ref, got_ref, ps, pr, *chain):
+    ne = parts_ref.shape[0]
+    me = lax.axis_index("experts")
+    chain = Chain(sum_ref, total_ref, chain, first, count)
+    greet(lax.axis_size("heads"), tuple(range(1, ne)))
+
+    def part(r):
+        return remote(parts_ref.at[r], got_ref.at[r - 1], ps.at[r], pr.at[r], "experts", me ^ r)
+
+    chain.begin()
+    for r in range(ne - 1, 0, -1):
+        part(r).start()
+    chain.run(0, chain.steps())
+    chain.finish()
+    for r in range(1, ne):
+        part(r).wait()
+
+
+def last(first, count, sums, parts):
+    ne, tokens, width = parts.shape
+    hbm = pl.BlockSpec(memory_space=pl.ANY)
+    return pl.pallas_call(
+        functools.partial(last_kernel, first, count),
+        in_specs=[hbm, hbm],
+        out_specs=[hbm, hbm],
+        out_shape=[
+            jax.ShapeDtypeStruct((count * CHUNK, width), BF),
+            jax.ShapeDtypeStruct((ne - 1, tokens, width), BF),
+        ],
+        scratch_shapes=[DMA((ne,)), DMA((ne,))] + chain_scratch(count, width),
+        compiler_params=pltpu.CompilerParams(
+            collective_id=2, has_side_effects=True, vmem_limit_bytes=VMEM
+        ),
+        cost_estimate=pl.CostEstimate(flops=2 * 10**11, bytes_accessed=30 * 2**20, transcendentals=0),
+        name="last",
+    )(sums, parts)
 
 
 def body(layer_input, seq_lengths, expert_ids, route_weight, priority, attn_gain, moe_gain,
@@ -482,38 +800,47 @@
     d_rows = gather_rows(slots, weights, grads_all, cap)
     tokens_all = plane_gather(moe_in, ne)
     x_rows = gather_rows(slots, None, tokens_all, cap)
-    outs, drows, gins, gdowns = [], [], [], []
-    for j in range(here):
-        o, dr, gi, gd = experts_call(j, 1, slots, weights, x_rows, d_rows, expert_in, expert_down)
-        outs.append(o)
-        drows.append(dr)
-        gins.append(heads_sum(gi, z, nh))
-        gdowns.append(heads_sum(gd, z, nh))
-    grad_in = jnp.concatenate(gins, axis=0)
-    grad_down = jnp.concatenate(gdowns, axis=0)
-    moe_parts, d_parts = combine(jnp.swapaxes(slots, 1, 2), outs, drows)
-    d_moe = plane_scatter(d_parts, ne)
-    moe_sum = plane_scatter(moe_parts, ne)
+    results, drows, sums = experts_call(slots, weights, x_rows, d_rows, expert_in, expert_down)
+    slots_t = jnp.swapaxes(slots, 1, 2)
+    d_parts = combine(slots_t, drows)
+    moe_parts = combine(slots_t, results)
+    if nh == 4 and ne == 8:
+        flat = sums.reshape(-1, width)
+        chunks = flat.shape[0] // CHUNK
+        half = chunks // 2
+        total_a, d_mid, d_branch, gain_two, dqkv = middle(
+            half, seq_lengths, flat, d_parts, mid, grad, moe_gain.reshape(1, width), o_parts, qkv, lse, tables)
+        gain_two = gain_two.reshape(width)
+        back = lax.all_to_all(dqkv, "heads", split_axis=0, concat_axis=0, tiled=True)
+        flat, moe_parts, d_branch = lax.optimization_barrier((flat, moe_parts, d_branch))
+        total_b, got = last(half, chunks - half, flat, moe_parts)
+        moe_sum = moe_parts[0].astype(F32) + jnp.sum(got.astype(F32), axis=0)
+        totals = [t.reshape(here // 2, sums.shape[1], width).astype(F32) for t in (total_a, total_b)]
+        grad_in = jnp.concatenate([t[:, :width] for t in totals], axis=0)
+        grad_down = jnp.concatenate([t[:, width:] for t in totals], axis=0)
+    else:
+        totals = heads_sum(sums, z, nh)
+        grad_in, grad_down = totals[:, :width], totals[:, width:]
+        d_moe = plane_scatter(d_parts, ne)
+        moe_sum = plane_scatter(moe_parts, ne)
+        zed = moe_gain * d_moe
+        d_mid = grad.astype(F32) + inv_two * zed - mid * (inv_two ** 3 * jnp.mean(zed * mid, axis=-1, keepdims=True))
+        gain_two = jnp.sum(d_moe * mid * inv_two, axis=0)
+        d_branch = d_mid.astype(BF)
+        d_heads = jnp.einsum("tw,zmw->ztm", d_branch, o_parts, preferred_element_type=F32).astype(BF)
+        d_heads = d_heads.reshape(nh, nseq, seg, groups * 128)
+        d_heads = lax.all_to_all(d_heads, "heads", split_axis=0, concat_axis=0, tiled=True)
+        dqkv = attn_backward(qkv, d_heads, lse, seq_lengths, tables)
+        back = lax.all_to_all(dqkv, "heads", split_axis=0, concat_axis=0, tiled=True)
     out = (mid + moe_sum).astype(BF)
 
-    gf = grad.astype(F32)
-    zed = moe_gain * d_moe
-    d_mid = gf + inv_two * zed - mid * (inv_two ** 3 * jnp.mean(zed * mid, axis=-1, keepdims=True))
-    gain_two = jnp.sum(d_moe * mid * inv_two, axis=0)
-    d_branch = d_mid.astype(BF)
-    d_heads = jnp.einsum("tw,zmw->ztm", d_branch, o_parts, preferred_element_type=F32).astype(BF)
-    d_heads = d_heads.reshape(nh, nseq, seg, groups * 128)
-    d_heads = lax.all_to_all(d_heads, "heads", split_axis=0, concat_axis=0, tiled=True)
     o_partial = jnp.einsum("ztm,tw->zmw", heads_in, d_branch, preferred_element_type=F32)
     o_grad = lax.psum_scatter(o_partial, "heads", scatter_dimension=0)
     o_grad = lax.psum(o_grad, "experts")
-
-    dqkv = attn_backward(qkv, d_heads, lse, seq_lengths, tables)
     w_partial = jnp.einsum("zsrm,zsrc->mc", gathered, dqkv, preferred_element_type=F32)
-    back = lax.all_to_all(dqkv, "heads", split_axis=0, concat_axis=0, tiled=True)
+    w_grad = lax.psum(w_partial, "experts").reshape(width, groups, 256)
     back = back.reshape(nh, tokens, groups * 256)
     d_attn = jnp.einsum("ztc,zmc->tm", back, w_full, preferred_element_type=F32)
-    w_grad = lax.psum(w_partial, "experts").reshape(width, groups, 256)
     wed = attn_gain * d_attn
     x_grad = d_mid + inv_one * wed - xf * (inv_one ** 3 * jnp.mean(wed * xf, axis=-1, keepdims=True))
     gain_one = jnp.sum(d_attn * xf * inv_one, axis=0)

time: 1130 us -> 975 us (0.86)
  Pallas kernels: 171 us -> 597 us
  waiting for transfers between devices: 573 us -> 155 us
  other arithmetic: 121 us -> 40.9 us
  starting transfers between devices: 97.7 us -> 22.5 us
    pallas_call x2 -> x4, Pallas kernels: 44.4 us -> 491 us  [the longest x1 264 us: last(): pl.pallas_call(functools.partial(last_kernel, first, count), in_specs=[hb...]
    ppermute x24 -> x0, waiting for transfers between devices: 258 us -> none  [the longest x8 236 us: heads_sum(): first = lax.ppermute(x, 'heads', [(0, 1), (3, 2)])]
    all_to_all x1 -> x0, waiting for transfers between devices: 146 us -> none  [body(): lax.all_to_all(d_heads, 'heads', split_axis=0, concat_axis=0, tiled=True)]
    convert_element_type x19 -> x1, other arithmetic: 67.3 us -> 2.04 us  [body(): out = (mid + moe_sum).astype(BF)]
    ppermute x22 -> x14, waiting for transfers between devices: 77.4 us -> 15.2 us  [swap(): return lax.ppermute(x, 'experts', [(i, i ^ bit) for i in range(n)])]
    ppermute x24 -> x0, starting transfers between devices: 58.5 us -> none  [the longest x8 32.4 us: heads_sum(): first = lax.ppermute(x, 'heads', [(0, 1), (3, 2)])]
    all_gather x1, waiting for transfers between devices: 0.01 us -> 49.1 us  [body(): w_full = lax.all_gather(w_piece, ('heads', 'experts'), axis=0, tiled=True)]
    pallas_call x4 -> x1, Pallas kernels: 81.2 us -> 60.4 us  [experts_call(): pl.pallas_call(functools.partial(expert_kernel, steps), grid=(count, step...]
  transfers between devices with their start and end apart: 55 -> 22, of which waited for: 19 -> 5; matrix products, arithmetic and copies ran while one was open for 18% -> 12% of each run, Pallas kernels for 15% -> 31%
where the time goes in v2:
time: 975 us; the launch traced here: 965 us
  Pallas kernels  597 us (61%)
  waiting for transfers between devices  155 us (16%)
  local copies, waits for them, and re-layouts  77.4 us (8%)
  other arithmetic  40.9 us (4%)
  blocking collectives  37.8 us (4%)
  starting transfers between devices  22.5 us (2%)
  matrix products  19.8 us (2%)
  between operations  14.7 us (2%)
    pallas_call x1, Pallas kernels, last(): pl.pallas_call(functools.partial(last_kernel, first, count), in_specs=[hb...  264 us
    pallas_call x1, Pallas kernels, middle(): pl.pallas_call(functools.partial(middle_kernel, count), in_specs=[pl.Bloc...  197 us
    pallas_call x1, Pallas kernels, experts_call(): pl.pallas_call(functools.partial(expert_kernel, steps), grid=(count, step...  60.4 us
    all_gather x1, waiting for transfers between devices, body(): lax.all_gather(attn_in.reshape(nseq, seg, width), 'heads', axis=0)  56.2 us
    all_gather x1, waiting for transfers between devices, body(): w_full = lax.all_gather(w_piece, ('heads', 'experts'), axis=0, tiled=True)  49.1 us
    psum x1, blocking collectives, body(): gain_one, gain_two = lax.psum((gain_one, gain_two), ('heads', 'experts'))  37.8 us
    unnamed x69, local copies, waits for them, and re-layouts  36.5 us
    pallas_call x2, Pallas kernels, combine(): pl.pallas_call(combine_kernel, grid=(sources,), in_specs=[pl.BlockSpec((1...  30.8 us
  transfers between devices with their start and end apart: 22, of which 5 were waited for; matrix products, arithmetic and copies ran while one was open for 12% of the time, Pallas kernels for 31%

profile of v2, /device:TPU:0, one launch (start us, length us, event | category | flops | bytes accessed | tf_op | source)
XLA Modules:
  0.0 964.5 jit_solution(6303897605250098152)
XLA Ops:
  9.0 2.5 fusion.8
  18.9 2.5 copy.138
  21.8 2.6 collective-permute-start.8
  27.3 4.2 all-to-all-start.1
  39.0 56.2 %all-gather.9.cloned.1.call-done = bf16[8,256,1024]{2,1,0:T(8,128)(2,1)} async-done(((bf16[2,256,1024]{2,1,0:T(8,128)(2,1)}), bf16[8,256,1024]{2,1,0:T(8,128)(2,1)}) %all-gather.9.cloned.1.call-update) | async-done | bytes 4194320 | tf_op jit(solution)/shard_map/all_gather | solution.py:773
  95.2 20.5 %attn_forward.1 = (bf16[2,2,1024,256]{3,2,1,0:T(8,128)(2,1)}, bf16[4,2,256,256]{3,2,1,0:T(8,128)(2,1)}, f32[2,2,4,512]{3,2,1,0:T(4,128)}) custom-call(s32[2]{0:T(128)} %len_ref.3, bf16[4,2,256,1024]{3,2,1,0:T(8,128)(2,1)} %bitcast.181, bf16[2,1024,256]{2,1,0:T(8,128)(2,1)} %fusion.39.w_ref, f32[1024,128]{1,0:T(8,128)} %get-tuple-element.98.cq, ...), custom_call_target="tpu_custom_call" | custom-call | flops 6000000000 | bytes 12582912 | tf_op jit(solution)/shard_map/attn_forward/pallas_call | solution.py:94
  115.6 4.3 all-to-all-start
  125.8 4.3 convert_bitcast_fusion.1
  130.1 2.8 copy.137.slot_ref
  142.2 20.9 %all-gather.5.cloned.1.call-done = bf16[1024,1024]{1,0:T(8,128)(2,1)} async-done(((bf16[32,1024]{1,0:T(8,128)(2,1)}), bf16[1024,1024]{1,0:T(8,128)(2,1)}) %all-gather.5.cloned.1.call-update) | async-done | bytes 2097168 | tf_op jit(solution)/shard_map/all_gather | solution.py:784
  163.1 3.5 multiply_reduce_fusion
  181.0 15.2 %collective-permute-done.1 = bf16[512,1024]{1,0:T(8,128)(2,1)} collective-permute-done((bf16[512,1024]{1,0:T(8,128)(2,1)}, bf16[512,1024]{1,0:T(8,128)(2,1)}, u32[]{:S(2)}, u32[]{:S(2)}) %collective-permute-start.1) | collective-permute-done | bytes 1048608 | tf_op jit(solution)/shard_map/ppermute | solution.py:382
  196.2 12.5 %gather_rows.3.d_ref = bf16[4,8,160,1024]{3,2,1,0:T(8,128)(2,1)} custom-call(s32[8,4,512]{2,1,0:T(4,128)} %copy.137.slot_ref, f32[8,4,512]{2,1,0:T(4,128)} %get-tuple-element.99.refs_0_, bf16[8,512,1024]{2,1,0:T(8,128)(2,1)} %bitcast_dynamic-update-slice_fusion.refs_1_), custom_call_target="tpu_custom_call" | custom-call | flops 5368709120 | bytes 18874368 | tf_op jit(solution)/shard_map/gather_rows/pallas_call | solution.py:232
  208.7 49.1 %all-gather.7.cloned.1.call-done = bf16[4096,512]{0,1:T(8,128)(2,1)} async-done(((bf16[128,512]{0,1:T(8,128)(2,1)}), bf16[4096,512]{0,1:T(8,128)(2,1)}) %all-gather.7.cloned.1.call-update) | async-done | bytes 4194320 | tf_op jit(solution)/shard_map/all_gather | solution.py:785
  257.8 6.5 copy.144
  275.7 12.0 %gather_rows.2.x_ref = bf16[4,8,160,1024]{3,2,1,0:T(8,128)(2,1)} custom-call(s32[8,4,512]{2,1,0:T(4,128)} %copy.137.slot_ref, bf16[8,512,1024]{2,1,0:T(8,128)(2,1)} %bitcast_dynamic-update-slice_fusion.8.refs_0_), custom_call_target="tpu_custom_call" | custom-call | flops 5368709120 | bytes 18874368 | tf_op jit(solution)/shard_map/gather_rows/pallas_call | solution.py:232
  287.7 60.4 %experts.1 = (bf16[4,8,160,1024]{3,2,1,0:T(8,128)(2,1)}, bf16[4,8,160,1024]{3,2,1,0:T(8,128)(2,1)}, bf16[4,1536,1024]{2,1,0:T(8,128)(2,1)}) custom-call(s32[8,4,1,512]{3,2,1,0:T(1,128)} %copy.141.slot_ref, f32[8,4,1,512]{3,2,1,0:T(1,128)} %bitcast.170, bf16[4,8,160,1024]{3,2,1,0:T(8,128)(2,1)} %gather_rows.2.x_ref, ...), custom_call_target="tpu_custom_call" | custom-call | flops 48318382080 | bytes 67108864 | tf_op jit(solution)/shard_map/experts/pallas_call | solution.py:313
  348.1 15.4 %combine.3.parts_ref = bf16[8,512,1024]{2,1,0:T(8,128)(2,1)} custom-call(s32[8,512,4]{2,1,0:T(8,128)} %get-tuple-element.92.slot_ref, bf16[4,8,160,1024]{3,2,1,0:T(8,128)(2,1)} %get-tuple-element.29.row_ref), custom_call_target="tpu_custom_call" | custom-call | flops 5368709120 | bytes 18874368 | tf_op jit(solution)/shard_map/combine/pallas_call | solution.py:362
  363.5 15.4 %combine.2.parts_ref = bf16[8,512,1024]{2,1,0:T(8,128)(2,1)} custom-call(s32[8,512,4]{2,1,0:T(8,128)} %get-tuple-element.92.slot_ref, bf16[4,8,160,1024]{3,2,1,0:T(8,128)(2,1)} %get-tuple-element.28.row_ref), custom_call_target="tpu_custom_call" | custom-call | flops 5368709120 | bytes 18874368 | tf_op jit(solution)/shard_map/combine/pallas_call | solution.py:362
  378.9 196.7 %middle.1 = (bf16[3072,1024]{1,0:T(8,128)(2,1)}, f32[512,1024]{1,0:T(8,128)}, bf16[512,1024]{1,0:T(8,128)(2,1)}, f32[1,1024]{1,0:T(1,128)}, bf16[4,2,256,512]{3,2,1,0:T(8,128)(2,1)}) custom-call(s32[2]{0:T(128)} %len_ref.3, bf16[6144,1024]{1,0:T(8,128)(2,1)} %bitcast.185, bf16[8,512,1024]{2,1,0:T(8,128)(2,1)} %combine.3.parts_ref, f32[512,1024]{1,0:T(8,128)} %copy-done.5, ...), custom_call_target="tpu_custom_call" | custom-call | flops 99999997952 | bytes 31457280 | tf_op jit(solution)/shard_map/middle/pallas_call | solution.py:663
  575.6 4.8 fusion.14
  580.5 4.5 all-to-all-start.2
  585.1 263.9 %last.1 = (bf16[3072,1024]{1,0:T(8,128)(2,1)}, bf16[7,512,1024]{2,1,0:T(8,128)(2,1)}) custom-call(bf16[6144,1024]{1,0:T(8,128)(2,1)} %bitcast.186, bf16[8,512,1024]{2,1,0:T(8,128)(2,1)} %combine.2.parts_ref), custom_call_target="tpu_custom_call" | custom-call | flops 199999995904 | bytes 31457280 | tf_op jit(solution)/shard_map/last/pallas_call | solution.py:719
  849.0 4.3 slice.50
  859.3 5.2 convert_reduce_fusion
  868.7 5.3 fusion
  874.0 6.5 pad_maximum_fusion
  880.5 8.6 pad_maximum_fusion.1
  889.1 5.8 fusion.13
  895.5 2.9 copy.173
  898.5 37.8 %all-reduce = (f32[1024]{0:T(1024)}, f32[1024]{0:T(1024)}) all-reduce(f32[1024]{0:T(1024)S(1)} %get-tuple-element.82, f32[1024]{0:T(1024)S(1)} %bitcast.178), channel_id=1, replica_groups=mesh['heads'=4,'experts'=8] {'heads','experts'}, use_global_device_ids=true, to_apply=%region_7.8 | all-reduce | flops 2048 | bytes 16384 | tf_op jit(solution)/shard_map/psum | solution.py:847
  936.2 13.1 %all-reduce.4.cloned.1.call-done = (f32[1024,2,256]{0,2,1:T(8,128)}, f32[256,1024]{1,0:T(8,128)}) async-done(((f32[1024,2,256]{0,2,1:T(8,128)}, f32[256,1024]{1,0:T(8,128)}), (f32[1024,2,256]{0,2,1:T(8,128)}, f32[256,1024]{1,0:T(8,128)})) %all-reduce.4.cloned.1.call-update) | async-done | bytes 3145744 | tf_op jit(solution)/shard_map/psum | solution.py:841
  (154 shorter events, 79.7 us)
Async XLA Ops:
  7.2 87.9 %all-gather.9.cloned.1.call-start = ((), (), s32[]{:S(2)}) async-start(), calls=%async_computation.7 | async-start | bytes 5242880 | tf_op jit(solution)/shard_map/all_gather | solution.py:773
  11.5 151.5 %all-gather.5.cloned.1.call-start = ((), (), s32[]{:S(2)}) async-start(), calls=%async_computation.4 | async-start | bytes 2162688 | tf_op jit(solution)/shard_map/all_gather | solution.py:784
  12.3 245.5 %all-gather.7.cloned.1.call-start = ((), (), s32[]{:S(2)}) async-start(), calls=%async_computation.5 | async-start | bytes 4325376 | tf_op jit(solution)/shard_map/all_gather | solution.py:785
  13.3 12.7 %copy-start.18 = (s32[2]{0:T(128)S(1)}, s32[2]{0:T(128)}, u32[]{:S(2)}) copy-start(s32[2]{0:T(128)} %len_ref.3) | copy-start | bytes 28
  13.3 12.7 %copy-start.17 = (s32[256,2]{0,1:T(2,128)S(1)}, s32[256,2]{0,1:T(2,128)}, u32[]{:S(2)}) copy-start(s32[256,2]{0,1:T(2,128)} %param.18) | copy-start | bytes 6148
  13.3 12.7 %copy-start.11 = (s32[256,2,8]{0,2,1:T(8,128)S(1)}, s32[256,2,8]{0,2,1:T(8,128)}, u32[]{:S(2)}) copy-start(s32[256,2,8]{0,2,1:T(8,128)} %param.16) | copy-start | bytes 49156
  13.5 13.0 %copy-start.14 = (f32[256,2,8]{0,2,1:T(8,128)S(1)}, f32[256,2,8]{0,2,1:T(8,128)}, u32[]{:S(2)}) copy-start(f32[256,2,8]{0,2,1:T(8,128)} %param.17) | copy-start | bytes 49156
  13.8 17.7 %copy-start.3 = (bf16[256,2,1024]{2,1,0:T(2,128)(2,1)S(1)}, bf16[256,2,1024]{2,1,0:T(2,128)(2,1)}, u32[]{:S(2)}) copy-start(bf16[256,2,1024]{2,1,0:T(2,128)(2,1)} %param.14) | copy-start | bytes 3145732
  21.4 114.0 %collective-permute-start.7 = (bf16[512,1024]{1,0:T(8,128)(2,1)}, bf16[512,1024]{1,0:T(8,128)(2,1)}, u32[]{:S(2)}, u32[]{:S(2)}) collective-permute-start(bf16[512,1024]{1,0:T(8,128)(2,1)} %bitcast.32.grad_ref), channel_id=1, source_target_pairs={{0,1},{1,0},{2,3},{3,2},{4,5},{5,4},{6,7},{7,6},{8,9},{9,8},{10,11... | collective-permute-start | bytes 3145736 | tf_op jit(solution)/shard_map/ppermute | solution.py:382
  21.8 101.2 %collective-permute-start.8 = (bf16[512,1024]{1,0:T(8,128)(2,1)}, bf16[512,1024]{1,0:T(8,128)(2,1)}, u32[]{:S(2)}, u32[]{:S(2)}) collective-permute-start(bf16[512,1024]{1,0:T(8,128)(2,1)} %bitcast.32.grad_ref), channel_id=1, source_target_pairs={{0,2},{1,3},{2,0},{3,1},{4,6},{5,7},{6,4},{7,5},{8,10},{9,11},{10,... | collective-permute-start | bytes 3145736 | tf_op jit(solution)/shard_map/ppermute | solution.py:382
  24.4 110.4 %collective-permute-start.10 = (bf16[512,1024]{1,0:T(8,128)(2,1)}, bf16[512,1024]{1,0:T(8,128)(2,1)}, u32[]{:S(2)}, u32[]{:S(2)}) collective-permute-start(bf16[512,1024]{1,0:T(8,128)(2,1)} %bitcast.32.grad_ref), channel_id=1, source_target_pairs={{0,4},{1,5},{2,6},{3,7},{4,0},{5,1},{6,2},{7,3},{8,12},{9,13},{10,... | collective-permute-start | bytes 3145736 | tf_op jit(solution)/shard_map/ppermute | solution.py:382
  25.9 109.4 %collective-permute-start.12 = (bf16[512,1024]{1,0:T(8,128)(2,1)}, bf16[512,1024]{1,0:T(8,128)(2,1)}, u32[]{:S(2)}, u32[]{:S(2)}) collective-permute-start(bf16[512,1024]{1,0:T(8,128)(2,1)} %bitcast.32.grad_ref), channel_id=1, source_target_pairs={{0,6},{1,7},{2,4},{3,5},{4,2},{5,3},{6,0},{7,1},{8,14},{9,15},{10,... | collective-permute-start | bytes 3145736 | tf_op jit(solution)/shard_map/ppermute | solution.py:382
  27.3 88.3 %all-to-all-start.1 = ((f32[8,2,4,512]{3,2,1,0:T(4,128)}), f32[8,2,4,512]{3,2,1,0:T(4,128)S(1)}, u32[]{:S(2)}, u32[]{:S(2)}) async-start(f32[8,2,4,512]{3,2,1,0:T(4,128)} %pad_maximum_fusion.7), calls=%async_computation.1 | async-start | bytes 262144 | tf_op jit(solution)/shard_map/all_to_all | solution.py:765
  115.6 47.4 %all-to-all-start = ((bf16[4,2,256,256]{3,2,1,0:T(8,128)(2,1)}), bf16[4,2,256,256]{3,2,1,0:T(8,128)(2,1)}, u32[]{:S(2)}, u32[]{:S(2)}) async-start(bf16[4,2,256,256]{3,2,1,0:T(8,128)(2,1)} %get-tuple-element.26), calls=%async_computation | async-start | bytes 2097152 | tf_op jit(solution)/shard_map/all_to_all | solution.py:790
  119.9 760.5 %reduce-scatter.2.cloned.1.call-start = ((), (), s32[]{:S(2)}) async-start(), calls=%async_computation.6 | async-start | bytes 5242880 | tf_op jit(solution)/shard_map/reduce_scatter | solution.py:838
  123.1 16.8 %collective-permute-start.9 = (bf16[512,1024]{1,0:T(8,128)(2,1)}, bf16[512,1024]{1,0:T(8,128)(2,1)}, u32[]{:S(2)}, u32[]{:S(2)}) collective-permute-start(bf16[512,1024]{1,0:T(8,128)(2,1)} %collective-permute-done.8), channel_id=1, source_target_pairs={{0,1},{1,0},{2,3},{3,2},{4,5},{5,4},{6,7},{7,6},{8,9},{9,8},{10,11... | collective-permute-start | bytes 3145736 | tf_op jit(solution)/shard_map/ppermute | solution.py:382
  134.8 37.3 %collective-permute-start.11 = (bf16[512,1024]{1,0:T(8,128)(2,1)}, bf16[512,1024]{1,0:T(8,128)(2,1)}, u32[]{:S(2)}, u32[]{:S(2)}) collective-permute-start(bf16[512,1024]{1,0:T(8,128)(2,1)} %collective-permute-done.10), channel_id=1, source_target_pairs={{0,1},{1,0},{2,3},{3,2},{4,5},{5,4},{6,7},{7,6},{8,9},{9,8},{10,11... | collective-permute-start | bytes 3145736 | tf_op jit(solution)/shard_map/ppermute | solution.py:382
  135.3 43.4 %collective-permute-start.13 = (bf16[512,1024]{1,0:T(8,128)(2,1)}, bf16[512,1024]{1,0:T(8,128)(2,1)}, u32[]{:S(2)}, u32[]{:S(2)}) collective-permute-start(bf16[512,1024]{1,0:T(8,128)(2,1)} %collective-permute-done.12), channel_id=1, source_target_pairs={{0,1},{1,0},{2,3},{3,2},{4,5},{5,4},{6,7},{7,6},{8,9},{9,8},{10,11... | collective-permute-start | bytes 3145736 | tf_op jit(solution)/shard_map/ppermute | solution.py:382
  142.2 24.4 %copy-start.15 = (f32[1024]{0:T(1024)S(1)}, f32[1024]{0:T(1024)}, u32[]{:S(2)}) copy-start(f32[1024]{0:T(1024)} %param.20) | copy-start | bytes 12292
  168.4 27.7 %collective-permute-start.1 = (bf16[512,1024]{1,0:T(8,128)(2,1)}, bf16[512,1024]{1,0:T(8,128)(2,1)}, u32[]{:S(2)}, u32[]{:S(2)}) collective-permute-start(bf16[512,1024]{1,0:T(8,128)(2,1)} %get-tuple-element.89), channel_id=1, source_target_pairs={{0,2},{1,3},{2,0},{3,1},{4,6},{5,7},{6,4},{7,5},{8,10},{9,11},{10,... | collective-permute-start | bytes 3145736 | tf_op jit(solution)/shard_map/ppermute | solution.py:382
  174.4 90.3 %collective-permute-start = (bf16[512,1024]{1,0:T(8,128)(2,1)}, bf16[512,1024]{1,0:T(8,128)(2,1)}, u32[]{:S(2)}, u32[]{:S(2)}) collective-permute-start(bf16[512,1024]{1,0:T(8,128)(2,1)} %get-tuple-element.89), channel_id=1, source_target_pairs={{0,1},{1,0},{2,3},{3,2},{4,5},{5,4},{6,7},{7,6},{8,9},{9,8},{10,11... | collective-permute-start | bytes 3145736 | tf_op jit(solution)/shard_map/ppermute | solution.py:382
  174.4 89.8 %collective-permute-start.3 = (bf16[512,1024]{1,0:T(8,128)(2,1)}, bf16[512,1024]{1,0:T(8,128)(2,1)S(1)}, u32[]{:S(2)}, u32[]{:S(2)}) collective-permute-start(bf16[512,1024]{1,0:T(8,128)(2,1)} %get-tuple-element.89), channel_id=1, source_target_pairs={{0,4},{1,5},{2,6},{3,7},{4,0},{5,1},{6,2},{7,3},{8,12},{9,13},{10,... | collective-permute-start | bytes 3145736 | tf_op jit(solution)/shard_map/ppermute | solution.py:382
  175.0 89.5 %collective-permute-start.5 = (bf16[512,1024]{1,0:T(8,128)(2,1)}, bf16[512,1024]{1,0:T(8,128)(2,1)S(1)}, u32[]{:S(2)}, u32[]{:S(2)}) collective-permute-start(bf16[512,1024]{1,0:T(8,128)(2,1)} %get-tuple-element.89), channel_id=1, source_target_pairs={{0,6},{1,7},{2,4},{3,5},{4,2},{5,3},{6,0},{7,1},{8,14},{9,15},{10,... | collective-permute-start | bytes 3145736 | tf_op jit(solution)/shard_map/ppermute | solution.py:382
  196.2 73.1 %collective-permute-start.2 = (bf16[512,1024]{1,0:T(8,128)(2,1)}, bf16[512,1024]{1,0:T(8,128)(2,1)}, u32[]{:S(2)}, u32[]{:S(2)}) collective-permute-start(bf16[512,1024]{1,0:T(8,128)(2,1)} %collective-permute-done.1), channel_id=1, source_target_pairs={{0,1},{1,0},{2,3},{3,2},{4,5},{5,4},{6,7},{7,6},{8,9},{9,8},{10,11... | collective-permute-start | bytes 3145736 | tf_op jit(solution)/shard_map/ppermute | solution.py:382
  264.3 8.4 collective-permute-start.4
  264.5 10.2 %collective-permute-start.6 = (bf16[512,1024]{1,0:T(8,128)(2,1)S(1)}, bf16[512,1024]{1,0:T(8,128)(2,1)S(1)}, u32[]{:S(2)}, u32[]{:S(2)}) collective-permute-start(bf16[512,1024]{1,0:T(8,128)(2,1)S(1)} %collective-permute-done.5), channel_id=1, source_target_pairs={{0,1},{1,0},{2,3},{3,2},{4,5},{5,4},{6,7},{7,6},{8,9},{9,8},{10,11... | collective-permute-start | bytes 3145736 | tf_op jit(solution)/shard_map/ppermute | solution.py:382
  580.5 308.6 %all-to-all-start.2 = ((bf16[4,2,256,512]{3,2,1,0:T(8,128)(2,1)}), bf16[4,2,256,512]{3,2,1,0:T(8,128)(2,1)}, u32[]{:S(2)}, u32[]{:S(2)}) async-start(bf16[4,2,256,512]{3,2,1,0:T(8,128)(2,1)} %get-tuple-element.37), calls=%async_computation.2 | async-start | bytes 4194304 | tf_op jit(solution)/shard_map/all_to_all | solution.py:814
  585.0 364.3 %all-reduce.4.cloned.1.call-start = ((), (), s32[]{:S(2)}) async-start(), calls=%async_computation.8 | async-start | bytes 6291456 | tf_op jit(solution)/shard_map/psum | solution.py:841
  880.5 8.6 copy-start.4
  880.5 8.6 copy-start.12
  880.5 8.6 copy-start.13
  949.3 8.2 copy-start.1
  (12 other events, 60.8 us)
Sparse Core Ops, SparseCore 0:
  11.7 83.4 all-gather.8
  98.0 65.0 all-gather.4
  165.9 91.8 all-gather.6
  580.6 139.4 reduce-scatter.1
  880.6 68.6 all-reduce.3

commit v3 on v2

--- a/solution.py
+++ b/solution.py
@@ -15,7 +15,7 @@
 F32 = jnp.float32
 SCALE = HEAD ** (-0.5)
 NEG = -1e30
-VMEM = 60 * 1024 * 1024
+VMEM = 63 * 1024 * 1024
 MESH = pl.DeviceIdType.MESH
 DMA = pltpu.SemaphoreType.DMA
 
@@ -44,9 +44,8 @@
 
 
 def attn_mask(offset, n, block, length):
-    key = lax.broadcasted_iota(jnp.int32, (n, 2 * block), 0)
-    query = lax.broadcasted_iota(jnp.int32, (n, 2 * block), 1)
-    query = jnp.where(query >= block, query - block, query) + offset
+    key = lax.broadcasted_iota(jnp.int32, (n, block), 0)
+    query = lax.broadcasted_iota(jnp.int32, (n, block), 1) + offset
     return (key <= query) & (key < length)
 
 
@@ -76,7 +75,8 @@
         n = (i + 1) * block
         q2 = two_heads(q[i * block : n])
         s = dot_nt(k[:n], q2)
-        s = jnp.where(attn_mask(i * block, n, block, length), s * SCALE, NEG)
+        mask = attn_mask(i * block, n, block, length)
+        s = jnp.where(jnp.concatenate([mask, mask], axis=1), s * SCALE, NEG)
         m = jnp.max(s, axis=0, keepdims=True)
         e = jnp.exp(s - m)
         total = jnp.sum(e, axis=0, keepdims=True)
@@ -128,16 +128,20 @@
     for i in range(full // block):
         n = (i + 1) * block
         rows = pl.ds(i * block, block)
-        q2 = two_heads(q[i * block : n])
-        do2 = two_heads(heads(i))
-        s = dot_nt(k[:n], q2)
-        p = jnp.exp(jnp.where(attn_mask(i * block, n, block, length), s * SCALE - lses(i), NEG))
-        dp = dot_nt(v[:n], do2)
-        delta = jnp.sum(p * dp, axis=0, keepdims=True)
-        ds = (p * (dp - delta) * SCALE).astype(BF)
-        dkv_ref[:n, :HEAD] += dot(ds, q2)
-        dkv_ref[:n, HEAD:] += dot(p.astype(BF), do2)
-        dq = untwo(dot(kt[:, :n], ds), block)
+        mask = attn_mask(i * block, n, block, length)
+        grads = []
+        for h in range(2):
+            qh = q[i * block : n, h * HEAD : (h + 1) * HEAD]
+            doh = heads(i)[:, h * HEAD : (h + 1) * HEAD]
+            s = dot_nt(k[:n], qh)
+            p = jnp.exp(jnp.where(mask, s * SCALE - lses(i)[:, h * block : (h + 1) * block], NEG))
+            dp = dot_nt(v[:n], doh)
+            delta = jnp.sum(p * dp, axis=0, keepdims=True)
+            ds = (p * (dp - delta) * SCALE).astype(BF)
+            dkv_ref[:n, :HEAD] += dot(ds, qh)
+            dkv_ref[:n, HEAD:] += dot(p.astype(BF), doh)
+            grads.append(dot(kt[:, :n], ds))
+        dq = jnp.concatenate(grads, axis=0).T
         dq = dq * cq[rows, :] - swap_halves(dq) * sq[rows, :]
         put(i, 0, dq.astype(BF))
     dkv = dkv_ref[...]
@@ -418,6 +422,29 @@
     return jnp.where((z == 1) | (z == 2), total, third).astype(F32)
 
 
+def weight_sums(heads_in, d_branch, gathered, dqkv, ne):
+    nh, tokens, part = heads_in.shape
+    width, cols = d_branch.shape[1], dqkv.shape[2]
+    col, row = width // ne, width // ne
+    o = jnp.einsum("ztm,tew->ezmw", heads_in, d_branch.reshape(tokens, ne, col), preferred_element_type=F32)
+    w = jnp.einsum("ztm,ztc->mc", gathered.reshape(nh, tokens, width), dqkv, preferred_element_type=F32)
+    cut = cols // col
+    w = jnp.swapaxes(w.reshape(ne, row, cut, col), 1, 2).reshape(ne, cut * row, col)
+    both = jnp.concatenate([o.reshape(ne, nh * part, col), w], axis=1)
+    both = lax.psum_scatter(both, "experts", scatter_dimension=0)
+    o, w = both[: nh * part], both[nh * part :]
+    o = lax.psum_scatter(o.reshape(nh, part, col), "heads", scatter_dimension=0)
+    return weight_split(lax.all_gather(jnp.concatenate([o, w], axis=0), "experts", axis=0), part, cols)
+
+
+def weight_split(both, part, cols):
+    ne, _, col = both.shape
+    width, row, cut = ne * col, col, cols // col
+    o = jnp.swapaxes(both[:, :part], 0, 1).reshape(part, width)
+    w = jnp.swapaxes(both[:, part:].reshape(ne, cut, row, col), 1, 2)
+    return o, w.reshape(width, cols)
+
+
 CHUNK = 256
 LAG = 3
 
@@ -455,7 +482,7 @@
         return pltpu.make_async_copy(self.piece(k), self.buf.at[lax.rem(k, 2)], self.ls.at[lax.rem(k, 2)])
 
     def store(self, ref, k):
-        return pltpu.make_async_copy(ref.at[k], self.out.at[pl.ds(k * CHUNK, CHUNK)], self.os.at[k])
+        return pltpu.make_async_copy(ref.at[k], self.out.at[pl.ds((self.first + k) * CHUNK, CHUNK)], self.os.at[k])
 
     def up(self, k):
         return remote(self.piece(k), self.a.at[k], self.s1.at[k], self.r1.at[k], "heads", self.outer)
@@ -556,47 +583,147 @@
     ]
 
 
-def middle_kernel(count, len_ref, sum_ref, parts_ref, mid_ref, grad_ref, gain_ref, o_ref, qkv_ref, lse_ref,
-                  cq, sq, ckv, skv, total_ref, dmid_ref, dbranch_ref, gtwo_ref, dqkv_ref,
-                  c_buf, e_buf, f_buf, hs, hr, dmoe, dkv, cs, cr, fs, fr, hss, hrs, *chain):
-    nh, nseq, seg, _ = dqkv_ref.shape
-    groups = qkv_ref.shape[1]
-    tokens = nseq * seg
-    z, me = lax.axis_index("heads"), lax.axis_index("experts")
-    chain = Chain(sum_ref, total_ref, chain, 0, count)
+class PlaneSum:
+    order = (3, 1, 2)
+
+    def __init__(self, rows, slots, total, scratch):
+        self.rows, self.slots, self.total = rows, slots, total
+        self.buf, self.odd, self.c, self.e, self.f, self.ls, self.cs, self.cr, self.fs, self.fr = scratch
+        self.me = lax.axis_index("experts")
+        self.here, _, self.cap, self.width = rows.shape
+
+    def load(self, r, at):
+        return [
+            pltpu.make_async_copy(self.rows.at[j, r], self.buf.at[at, j], self.ls.at[at, j])
+            for j in range(self.here)
+        ]
+
+    def core(self, i):
+        return remote(self.odd.at[i], self.c.at[i], self.cs.at[i], self.cr.at[i], "experts", self.me ^ 1)
+
+    def chip(self, i):
+        return remote(self.e.at[i - 1], self.f.at[i - 1], self.fs.at[i - 1], self.fr.at[i - 1], "experts", self.me ^ (2 * i))
+
+    def part(self, r, at, after, after_at):
+        if after is not None:
+            for c in self.load(after, after_at):
+                c.start()
+        slots = self.slots[r].T.astype(jnp.int32)
+        lane = lax.broadcasted_iota(jnp.int32, (slots.shape[0], self.here * self.cap), 1)
+        hot = None
+        for j in range(self.here):
+            col = slots[:, j : j + 1]
+            hit = lane == jnp.where(col >= 0, col + j * self.cap, -1)
+            hot = hit if hot is None else hot | hit
+        for c in self.load(r, at):
+            c.wait()
+        rows = self.buf[at].reshape(self.here * self.cap, self.width)
+        return dot(hot.astype(F32).astype(BF), rows)
+
+    def run(self, chain, step):
+        turns = [2 * i + 1 for i in self.order + (0,)] + [2 * i for i in self.order + (0,)]
+        for c in self.load(turns[0], 0):
+            c.start()
+        for t, r in enumerate(turns):
+            after = turns[t + 1] if t + 1 < len(turns) else None
+            value = self.part(r, t % 2, after, (t + 1) % 2)
+            i = r // 2
+            if r % 2:
+                self.odd[i] = value.astype(BF)
+                self.core(i).start()
+            else:
+                self.core(i).wait_recv()
+                value = value + self.c[i].astype(F32)
+                if i:
+                    self.e[i - 1] = value.astype(BF)
+                    self.chip(i).start()
+                else:
+                    self.total[...] = value
+            if t == 3:
+                chain.run(step, step + 1)
+        chain.run(step + 1, step + 4)
+        for i in self.order:
+            self.chip(i).wait_recv()
+        return step + 4
+
+    def rows_total(self, rows):
+        d = self.total[rows]
+        for r in range(3):
+            d = d + self.f[r, rows].astype(F32)
+        return d
+
+    def finish(self):
+        for i in range(4):
+            self.core(i).wait_send()
+        for i in self.order:
+            self.chip(i).wait_send()
+
+
+def plane_scratch(here, cap, tokens, width):
+    return [
+        pltpu.VMEM((2, here, cap, width), BF),
+        pltpu.VMEM((4, tokens, width), BF),
+        pltpu.VMEM((4, tokens, width), BF),
+        pltpu.VMEM((3, tokens, width), BF),
+        pltpu.VMEM((3, tokens, width), BF),
+        DMA((2, here)),
+        DMA((4,)),
+        DMA((4,)),
+        DMA((3,)),
+        DMA((3,)),
+    ]
+
+
+PLANE = 10
+
+
+class Exchange:
+    def __init__(self, src, dst, send, recv, nh):
+        self.src, self.dst, self.ss, self.rs, self.nh = src, dst, send, recv, nh
+        self.z = lax.axis_index("heads")
+
+    def send(self, d):
+        to = lax.rem(self.z + d, self.nh)
+        return remote(self.src.at[to], self.dst.at[self.z], self.ss.at[d], self.rs.at[d], "heads", to)
+
+    def start(self):
+        for d in range(1, self.nh):
+            self.send(d).start()
+        own = pl.ds(self.z, 1)
+        self.dst[own] = self.src[own]
+
+    def wait_recv(self):
+        for d in range(1, self.nh):
+            at = lax.rem(self.z + self.nh - d, self.nh)
+            remote(self.src.at[at], self.dst.at[at], self.ss.at[d], self.rs.at[d], "heads", at).wait_recv()
+
+    def finish(self):
+        for d in range(1, self.nh):
+            self.send(d).wait_send()
+
+
+ROWS = 128
+
+
+def middle_kernel(count, len_ref, sum_ref, rows_ref, slot_ref, mid_ref, grad_ref, gain_ref, o_ref, qkv_ref, lse_ref,
+                  cq, sq, ckv, skv, hin_ref, x_ref, total_ref, dmid_ref, gtwo_ref, dqkv_ref, parts_ref,
+                  dbranch_ref, hs, hr, dmoe, dkv, hss, hrs, xs, *scratch):
+    nh, tokens, _ = dqkv_ref.shape
+    nseq, groups = qkv_ref.shape[:2]
+    seg = tokens // nseq
+    chain = Chain(sum_ref, total_ref, scratch[PLANE:], 0, count)
+    plane = PlaneSum(rows_ref, slot_ref, dmoe, scratch[:PLANE])
+    heads = Exchange(hs, hr, hss, hrs, nh)
     greet(nh, (1, 2, 4, 6))
-
-    def core(i):
-        return remote(parts_ref.at[2 * i + 1], c_buf.at[i], cs.at[i], cr.at[i], "experts", me ^ 1)
-
-    def chip(i):
-        return remote(e_buf.at[i - 1], f_buf.at[i - 1], fs.at[i - 1], fr.at[i - 1], "experts", me ^ (2 * i))
-
-    order = (3, 1, 2)
-    for i in order + (0,):
-        core(i).start()
     chain.begin()
     chain.run(0, 1)
-    for i in order:
-        core(i).wait_recv()
-        e_buf[i - 1] = (parts_ref[2 * i].astype(F32) + c_buf[i].astype(F32)).astype(BF)
-        chip(i).start()
-    chain.run(1, 2)
-    core(0).wait_recv()
-    dmoe[...] = parts_ref[0].astype(F32) + c_buf[0].astype(F32)
-    chain.run(2, 5)
-    for i in order:
-        chip(i).wait_recv()
-
+    step = plane.run(chain, 1)
     gtwo_ref[...] = jnp.zeros_like(gtwo_ref)
-    rows_at = 128
-
-    @pl.loop(0, tokens // rows_at)
+
+    @pl.loop(0, tokens // ROWS)
     def _(i):
-        rows = pl.ds(i * rows_at, rows_at)
-        d = dmoe[rows]
-        for r in range(3):
-            d = d + f_buf[r, rows].astype(F32)
+        rows = pl.ds(i * ROWS, ROWS)
+        d = plane.rows_total(rows)
         m = mid_ref[rows]
         inv = lax.rsqrt(jnp.mean(m * m, axis=-1, keepdims=True) + EPS)
         zed = gain_ref[...] * d
@@ -608,129 +735,277 @@
         for h in range(nh):
             hs[h, rows] = dot_nt(db, o_ref[h]).astype(BF)
 
-    def send(d):
-        to = lax.rem(z + d, nh)
-        return remote(hs.at[to], hr.at[z], hss.at[d], hrs.at[d], "heads", to)
-
-    def arrive(d):
-        src = lax.rem(z + nh - d, nh)
-        return remote(hs.at[src], hr.at[src], hss.at[d], hrs.at[d], "heads", src)
-
-    for d in range(1, nh):
-        send(d).start()
-    hr[pl.ds(z, 1)] = hs[pl.ds(z, 1)]
-    chain.run(5, 8)
-    for d in range(1, nh):
-        arrive(d).wait_recv()
+    heads.start()
+    chain.run(step, step + 3)
+    step = step + 3
+    heads.wait_recv()
 
     @pl.loop(0, nseq)
     def _(s):
         length = len_ref[s]
+        at = pl.ds(s * seg, seg)
         for g in range(groups):
             def put(i, lo, v):
-                dqkv_ref[i, s, :, g * 256 + lo : g * 256 + lo + 128] = v
+                dqkv_ref[i, at, g * 256 + lo : g * 256 + lo + 128] = v
 
             bwd_piece(
                 qkv_ref[s, g, :, :128],
                 qkv_ref[s, g, :, 128:],
-                lambda i: hr[i, pl.ds(s * seg, seg), g * 128 : (g + 1) * 128],
+                lambda i: hr[i, at, g * 128 : (g + 1) * 128],
                 lambda i: lse_ref[s, g, i : i + 1, :],
                 length,
                 (cq, sq, ckv, skv),
                 dkv,
                 put,
             )
-        chain.step(8 + s)
-
-    chain.run(8 + nseq, chain.steps())
+        chain.step(step + s)
+
+    step = step + nseq
+    for i in range(4):
+        plane.core(i).wait_send()
+    load = pltpu.make_async_copy(x_ref, plane.odd, xs)
+    load.start()
+    ne, _, col = parts_ref.shape
+    part = hin_ref.shape[2]
+    db = dbranch_ref[...]
+    for h in range(nh):
+        o = dot_tn(hin_ref[h], db)
+        for e in range(ne):
+            parts_ref[e, h * part : (h + 1) * part] = o[:, e * col : (e + 1) * col]
+    chain.run(step, step + 1)
+    load.wait()
+    wsum = dmoe
+    wsum[...] = dot_tn(dqkv_ref[0], plane.odd[0])
+    for h in range(1, nh):
+        wsum[...] += dot_tn(dqkv_ref[h], plane.odd[h])
+    row = wsum.shape[1] // ne
+    for e in range(ne):
+        for c in range(wsum.shape[0] // col):
+            at = nh * part + c * row
+            parts_ref[e, at : at + row] = wsum[c * col : (c + 1) * col, e * row : (e + 1) * row].T
+    chain.run(step + 1, chain.steps())
     chain.finish()
-    for i in range(4):
-        core(i).wait_send()
-    for i in order:
-        chip(i).wait_send()
-    for d in range(1, nh):
-        send(d).wait_send()
-
-
-def middle(count, lengths, sums, parts, mid, grad, gain, o_parts, qkv, lse, tables):
+    for i in plane.order:
+        plane.chip(i).wait_send()
+    heads.finish()
+
+
+def middle(count, lengths, sums, rows, slots, mid, grad, gain, o_parts, qkv, lse, tables, heads_in, x):
     nseq, groups, full, _ = qkv.shape
     nh = o_parts.shape[0]
     tokens, width = mid.shape
-    seg = tokens // nseq
+    here, ne, cap, _ = rows.shape
     vmem = pl.BlockSpec(memory_space=pltpu.VMEM)
     hbm = pl.BlockSpec(memory_space=pl.ANY)
     heads = (nh, tokens, groups * 128)
+    col = width // ne
+    cols = groups * 256
     return pl.pallas_call(
         functools.partial(middle_kernel, count),
-        in_specs=[pl.BlockSpec(memory_space=pltpu.SMEM), hbm] + [vmem] * 11,
+        in_specs=[pl.BlockSpec(memory_space=pltpu.SMEM), hbm, hbm] + [vmem] * 12 + [hbm],
         out_specs=[hbm] + [vmem] * 4,
         out_shape=[
-            jax.ShapeDtypeStruct((count * CHUNK, width), BF),
+            jax.ShapeDtypeStruct(sums.shape, BF),
             jax.ShapeDtypeStruct((tokens, width), F32),
-            jax.ShapeDtypeStruct((tokens, width), BF),
             jax.ShapeDtypeStruct((1, width), F32),
-            jax.ShapeDtypeStruct((nh, nseq, seg, groups * 256), BF),
+            jax.ShapeDtypeStruct((nh, tokens, cols), BF),
+            jax.ShapeDtypeStruct((ne, width + cols * width // (ne * col), col), F32),
         ],
         scratch_shapes=[
-            pltpu.VMEM((4, tokens, width), BF),
-            pltpu.VMEM((3, tokens, width), BF),
-            pltpu.VMEM((3, tokens, width), BF),
+            pltpu.VMEM((tokens, width), BF),
             pltpu.VMEM(heads, BF),
             pltpu.VMEM(heads, BF),
             pltpu.VMEM((tokens, width), F32),
             pltpu.VMEM((full, 128), F32),
-            DMA((4,)),
-            DMA((4,)),
-            DMA((3,)),
-            DMA((3,)),
             DMA((nh,)),
             DMA((nh,)),
+            DMA,
         ]
+        + plane_scratch(here, cap, tokens, width)
         + chain_scratch(count, width),
         compiler_params=pltpu.CompilerParams(
             collective_id=1, has_side_effects=True, vmem_limit_bytes=VMEM
         ),
         cost_estimate=pl.CostEstimate(flops=10**11, bytes_accessed=30 * 2**20, transcendentals=10**7),
         name="middle",
-    )(lengths, sums, parts, mid, grad, gain, o_parts, qkv, lse, *tables)
-
-
-def last_kernel(first, count, sum_ref, parts_ref, total_ref, got_ref, ps, pr, *chain):
-    ne = parts_ref.shape[0]
-    me = lax.axis_index("experts")
-    chain = Chain(sum_ref, total_ref, chain, first, count)
-    greet(lax.axis_size("heads"), tuple(range(1, ne)))
-
-    def part(r):
-        return remote(parts_ref.at[r], got_ref.at[r - 1], ps.at[r], pr.at[r], "experts", me ^ r)
-
+    )(lengths, sums, rows, slots, mid, grad, gain, o_parts, qkv, lse, *tables, heads_in, x)
+
+
+def last_kernel(first, count, begun_ref, sum_ref, rows_ref, slot_ref, mid_ref, dqkv_ref, w_ref, x_ref, dmid_ref, gain_ref, gtwo_ref,
+                parts_ref, total_ref, out_ref, xgrad_ref, gains_ref, got_ref, wide_ref,
+                br, moe, gp, gz, acc, stage, oz, fin, brs, brr, gps, gpr, gzs, gzr, ws, wr, wl, oss, ors, fs, fr, fl, *scratch):
+    nh, tokens, _ = dqkv_ref.shape
+    dattn = moe
+    ne = rows_ref.shape[1]
+    z, me = lax.axis_index("heads"), lax.axis_index("experts")
+    chain = Chain(sum_ref, total_ref, scratch[PLANE:], first, count)
+    plane = PlaneSum(rows_ref, slot_ref, moe, scratch[:PLANE])
+    back = Exchange(dqkv_ref, br, brs, brr, nh)
+    greet(nh, tuple(range(1, ne)))
+    back.start()
     chain.begin()
-    for r in range(ne - 1, 0, -1):
-        part(r).start()
-    chain.run(0, chain.steps())
+
+    def scatter(r, at):
+        return remote(parts_ref.at[me ^ r], got_ref.at[at], ws.at[r], wr.at[r], "experts", me ^ r)
+
+    for r in (6, 7, 2, 3, 4, 5, 1):
+        scatter(r, me).start()
+    chain.run(0, 3)
+    step = plane.run(chain, 3)
+
+    @pl.loop(0, tokens // ROWS)
+    def _(i):
+        rows = pl.ds(i * ROWS, ROWS)
+        out_ref[rows] = (mid_ref[rows] + plane.rows_total(rows)).astype(BF)
+
+    def fetch(r):
+        ref = got_ref.at[me ^ r] if r else parts_ref.at[me]
+        return pltpu.make_async_copy(ref, stage.at[r % 2], wl.at[r % 2])
+
+    for r in range(ne):
+        if r:
+            scatter(r, me ^ r).wait_recv()
+        fetch(r).start()
+        if r:
+            fetch(r - 1).wait()
+            acc[...] = stage[0] if r == 1 else acc[...] + stage[(r - 1) % 2]
+    fetch(ne - 1).wait()
+    acc[...] += stage[(ne - 1) % 2]
+    part = oz.shape[1]
+
+    def strip(d, to, at):
+        rows = pl.ds(pl.multiple_of(to * part, part), part)
+        return remote(acc.at[rows], oz.at[at], oss.at[d], ors.at[d], "heads", to)
+
+    for d in range(1, nh):
+        strip(d, lax.rem(z + d, nh), z).start()
+    oz[z] = acc[pl.ds(pl.multiple_of(z * part, part), part)]
+    chain.run(step, step + 1)
+    step = step + 1
+    back.wait_recv()
+    dattn[...] = dot_nt(br[0], w_ref[0])
+    for h in range(1, nh):
+        dattn[...] += dot_nt(br[h], w_ref[h])
+    pad = jnp.zeros((6, gtwo_ref.shape[1]), F32)
+    own = jnp.zeros_like(gtwo_ref[...])
+
+    def rows_back(i, total):
+        rows = pl.ds(i * ROWS, ROWS)
+        d = dattn[rows]
+        x = x_ref[rows].astype(F32)
+        inv = lax.rsqrt(jnp.mean(x * x, axis=-1, keepdims=True) + EPS)
+        wed = gain_ref[...] * d
+        xgrad_ref[rows] = dmid_ref[rows] + inv * wed - x * (inv * inv * inv * jnp.mean(wed * x, axis=-1, keepdims=True))
+        return total + jnp.sum(d * x * inv, axis=0, keepdims=True)
+
+    own = lax.fori_loop(0, tokens // ROWS, rows_back, own)
+    gp[me] = jnp.concatenate([own, gtwo_ref[...], pad], axis=0)
+
+    def near(r, at):
+        return remote(gp.at[me], gp.at[at], gps.at[r], gpr.at[r], "experts", me ^ r)
+
+    for r in range(1, ne):
+        near(r, me).start()
+    for d in range(1, nh):
+        src = lax.rem(z + nh - d, nh)
+        strip(d, src, src).wait_recv()
+    fin[:part] = oz[0] + oz[1] + oz[2] + oz[3]
+    fin[part:] = acc[nh * part :]
+
+    def spread(r, at):
+        return remote(fin, wide_ref.at[at], fs.at[r], fr.at[r], "experts", me ^ r)
+
+    for r in (6, 7, 2, 3, 4, 5, 1):
+        spread(r, me).start()
+    keep = pltpu.make_async_copy(fin, wide_ref.at[me], fl)
+    keep.start()
+    chain.run(step, step + 1)
+    total = None
+    for r in range(1, ne):
+        near(r, me ^ r).wait_recv()
+    for e in range(ne):
+        total = gp[e] if total is None else total + gp[e]
+    gz[z] = total
+
+    def far(d, to, at):
+        return remote(gz.at[z], gz.at[at], gzs.at[d], gzr.at[d], "heads", to)
+
+    for d in range(1, nh):
+        far(d, lax.rem(z + d, nh), z).start()
+    chain.run(step + 1, chain.steps())
+    total = None
+    for d in range(1, nh):
+        src = lax.rem(z + nh - d, nh)
+        far(d, src, src).wait_recv()
+    for h in range(nh):
+        total = gz[h] if total is None else total + gz[h]
+    gains_ref[...] = total
     chain.finish()
+    plane.finish()
+    back.finish()
+    keep.wait()
     for r in range(1, ne):
-        part(r).wait()
-
-
-def last(first, count, sums, parts):
-    ne, tokens, width = parts.shape
+        near(r, me).wait_send()
+        scatter(r, me).wait_send()
+        spread(r, me ^ r).wait_recv()
+        spread(r, me).wait_send()
+    for d in range(1, nh):
+        far(d, lax.rem(z + d, nh), z).wait_send()
+        strip(d, lax.rem(z + d, nh), z).wait_send()
+
+
+def last(first, count, total, sums, rows, slots, mid, dqkv, w_full, x, d_mid, gain, gain_two, parts):
+    nh, tokens, cols = dqkv.shape
+    here, ne, cap, width = rows.shape
+    col = parts.shape[2]
+    deep = parts.shape[1] - width + width // nh
     hbm = pl.BlockSpec(memory_space=pl.ANY)
+    vmem = pl.BlockSpec(memory_space=pltpu.VMEM)
     return pl.pallas_call(
         functools.partial(last_kernel, first, count),
-        in_specs=[hbm, hbm],
-        out_specs=[hbm, hbm],
+        in_specs=[hbm, hbm, hbm] + [vmem] * 8 + [hbm],
+        input_output_aliases={0: 0},
+        out_specs=[hbm] + [vmem] * 3 + [hbm, hbm],
         out_shape=[
-            jax.ShapeDtypeStruct((count * CHUNK, width), BF),
-            jax.ShapeDtypeStruct((ne - 1, tokens, width), BF),
+            jax.ShapeDtypeStruct(sums.shape, BF),
+            jax.ShapeDtypeStruct((tokens, width), BF),
+            jax.ShapeDtypeStruct((tokens, width), F32),
+            jax.ShapeDtypeStruct((8, width), F32),
+            jax.ShapeDtypeStruct(parts.shape, F32),
+            jax.ShapeDtypeStruct((ne, deep, col), F32),
         ],
-        scratch_shapes=[DMA((ne,)), DMA((ne,))] + chain_scratch(count, width),
+        scratch_shapes=[
+            pltpu.VMEM((nh, tokens, cols), BF),
+            pltpu.VMEM((tokens, width), F32),
+            pltpu.VMEM((ne, 8, width), F32),
+            pltpu.VMEM((nh, 8, width), F32),
+            pltpu.VMEM(parts.shape[1:], F32),
+            pltpu.VMEM((2,) + parts.shape[1:], F32),
+            pltpu.VMEM((nh, width // nh, col), F32),
+            pltpu.VMEM((deep, col), F32),
+            DMA((nh,)),
+            DMA((nh,)),
+            DMA((ne,)),
+            DMA((ne,)),
+            DMA((nh,)),
+            DMA((nh,)),
+            DMA((ne,)),
+            DMA((ne,)),
+            DMA((2,)),
+            DMA((nh,)),
+            DMA((nh,)),
+            DMA((ne,)),
+            DMA((ne,)),
+            DMA,
+        ]
+        + plane_scratch(here, cap, tokens, width)
+        + chain_scratch(count, width),
         compiler_params=pltpu.CompilerParams(
             collective_id=2, has_side_effects=True, vmem_limit_bytes=VMEM
         ),
         cost_estimate=pl.CostEstimate(flops=2 * 10**11, bytes_accessed=30 * 2**20, transcendentals=0),
         name="last",
-    )(sums, parts)
+    )(total, sums, rows, slots, mid, dqkv, w_full, x, d_mid, gain, gain_two, parts)
 
 
 def body(layer_input, seq_lengths, expert_ids, route_weight, priority, attn_gain, moe_gain,
@@ -779,11 +1054,10 @@
     w_groups = jnp.transpose(w_local, (1, 0, 2))
     rows_in = width // ne
     rows_out = output_matrix.shape[0] // ne
-    w_piece = lax.dynamic_slice_in_dim(w_local.reshape(width, groups * 256), me * rows_in, rows_in, 0)
+    w_local = w_local.reshape(width, groups * 256)
+    w_piece = lax.dynamic_slice_in_dim(w_local, me * rows_in, rows_in, 0)
     o_piece = lax.dynamic_slice_in_dim(output_matrix, me * rows_out, rows_out, 0)
     o_full = lax.all_gather(o_piece, ("heads", "experts"), axis=0, tiled=True)
-    w_full = lax.all_gather(w_piece, ("heads", "experts"), axis=0, tiled=True)
-    w_full = w_full.reshape(nh, width, groups * 256)
 
     tables = rotary_tables(nh * seg)
     qkv, heads_out, lse = attn_forward(gathered, w_groups, seq_lengths, tables)
@@ -798,31 +1072,38 @@
     grad = local(out_grad)
     grads_all = plane_gather(grad, ne)
     d_rows = gather_rows(slots, weights, grads_all, cap)
+    moe_in, d_rows = lax.optimization_barrier((moe_in, d_rows))
     tokens_all = plane_gather(moe_in, ne)
     x_rows = gather_rows(slots, None, tokens_all, cap)
+    w_piece, x_rows = lax.optimization_barrier((w_piece, x_rows))
+    w_full = lax.all_gather(w_piece, ("heads", "experts"), axis=0, tiled=True)
+    w_full = w_full.reshape(nh, width, groups * 256)
     results, drows, sums = experts_call(slots, weights, x_rows, d_rows, expert_in, expert_down)
     slots_t = jnp.swapaxes(slots, 1, 2)
-    d_parts = combine(slots_t, drows)
-    moe_parts = combine(slots_t, results)
     if nh == 4 and ne == 8:
+        w_full, drows = lax.optimization_barrier((w_full, drows))
         flat = sums.reshape(-1, width)
         chunks = flat.shape[0] // CHUNK
-        half = chunks // 2
-        total_a, d_mid, d_branch, gain_two, dqkv = middle(
-            half, seq_lengths, flat, d_parts, mid, grad, moe_gain.reshape(1, width), o_parts, qkv, lse, tables)
-        gain_two = gain_two.reshape(width)
-        back = lax.all_to_all(dqkv, "heads", split_axis=0, concat_axis=0, tiled=True)
-        flat, moe_parts, d_branch = lax.optimization_barrier((flat, moe_parts, d_branch))
-        total_b, got = last(half, chunks - half, flat, moe_parts)
-        moe_sum = moe_parts[0].astype(F32) + jnp.sum(got.astype(F32), axis=0)
-        totals = [t.reshape(here // 2, sums.shape[1], width).astype(F32) for t in (total_a, total_b)]
-        grad_in = jnp.concatenate([t[:, :width] for t in totals], axis=0)
-        grad_down = jnp.concatenate([t[:, width:] for t in totals], axis=0)
+        half = (3 * chunks) // 8
+        slots8 = jnp.pad(packed[:, 0], ((0, 0), (0, 8 - here), (0, 0)), constant_values=-1.0)
+        total, d_mid, gain_two, dqkv, parts = middle(
+            half, seq_lengths, flat, drows, slots8, mid, grad, moe_gain.reshape(1, width), o_parts, qkv, lse, tables,
+            heads_in, gathered.reshape(nh, tokens, width))
+        total, out, x_grad, gains, _, wide = last(
+            half, chunks - half, total, flat, results, slots8, mid, dqkv, w_full, local(layer_input), d_mid,
+            attn_gain.reshape(1, width), gain_two, parts)
+        o_grad, w_grad = weight_split(wide, groups * 128, groups * 256)
+        gain_one, gain_two = gains[0], gains[1]
+        totals = total.reshape(sums.shape).astype(F32)
+        grad_in, grad_down = totals[:, :width], totals[:, width:]
     else:
+        d_parts = combine(slots_t, drows)
+        moe_parts = combine(slots_t, results)
         totals = heads_sum(sums, z, nh)
         grad_in, grad_down = totals[:, :width], totals[:, width:]
         d_moe = plane_scatter(d_parts, ne)
         moe_sum = plane_scatter(moe_parts, ne)
+        out = (mid + moe_sum).astype(BF)
         zed = moe_gain * d_moe
         d_mid = grad.astype(F32) + inv_two * zed - mid * (inv_two ** 3 * jnp.mean(zed * mid, axis=-1, keepdims=True))
         gain_two = jnp.sum(d_moe * mid * inv_two, axis=0)
@@ -831,20 +1112,15 @@
         d_heads = d_heads.reshape(nh, nseq, seg, groups * 128)
         d_heads = lax.all_to_all(d_heads, "heads", split_axis=0, concat_axis=0, tiled=True)
         dqkv = attn_backward(qkv, d_heads, lse, seq_lengths, tables)
+        dqkv = dqkv.reshape(nh, tokens, groups * 256)
         back = lax.all_to_all(dqkv, "heads", split_axis=0, concat_axis=0, tiled=True)
-    out = (mid + moe_sum).astype(BF)
-
-    o_partial = jnp.einsum("ztm,tw->zmw", heads_in, d_branch, preferred_element_type=F32)
-    o_grad = lax.psum_scatter(o_partial, "heads", scatter_dimension=0)
-    o_grad = lax.psum(o_grad, "experts")
-    w_partial = jnp.einsum("zsrm,zsrc->mc", gathered, dqkv, preferred_element_type=F32)
-    w_grad = lax.psum(w_partial, "experts").reshape(width, groups, 256)
-    back = back.reshape(nh, tokens, groups * 256)
-    d_attn = jnp.einsum("ztc,zmc->tm", back, w_full, preferred_element_type=F32)
-    wed = attn_gain * d_attn
-    x_grad = d_mid + inv_one * wed - xf * (inv_one ** 3 * jnp.mean(wed * xf, axis=-1, keepdims=True))
-    gain_one = jnp.sum(d_attn * xf * inv_one, axis=0)
-    gain_one, gain_two = lax.psum((gain_one, gain_two), ("heads", "experts"))
+        d_attn = jnp.einsum("ztc,zmc->tm", back, w_full, preferred_element_type=F32)
+        o_grad, w_grad = weight_sums(heads_in, d_branch, gathered, dqkv, ne)
+        wed = attn_gain * d_attn
+        x_grad = d_mid + inv_one * wed - xf * (inv_one ** 3 * jnp.mean(wed * xf, axis=-1, keepdims=True))
+        gain_one = jnp.sum(d_attn * xf * inv_one, axis=0)
+        gain_one, gain_two = lax.psum((gain_one, gain_two), ("heads", "experts"))
+    w_grad = w_grad.reshape(width, groups, 256)
     return (
         unlocal(out),
         unlocal(x_grad),

time: 975 us -> 797 us (0.82)
  Pallas kernels: 597 us -> 531 us
  waiting for transfers between devices: 155 us -> 109 us
  blocking collectives: 37.8 us -> 0 us
  other arithmetic: 40.9 us -> 18.4 us
  matrix products: 19.8 us -> 3.87 us
  local copies, waits for them, and re-layouts: 77.4 us -> 92.5 us
    ppermute x14, waiting for transfers between devices: 15.2 us -> 66.5 us  [swap(): return lax.ppermute(x, 'experts', [(i, i ^ bit) for i in range(n)])]
    all_gather x1, waiting for transfers between devices: 49.1 us -> 2.44 us  [body(): w_full = lax.all_gather(w_piece, ('heads', 'experts'), axis=0, tiled=True)]
    psum x1 -> x0, blocking collectives: 37.8 us -> none  [body(): gain_one, gain_two = lax.psum((gain_one, gain_two), ('heads', 'experts'))]
    all_gather x1, waiting for transfers between devices: 56.2 us -> 19.1 us  [body(): lax.all_gather(attn_in.reshape(nseq, seg, width), 'heads', axis=0)]
    pallas_call x1, Pallas kernels: 197 us -> 163 us  [middle(): pl.pallas_call(functools.partial(middle_kernel, count), in_specs=[pl.Bloc...]
    pallas_call x2 -> x0, Pallas kernels: 30.8 us -> none  [combine(): pl.pallas_call(combine_kernel, grid=(sources,), in_specs=[pl.BlockSpec((1...]
    dot_general x3 -> x0, matrix products: 15.9 us -> none  [the longest x1 5.76 us: body(): d_attn = jnp.einsum('ztc,zmc->tm', back, w_full, preferred_element_type=F32)]
    concatenate x2 -> x0, other arithmetic: 15.1 us -> none  [the longest x1 8.59 us: body(): grad_down = jnp.concatenate([t[:, width:] for t in totals], axis=0)]
  transfers between devices with their start and end apart: 22 -> 19, of which waited for: 5 -> 7; matrix products, arithmetic and copies ran while one was open for 12% -> 7% of each run, Pallas kernels for 31% -> 12%
where the time goes in v3:
time: 797 us; the launch traced here: 787 us
  Pallas kernels  531 us (67%)
  waiting for transfers between devices  109 us (14%)
  local copies, waits for them, and re-layouts  92.5 us (12%)
  other arithmetic  18.4 us (2%)
  starting transfers between devices  17.7 us (2%)
  between operations  14.3 us (2%)
    pallas_call x1, Pallas kernels, last(): pl.pallas_call(functools.partial(last_kernel, first, count), in_specs=[hb...  263 us
    pallas_call x1, Pallas kernels, middle(): pl.pallas_call(functools.partial(middle_kernel, count), in_specs=[pl.Bloc...  163 us
    ppermute x14, waiting for transfers between devices, swap(): return lax.ppermute(x, 'experts', [(i, i ^ bit) for i in range(n)])  66.5 us
    pallas_call x1, Pallas kernels, experts_call(): pl.pallas_call(functools.partial(expert_kernel, steps), grid=(count, step...  60 us
    unnamed x52, local copies, waits for them, and re-layouts  39.5 us
    pallas_call x2, Pallas kernels, gather_rows(): pl.pallas_call(functools.partial(gather_kernel, weighted), grid=(sources,...  24.6 us
    all_gather x1, waiting for transfers between devices, body(): o_full = lax.all_gather(o_piece, ('heads', 'experts'), axis=0, tiled=True)  21 us
    pallas_call x1, Pallas kernels, attn_forward(): pl.pallas_call(fwd_kernel, grid=(nseq, groups), in_specs=[pl.BlockSpec(me...  20.4 us
  transfers between devices with their start and end apart: 19, of which 7 were waited for; matrix products, arithmetic and copies ran while one was open for 7% of the time, Pallas kernels for 12%

profile of v3, /device:TPU:0, one launch (start us, length us, event | category | flops | bytes accessed | tf_op | source)
XLA Modules:
  0.0 787.5 jit_solution(835320028676332982)
XLA Ops:
  8.9 2.5 fusion.2
  11.5 2.5 copy.94
  14.0 3.9 collective-permute-start.5
  22.6 4.3 all-to-all-start
  27.6 2.9 fusion.12
  33.3 2.5 bitcast_dynamic-update-slice_fusion.15
  35.8 4.7 fusion.5
  40.5 24.3 %collective-permute-done.1 = bf16[512,1024]{1,0:T(8,128)(2,1)} collective-permute-done((bf16[512,1024]{1,0:T(8,128)(2,1)}, bf16[512,1024]{1,0:T(8,128)(2,1)}, u32[]{:S(2)}, u32[]{:S(2)}) %collective-permute-start.1) | collective-permute-done | bytes 1048608 | tf_op jit(solution)/shard_map/ppermute | solution.py:386
  69.3 2.3 bitcast_dynamic-update-slice_fusion.14
  73.8 2.3 bitcast_dynamic-update-slice_fusion.12
  76.1 19.1 %all-gather.9.cloned.1.call-done = bf16[8,256,1024]{2,1,0:T(8,128)(2,1)} async-done(((bf16[2,256,1024]{2,1,0:T(8,128)(2,1)}), bf16[8,256,1024]{2,1,0:T(8,128)(2,1)}) %all-gather.9.cloned.1.call-update) | async-done | bytes 4194320 | tf_op jit(solution)/shard_map/all_gather | solution.py:1048
  95.2 20.4 %attn_forward.1 = (bf16[2,2,1024,256]{3,2,1,0:T(8,128)(2,1)}, bf16[4,2,256,256]{3,2,1,0:T(8,128)(2,1)}, f32[2,2,4,512]{3,2,1,0:T(4,128)}) custom-call(s32[2]{0:T(128)} %len_ref.3, bf16[4,2,256,1024]{3,2,1,0:T(8,128)(2,1)} %bitcast.146, bf16[2,1024,256]{2,1,0:T(8,128)(2,1)} %fusion.24.w_ref, f32[1024,128]{1,0:T(8,128)} %get-tuple-element.89.cq, ...), custom_call_target="tpu_custom_call" | custom-call | flops 6000000000 | bytes 12582912 | tf_op jit(solution)/shard_map/attn_forward/pallas_call | solution.py:94
  115.5 4.2 all-to-all-start.1
  120.3 2.3 bitcast_dynamic-update-slice_fusion.11
  122.6 2.3 bitcast_dynamic-update-slice_fusion.10
  127.1 2.3 bitcast_dynamic-update-slice_fusion.8.refs_1_
  129.4 12.6 %gather_rows.2.d_ref = bf16[4,8,160,1024]{3,2,1,0:T(8,128)(2,1)} custom-call(s32[8,4,512]{2,1,0:T(4,128)} %get-tuple-element.92.slot_ref, f32[8,4,512]{2,1,0:T(4,128)} %get-tuple-element.91.refs_0_, bf16[8,512,1024]{2,1,0:T(8,128)(2,1)} %bitcast_dynamic-update-slice_fusion.8.refs_1_), custom_call_target="tpu_custom_call" | custom-call | flops 5368709120 | bytes 18874368 | tf_op jit(solution)/shard_map/gather_rows/pallas_call | solution.py:236
  141.9 21.0 %all-gather.5.cloned.1.call-done = bf16[1024,1024]{1,0:T(8,128)(2,1)} async-done(((bf16[32,1024]{1,0:T(8,128)(2,1)}), bf16[1024,1024]{1,0:T(8,128)(2,1)}) %all-gather.5.cloned.1.call-update) | async-done | bytes 2097168 | tf_op jit(solution)/shard_map/all_gather | solution.py:1060
  162.9 3.5 multiply_reduce_fusion
  170.3 22.6 %collective-permute-done.8 = bf16[512,1024]{1,0:T(8,128)(2,1)} collective-permute-done((bf16[512,1024]{1,0:T(8,128)(2,1)S(1)}, bf16[512,1024]{1,0:T(8,128)(2,1)}, u32[]{:S(2)}, u32[]{:S(2)}) %collective-permute-start.8) | collective-permute-done | bytes 1048608 | tf_op jit(solution)/shard_map/ppermute | solution.py:386
  197.4 18.3 %collective-permute-done.12 = bf16[512,1024]{1,0:T(8,128)(2,1)} collective-permute-done((bf16[512,1024]{1,0:T(8,128)(2,1)S(1)}, bf16[512,1024]{1,0:T(8,128)(2,1)}, u32[]{:S(2)}, u32[]{:S(2)}) %collective-permute-start.12) | collective-permute-done | bytes 1048608 | tf_op jit(solution)/shard_map/ppermute | solution.py:386
  217.1 2.3 bitcast_dynamic-update-slice_fusion.6
  230.5 12.0 %gather_rows.3.x_ref = bf16[4,8,160,1024]{3,2,1,0:T(8,128)(2,1)} custom-call(s32[8,4,512]{2,1,0:T(4,128)} %get-tuple-element.92.slot_ref, bf16[8,512,1024]{2,1,0:T(8,128)(2,1)} %bitcast_dynamic-update-slice_fusion.refs_0_), custom_call_target="tpu_custom_call" | custom-call | flops 5368709120 | bytes 18874368 | tf_op jit(solution)/shard_map/gather_rows/pallas_call | solution.py:236
  244.6 60.0 %experts.1 = (bf16[4,8,160,1024]{3,2,1,0:T(8,128)(2,1)}, bf16[4,8,160,1024]{3,2,1,0:T(8,128)(2,1)}, bf16[4,1536,1024]{2,1,0:T(8,128)(2,1)}) custom-call(s32[8,4,1,512]{3,2,1,0:T(1,128)} %copy.96.slot_ref, f32[8,4,1,512]{3,2,1,0:T(1,128)} %bitcast.136, bf16[4,8,160,1024]{3,2,1,0:T(8,128)(2,1)} %gather_rows.3.x_ref, ...), custom_call_target="tpu_custom_call" | custom-call | flops 48318382080 | bytes 67108864 | tf_op jit(solution)/shard_map/experts/pallas_call | solution.py:317
  304.6 2.4 all-gather.7.cloned.1.call-done
  307.0 6.4 copy.97
  313.4 163.4 %middle.1 = (bf16[6144,1024]{1,0:T(8,128)(2,1)}, f32[512,1024]{1,0:T(8,128)}, f32[1,1024]{1,0:T(1,128)}, bf16[4,512,512]{2,1,0:T(8,128)(2,1)}, f32[8,1536,128]{2,1,0:T(8,128)}) custom-call(s32[2]{0:T(128)} %len_ref.3, bf16[6144,1024]{1,0:T(8,128)(2,1)} %bitcast.150, bf16[4,8,160,1024]{3,2,1,0:T(8,128)(2,1)} %get-tuple-element.39.rows_ref, ...), custom_call_target="tpu_custom_call" | custom-call | flops 99999997952 | bytes 31457280 | tf_op jit(solution)/shard_map/middle/pallas_call | solution.py:803
  476.9 263.1 %last.1 = (bf16[6144,1024]{1,0:T(8,128)(2,1)}, bf16[512,1024]{1,0:T(8,128)(2,1)}, f32[512,1024]{1,0:T(8,128)}, f32[8,1024]{1,0:T(8,128)}, f32[8,1536,128]{2,1,0:T(8,128)}, /*index=5*/f32[8,768,128]{2,1,0:T(8,128)}) custom-call(bf16[6144,1024]{1,0:T(8,128)(2,1)} %get-tuple-element.42.begun_ref, ...), custom_call_target="tpu_custom_call", output_to_operand_aliasing={{0}: (0, {})} | custom-call | flops 199999995904 | bytes 31457280 | tf_op jit(solution)/shard_map/last/pallas_call | solution.py:964
  740.0 2.3 slice_bitcast_fusion
  748.5 6.6 slice.53
  755.2 11.9 %slice.52 = f32[4,1024,1024]{2,1,0:T(8,128)} slice(bf16[4,1536,1024]{2,1,0:T(8,128)(2,1)} %bitcast.116), slice={[0:4], [0:1024], [0:1024]} | slice | bytes 33554432 | tf_op jit(solution)/shard_map/slice | solution.py:1098
  769.1 2.9 copy.115
  (120 shorter events, 59.2 us)
Async XLA Ops:
  7.2 19.7 %copy-start = (bf16[256,1024]{1,0:T(8,128)(2,1)S(1)}, bf16[256,1024]{1,0:T(8,128)(2,1)}, u32[]{:S(2)}) copy-start(bf16[256,1024]{1,0:T(8,128)(2,1)} %param.24) | copy-start | bytes 1572868
  7.2 23.5 %copy-start.11 = (bf16[1024,128]{1,0:T(8,128)(2,1)S(1)}, bf16[1024,128]{1,0:T(8,128)(2,1)}, u32[]{:S(2)}) copy-start(bf16[1024,128]{1,0:T(8,128)(2,1)} %param.22) | copy-start | bytes 786436
  7.2 24.0 %copy-start.12 = (bf16[1024,128]{1,0:T(8,128)(2,1)S(1)}, bf16[1024,128]{1,0:T(8,128)(2,1)}, u32[]{:S(2)}) copy-start(bf16[1024,128]{1,0:T(8,128)(2,1)} %param.23) | copy-start | bytes 786436
  7.2 88.0 %all-gather.9.cloned.1.call-start = ((), (), s32[]{:S(2)}) async-start(), calls=%async_computation.4 | async-start | bytes 5242880 | tf_op jit(solution)/shard_map/all_gather | solution.py:1048
  14.0 52.1 %copy-start.2 = (bf16[256,2,1024]{2,1,0:T(2,128)(2,1)S(1)}, bf16[256,2,1024]{2,1,0:T(2,128)(2,1)}, u32[]{:S(2)}) copy-start(bf16[256,2,1024]{2,1,0:T(2,128)(2,1)} %param.14) | copy-start | bytes 3145732
  14.0 54.7 %collective-permute-start.5 = (bf16[512,1024]{1,0:T(8,128)(2,1)}, bf16[512,1024]{1,0:T(8,128)(2,1)}, u32[]{:S(2)}, u32[]{:S(2)}) collective-permute-start(bf16[512,1024]{1,0:T(8,128)(2,1)} %bitcast.25.grad_ref), channel_id=1, source_target_pairs={{0,6},{1,7},{2,4},{3,5},{4,2},{5,3},{6,0},{7,1},{8,14},{9,15},{10,... | collective-permute-start | bytes 3145736 | tf_op jit(solution)/shard_map/ppermute | solution.py:386
  17.8 51.3 %collective-permute-start.3 = (bf16[512,1024]{1,0:T(8,128)(2,1)}, bf16[512,1024]{1,0:T(8,128)(2,1)}, u32[]{:S(2)}, u32[]{:S(2)}) collective-permute-start(bf16[512,1024]{1,0:T(8,128)(2,1)} %bitcast.25.grad_ref), channel_id=1, source_target_pairs={{0,4},{1,5},{2,6},{3,7},{4,0},{5,1},{6,2},{7,3},{8,12},{9,13},{10,... | collective-permute-start | bytes 3145736 | tf_op jit(solution)/shard_map/ppermute | solution.py:386
  18.4 46.4 %collective-permute-start.1 = (bf16[512,1024]{1,0:T(8,128)(2,1)}, bf16[512,1024]{1,0:T(8,128)(2,1)}, u32[]{:S(2)}, u32[]{:S(2)}) collective-permute-start(bf16[512,1024]{1,0:T(8,128)(2,1)} %bitcast.25.grad_ref), channel_id=1, source_target_pairs={{0,2},{1,3},{2,0},{3,1},{4,6},{5,7},{6,4},{7,5},{8,10},{9,11},{10,... | collective-permute-start | bytes 3145736 | tf_op jit(solution)/shard_map/ppermute | solution.py:386
  18.4 50.8 %collective-permute-start = (bf16[512,1024]{1,0:T(8,128)(2,1)}, bf16[512,1024]{1,0:T(8,128)(2,1)}, u32[]{:S(2)}, u32[]{:S(2)}) collective-permute-start(bf16[512,1024]{1,0:T(8,128)(2,1)} %bitcast.25.grad_ref), channel_id=1, source_target_pairs={{0,1},{1,0},{2,3},{3,2},{4,5},{5,4},{6,7},{7,6},{8,9},{9,8},{10,11... | collective-permute-start | bytes 3145736 | tf_op jit(solution)/shard_map/ppermute | solution.py:386
  22.6 44.8 %all-to-all-start = ((f32[8,2,4,512]{3,2,1,0:T(4,128)}), f32[8,2,4,512]{3,2,1,0:T(4,128)S(1)}, u32[]{:S(2)}, u32[]{:S(2)}) async-start(f32[8,2,4,512]{3,2,1,0:T(4,128)} %pad_maximum_fusion.5), calls=%async_computation | async-start | bytes 262144 | tf_op jit(solution)/shard_map/all_to_all | solution.py:1040
  26.9 136.0 %all-gather.5.cloned.1.call-start = ((), (), s32[]{:S(2)}) async-start(), calls=%async_computation.2 | async-start | bytes 2162688 | tf_op jit(solution)/shard_map/all_gather | solution.py:1060
  31.6 42.2 %copy-start.4 = (bf16[1024,2,64]{2,0,1:T(8,128)(2,1)}, bf16[1024,2,64]{2,0,1:T(8,128)(2,1)S(1)}, u32[]{:S(2)}) copy-start(bf16[1024,2,64]{2,0,1:T(8,128)(2,1)S(1)} %copy.91) | copy-start | bytes 786436
  33.3 42.7 %copy-start.6 = (bf16[1024,2,128]{2,0,1:T(8,128)(2,1)}, bf16[1024,2,128]{2,0,1:T(8,128)(2,1)S(1)}, u32[]{:S(2)}) copy-start(bf16[1024,2,128]{2,0,1:T(8,128)(2,1)S(1)} %copy.89) | copy-start | bytes 1572868
  64.8 9.0 %collective-permute-start.2 = (bf16[512,1024]{1,0:T(8,128)(2,1)}, bf16[512,1024]{1,0:T(8,128)(2,1)}, u32[]{:S(2)}, u32[]{:S(2)}) collective-permute-start(bf16[512,1024]{1,0:T(8,128)(2,1)} %collective-permute-done.1), channel_id=1, source_target_pairs={{0,1},{1,0},{2,3},{3,2},{4,5},{5,4},{6,7},{7,6},{8,9},{9,8},{10,11... | collective-permute-start | bytes 3145736 | tf_op jit(solution)/shard_map/ppermute | solution.py:386
  68.7 58.4 %collective-permute-start.6 = (bf16[512,1024]{1,0:T(8,128)(2,1)}, bf16[512,1024]{1,0:T(8,128)(2,1)}, u32[]{:S(2)}, u32[]{:S(2)}) collective-permute-start(bf16[512,1024]{1,0:T(8,128)(2,1)} %collective-permute-done.5), channel_id=1, source_target_pairs={{0,1},{1,0},{2,3},{3,2},{4,5},{5,4},{6,7},{7,6},{8,9},{9,8},{10,11... | collective-permute-start | bytes 3145736 | tf_op jit(solution)/shard_map/ppermute | solution.py:386
  69.2 53.4 %collective-permute-start.4 = (bf16[512,1024]{1,0:T(8,128)(2,1)}, bf16[512,1024]{1,0:T(8,128)(2,1)}, u32[]{:S(2)}, u32[]{:S(2)}) collective-permute-start(bf16[512,1024]{1,0:T(8,128)(2,1)} %collective-permute-done.3), channel_id=1, source_target_pairs={{0,1},{1,0},{2,3},{3,2},{4,5},{5,4},{6,7},{7,6},{8,9},{9,8},{10,11... | collective-permute-start | bytes 3145736 | tf_op jit(solution)/shard_map/ppermute | solution.py:386
  115.5 47.4 %all-to-all-start.1 = ((bf16[4,2,256,256]{3,2,1,0:T(8,128)(2,1)}), bf16[4,2,256,256]{3,2,1,0:T(8,128)(2,1)}, u32[]{:S(2)}, u32[]{:S(2)}) async-start(bf16[4,2,256,256]{3,2,1,0:T(8,128)(2,1)} %get-tuple-element.32), calls=%async_computation.1 | async-start | bytes 2097152 | tf_op jit(solution)/shard_map/all_to_all | solution.py:1064
  119.8 187.2 %all-gather.7.cloned.1.call-start = ((), (), s32[]{:S(2)}) async-start(), calls=%async_computation.3 | async-start | bytes 4325376 | tf_op jit(solution)/shard_map/all_gather | solution.py:1079
  129.4 37.1 %copy-start.13 = (f32[1024]{0:T(1024)S(1)}, f32[1024]{0:T(1024)}, u32[]{:S(2)}) copy-start(f32[1024]{0:T(1024)} %param.20) | copy-start | bytes 12292
  141.9 51.0 %copy-start.5 = (bf16[1024,2,64]{2,0,1:T(8,128)(2,1)S(1)}, bf16[1024,2,64]{2,0,1:T(8,128)(2,1)}, u32[]{:S(2)}) copy-start(bf16[1024,2,64]{2,0,1:T(8,128)(2,1)} %copy-done.4) | copy-start | bytes 786436
  141.9 51.0 %copy-start.7 = (bf16[1024,2,128]{2,0,1:T(8,128)(2,1)S(1)}, bf16[1024,2,128]{2,0,1:T(8,128)(2,1)}, u32[]{:S(2)}) copy-start(bf16[1024,2,128]{2,0,1:T(8,128)(2,1)} %copy-done.6) | copy-start | bytes 1572868
  166.7 26.2 %collective-permute-start.8 = (bf16[512,1024]{1,0:T(8,128)(2,1)S(1)}, bf16[512,1024]{1,0:T(8,128)(2,1)}, u32[]{:S(2)}, u32[]{:S(2)}) collective-permute-start(bf16[512,1024]{1,0:T(8,128)(2,1)S(1)} %multiply_convert_fusion), channel_id=1, source_target_pairs={{0,2},{1,3},{2,0},{3,1},{4,6},{5,7},{6,4},{7,5},{8,10},{9,11},{10,... | collective-permute-start | bytes 3145736 | tf_op jit(solution)/shard_map/ppermute | solution.py:386
  168.2 47.5 %collective-permute-start.12 = (bf16[512,1024]{1,0:T(8,128)(2,1)S(1)}, bf16[512,1024]{1,0:T(8,128)(2,1)}, u32[]{:S(2)}, u32[]{:S(2)}) collective-permute-start(bf16[512,1024]{1,0:T(8,128)(2,1)S(1)} %multiply_convert_fusion), channel_id=1, source_target_pairs={{0,6},{1,7},{2,4},{3,5},{4,2},{5,3},{6,0},{7,1},{8,14},{9,15},{10,... | collective-permute-start | bytes 3145736 | tf_op jit(solution)/shard_map/ppermute | solution.py:386
  169.7 47.3 %collective-permute-start.10 = (bf16[512,1024]{1,0:T(8,128)(2,1)S(1)}, bf16[512,1024]{1,0:T(8,128)(2,1)}, u32[]{:S(2)}, u32[]{:S(2)}) collective-permute-start(bf16[512,1024]{1,0:T(8,128)(2,1)S(1)} %multiply_convert_fusion), channel_id=1, source_target_pairs={{0,4},{1,5},{2,6},{3,7},{4,0},{5,1},{6,2},{7,3},{8,12},{9,13},{10,... | collective-permute-start | bytes 3145736 | tf_op jit(solution)/shard_map/ppermute | solution.py:386
  170.3 46.8 %collective-permute-start.7 = (bf16[512,1024]{1,0:T(8,128)(2,1)S(1)}, bf16[512,1024]{1,0:T(8,128)(2,1)}, u32[]{:S(2)}, u32[]{:S(2)}) collective-permute-start(bf16[512,1024]{1,0:T(8,128)(2,1)S(1)} %multiply_convert_fusion), channel_id=1, source_target_pairs={{0,1},{1,0},{2,3},{3,2},{4,5},{5,4},{6,7},{7,6},{8,9},{9,8},{10,11... | collective-permute-start | bytes 3145736 | tf_op jit(solution)/shard_map/ppermute | solution.py:386
  192.9 28.7 %collective-permute-start.9 = (bf16[512,1024]{1,0:T(8,128)(2,1)}, bf16[512,1024]{1,0:T(8,128)(2,1)}, u32[]{:S(2)}, u32[]{:S(2)}) collective-permute-start(bf16[512,1024]{1,0:T(8,128)(2,1)} %collective-permute-done.8), channel_id=1, source_target_pairs={{0,1},{1,0},{2,3},{3,2},{4,5},{5,4},{6,7},{7,6},{8,9},{9,8},{10,11... | collective-permute-start | bytes 3145736 | tf_op jit(solution)/shard_map/ppermute | solution.py:386
  215.7 13.7 %collective-permute-start.13 = (bf16[512,1024]{1,0:T(8,128)(2,1)}, bf16[512,1024]{1,0:T(8,128)(2,1)S(1)}, u32[]{:S(2)}, u32[]{:S(2)}) collective-permute-start(bf16[512,1024]{1,0:T(8,128)(2,1)} %collective-permute-done.12), channel_id=1, source_target_pairs={{0,1},{1,0},{2,3},{3,2},{4,5},{5,4},{6,7},{7,6},{8,9},{9,8},{10,11... | collective-permute-start | bytes 3145736 | tf_op jit(solution)/shard_map/ppermute | solution.py:386
  217.0 9.1 %collective-permute-start.11 = (bf16[512,1024]{1,0:T(8,128)(2,1)}, bf16[512,1024]{1,0:T(8,128)(2,1)S(1)}, u32[]{:S(2)}, u32[]{:S(2)}) collective-permute-start(bf16[512,1024]{1,0:T(8,128)(2,1)} %collective-permute-done.10), channel_id=1, source_target_pairs={{0,1},{1,0},{2,3},{3,2},{4,5},{5,4},{6,7},{7,6},{8,9},{9,8},{10,11... | collective-permute-start | bytes 3145736 | tf_op jit(solution)/shard_map/ppermute | solution.py:386
  755.2 11.9 %copy-start.10 = (bf16[512,1024]{1,0:T(8,128)(2,1)S(1)}, bf16[512,1024]{1,0:T(8,128)(2,1)}, u32[]{:S(2)}) copy-start(bf16[512,1024]{1,0:T(8,128)(2,1)} %get-tuple-element.49) | copy-start | bytes 3145732
  755.2 13.9 %copy-start.9 = (f32[512,1024]{1,0:T(8,128)S(1)}, f32[512,1024]{1,0:T(8,128)}, u32[]{:S(2)}) copy-start(f32[512,1024]{1,0:T(8,128)} %get-tuple-element.50) | copy-start | bytes 6291460
  755.2 25.5 %copy-start.1 = (bf16[256,1024]{1,0:T(8,128)(2,1)S(1)}, bf16[256,1024]{1,0:T(8,128)(2,1)}, u32[]{:S(2)}) copy-start(bf16[256,1024]{1,0:T(8,128)(2,1)} %param.24) | copy-start | bytes 1572868
  767.1 12.3 %slice-start = ((f32[1024,2,256]{0,2,1:T(8,128)}), f32[1024,2,128]{0,2,1:T(8,128)S(1)}, s32[]{:S(2)}) async-start(f32[1024,2,256]{0,2,1:T(8,128)} %copy-done.3), calls=%async_computation.5 | async-start | bytes 2097152 | tf_op jit(solution)/shard_map/slice | solution.py:1129
  (2 other events, 10.9 us)
Sparse Core Ops, SparseCore 0:
  11.6 83.5 all-gather.8
  98.0 64.8 all-gather.4
  242.6 64.3 all-gather.6

commit v4 on v3

--- a/solution.py
+++ b/solution.py
@@ -703,6 +703,329 @@
 
 
 ROWS = 128
+
+
+class PlaneGather:
+    order = (3, 1, 2)
+
+    def __init__(self, own, slot, sems):
+        self.own, self.slot = own, slot
+        self.cs, self.cr, self.ks, self.kr = sems
+        self.me = lax.axis_index("experts")
+
+    def chip(self, i, e):
+        return remote(self.own, self.slot(e), self.cs.at[i], self.cr.at[i], "experts", self.me ^ (2 * i))
+
+    def core(self, i, src, e):
+        return remote(src, self.slot(e), self.ks.at[i], self.kr.at[i], "experts", self.me ^ 1)
+
+    def start(self):
+        self.core(0, self.own, self.me).start()
+        for i in self.order:
+            self.chip(i, self.me).start()
+
+    def forward(self, i):
+        e = self.me ^ (2 * i)
+        self.chip(i, e).wait_recv()
+        self.core(i, self.slot(e), e).start()
+
+    def core_arrive(self, i):
+        e = self.me ^ 1 ^ (2 * i)
+        self.core(i, self.slot(e), e).wait_recv()
+
+    def finish(self):
+        for i in range(1, 4):
+            self.chip(i, self.me).wait_send()
+        for i in range(4):
+            self.core(i, self.own if i == 0 else self.slot(self.me ^ (2 * i)), self.me).wait_send()
+
+
+GATHER = 4
+
+
+def gather_sems():
+    return [DMA((4,)), DMA((4,)), DMA((4,)), DMA((4,))]
+
+
+class Picker:
+    def __init__(self, pack, stage, sems, here, cap):
+        self.pack, self.stage, self.sems, self.here, self.cap = pack, stage, sems, here, cap
+        self.turn, self.pending = 0, {}
+
+    def pick(self, r, tokens, out, weighted):
+        at = self.turn % 2
+        self.turn += 1
+        info = self.pack[r]
+        slots = info.astype(jnp.int32)
+        index = lax.broadcasted_iota(jnp.int32, (self.cap, slots.shape[1]), 0)
+        hits = [index == slots[j : j + 1] for j in range(self.here)]
+        rows = dot(jnp.concatenate([h.astype(F32) for h in hits], axis=0).astype(BF), tokens)
+        for c in self.pending.get(at, []):
+            c.wait()
+        for j, hit in enumerate(hits):
+            part = rows[j * self.cap : (j + 1) * self.cap]
+            if weighted:
+                w = info[self.here + j : self.here + j + 1]
+                part = part * jnp.sum(jnp.where(hit, w, 0.0), axis=1, keepdims=True)
+            self.stage[at, j] = part.astype(BF)
+        self.pending[at] = [
+            pltpu.make_async_copy(self.stage.at[at, j], out.at[j, r], self.sems.at[at, j])
+            for j in range(self.here)
+        ]
+        for c in self.pending[at]:
+            c.start()
+
+    def finish(self):
+        for copies in self.pending.values():
+            for c in copies:
+                c.wait()
+
+
+def front_kernel(len_ref, x_ref, og_ref, w_ref, om_ref, pk_ref, again_ref, mgain_ref, cq, sq, ckv, skv,
+                 xg_ref, qkv_ref, lse_ref, hin_ref, of_ref, wf_ref, mid_ref, pack_ref, drows_ref, xrows_ref,
+                 hs, ogb, mt, stage, ls, lr, ps, pr, hss, hrs, os_, or_, ws, wr, ss, *sems):
+    nh, tokens, width = xg_ref.shape
+    nseq, groups, full, _ = qkv_ref.shape
+    ne = ogb.shape[0]
+    seg = tokens // nseq
+    here, _, cap, _ = drows_ref.shape
+    z, me = lax.axis_index("heads"), lax.axis_index("experts")
+    og = PlaneGather(og_ref, lambda e: ogb.at[e], sems[:GATHER])
+    og_moe = PlaneGather(mt.at[me], lambda e: mt.at[e], sems[GATHER : 2 * GATHER])
+    og_o = PlaneGather(of_ref.at[:, me], lambda e: of_ref.at[:, e], sems[2 * GATHER : 3 * GATHER])
+    og_w = PlaneGather(wf_ref.at[:, me], lambda e: wf_ref.at[:, e], sems[3 * GATHER : 4 * GATHER])
+    heads = Exchange(hs, hin_ref, hss, hrs, nh)
+    picker = Picker(pack_ref, stage, ss, here, cap)
+
+    @pl.loop(0, tokens // ROWS)
+    def _(i):
+        rows = pl.ds(i * ROWS, ROWS)
+        x = x_ref[rows].astype(F32)
+        inv = lax.rsqrt(jnp.mean(x * x, axis=-1, keepdims=True) + EPS)
+        xg_ref[z, rows] = (x * inv * again_ref[...]).astype(BF)
+
+    greet(nh, tuple(range(1, ne)))
+
+    def hop(way, t, p, s, to):
+        ref = xg_ref.at[s, pl.ds(p * seg, seg)]
+        return remote(ref, ref, ls.at[way, t, p], lr.at[s, p], "heads", to)
+
+    right, left = jnp.minimum(z + 1, nh - 1), jnp.maximum(z - 1, 0)
+    for p in range(nseq):
+        @pl.when(z < nh - 1)
+        def _():
+            hop(0, 0, p, z, right).start()
+
+        @pl.when(z > 0)
+        def _():
+            hop(1, 0, p, z, left).start()
+
+    def info(r):
+        return remote(pk_ref.at[me ^ r], pack_ref.at[r], ps.at[r], pr.at[r], "experts", me ^ r)
+
+    for r in range(1, ne):
+        info(r).start()
+    og.start()
+    pack_ref[0] = pk_ref[me]
+
+    def project(s, p):
+        x = xg_ref[s, pl.ds(p * seg, seg)]
+        at = pl.ds(s * seg, seg)
+        for g in range(groups):
+            lin = dot(x, w_ref[:, g * 256 : (g + 1) * 256])
+            q, kv = lin[:, :128], lin[:, 128:]
+            qkv_ref[p, g, at, :128] = (q * cq[at] + swap_halves(q) * sq[at]).astype(BF)
+            qkv_ref[p, g, at, 128:] = (kv * ckv[at] + swap_halves(kv) * skv[at]).astype(BF)
+
+    @pl.loop(0, nseq)
+    def _(p):
+        project(z, p)
+
+    def round_of(t):
+        @pl.loop(0, nseq)
+        def _(p):
+            @pl.when(z >= t)
+            def _():
+                s = z - t
+                hop(0, t, p, s, left).wait_recv()
+
+                @pl.when(z < nh - 1)
+                def _():
+                    hop(0, t, p, s, right).start()
+
+                project(s, p)
+
+            @pl.when(z + t < nh)
+            def _():
+                s = z + t
+                hop(1, t, p, s, right).wait_recv()
+
+                @pl.when(z > 0)
+                def _():
+                    hop(1, t, p, s, left).start()
+
+                project(s, p)
+
+    picker.pick(0, og_ref[...], drows_ref, True)
+    round_of(1)
+    for r in range(1, ne):
+        info(r).wait_recv()
+    og.core_arrive(0)
+    picker.pick(1, ogb[me ^ 1], drows_ref, True)
+    round_of(2)
+    for i in og.order:
+        og.forward(i)
+    for i in og.order:
+        picker.pick(2 * i, ogb[me ^ (2 * i)], drows_ref, True)
+    round_of(3)
+
+    rows_o, rows_w = of_ref.shape[2], wf_ref.shape[2]
+    of_ref[z, me] = om_ref[pl.ds(pl.multiple_of(me * rows_o, rows_o), rows_o)]
+    wf_ref[z, me] = w_ref[pl.ds(pl.multiple_of(me * rows_w, rows_w), rows_w)]
+
+    def piece(ref, s, r, d, to, h):
+        return remote(ref.at[h, me], ref.at[h, me], s.at[d], r.at[d], "heads", to)
+
+    for ref, s, r in ((of_ref, os_, or_), (wf_ref, ws, wr)):
+        for d in range(1, nh):
+            piece(ref, s, r, d, lax.rem(z + d, nh), z).start()
+
+    @pl.loop(0, nseq)
+    def _(p):
+        length = len_ref[p]
+        at = pl.ds(p * seg, seg)
+        for g in range(groups):
+            q = qkv_ref[p, g, :, :128]
+            kv = qkv_ref[p, g, :, 128:]
+            k = kv[:, :HEAD]
+            vt = kv.astype(F32).T[HEAD:].astype(BF)
+            for i in range(nh):
+                n = (i + 1) * seg
+                q2 = two_heads(q[i * seg : n])
+                s = dot_nt(k[:n], q2)
+                mask = attn_mask(i * seg, n, seg, length)
+                s = jnp.where(jnp.concatenate([mask, mask], axis=1), s * SCALE, NEG)
+                m = jnp.max(s, axis=0, keepdims=True)
+                e = jnp.exp(s - m)
+                total = jnp.sum(e, axis=0, keepdims=True)
+                prob = (e * (1.0 / total)).astype(BF)
+                lse_ref[p, g, i : i + 1, :] = m + jnp.log(total)
+                hs[i, at, g * 128 : (g + 1) * 128] = untwo(dot(vt[:, :n], prob), seg).astype(BF)
+
+    heads.start()
+    for ref, s, r, gather in ((of_ref, os_, or_, og_o), (wf_ref, ws, wr, og_w)):
+        for d in range(1, nh):
+            src = lax.rem(z + nh - d, nh)
+            piece(ref, s, r, d, src, src).wait_recv()
+        gather.start()
+    for i in (0,) + og.order:
+        if i:
+            og.core_arrive(i)
+            picker.pick(2 * i + 1, ogb[me ^ 1 ^ (2 * i)], drows_ref, True)
+    for i in og.order:
+        og_o.forward(i)
+    for i in range(4):
+        og_o.core_arrive(i)
+    heads.wait_recv()
+
+    mid_ref[...] = x_ref[...].astype(F32) + dot(hin_ref[0], of_ref[0].reshape(-1, width))
+    for h in range(1, nh):
+        mid_ref[...] += dot(hin_ref[h], of_ref[h].reshape(-1, width))
+
+    @pl.loop(0, tokens // ROWS)
+    def _(i):
+        rows = pl.ds(i * ROWS, ROWS)
+        m = mid_ref[rows]
+        inv = lax.rsqrt(jnp.mean(m * m, axis=-1, keepdims=True) + EPS)
+        mt[me, rows] = (m * inv * mgain_ref[...]).astype(BF)
+
+    og_moe.start()
+    picker.pick(0, mt[me], xrows_ref, False)
+    og_moe.core_arrive(0)
+    picker.pick(1, mt[me ^ 1], xrows_ref, False)
+    for i in og.order:
+        og_w.forward(i)
+    for i in (1, 2, 3):
+        og_moe.forward(i)
+        picker.pick(2 * i, mt[me ^ (2 * i)], xrows_ref, False)
+        if i > 1:
+            og_moe.core_arrive(i - 1)
+            picker.pick(2 * i - 1, mt[me ^ 1 ^ (2 * i - 2)], xrows_ref, False)
+    og_moe.core_arrive(3)
+    picker.pick(7, mt[me ^ 7], xrows_ref, False)
+    picker.finish()
+    for i in range(4):
+        og_w.core_arrive(i)
+    for gather in (og, og_moe, og_o, og_w):
+        gather.finish()
+    heads.finish()
+    for r in range(1, ne):
+        info(r).wait_send()
+    for ref, s, r in ((of_ref, os_, or_), (wf_ref, ws, wr)):
+        for d in range(1, nh):
+            piece(ref, s, r, d, lax.rem(z + d, nh), z).wait_send()
+    for p in range(nseq):
+        for t in range(nh):
+            @pl.when((z >= t) & (z < nh - 1))
+            def _():
+                hop(0, t, p, z - t, right).wait_send()
+
+            @pl.when((z + t < nh) & (z > 0))
+            def _():
+                hop(1, t, p, z + t, left).wait_send()
+
+
+def front(lengths, x, og, w_local, o_local, packed, attn_gain, moe_gain, tables, nh, nseq, cap):
+    ne, info, _ = packed.shape
+    tokens, width = x.shape
+    here = info // 2
+    cols = w_local.shape[1]
+    groups, seg = cols // 256, tokens // nseq
+    full = nh * seg
+    part = o_local.shape[0]
+    vmem = pl.BlockSpec(memory_space=pltpu.VMEM)
+    hbm = pl.BlockSpec(memory_space=pl.ANY)
+    rows = jax.ShapeDtypeStruct((here, ne, cap, width), BF)
+    return pl.pallas_call(
+        front_kernel,
+        in_specs=[pl.BlockSpec(memory_space=pltpu.SMEM)] + [vmem] * 11,
+        out_specs=[vmem] * 8 + [hbm, hbm],
+        out_shape=[
+            jax.ShapeDtypeStruct((nh, tokens, width), BF),
+            jax.ShapeDtypeStruct((nseq, groups, full, 256), BF),
+            jax.ShapeDtypeStruct((nseq, groups, nh, 2 * seg), F32),
+            jax.ShapeDtypeStruct((nh, tokens, part), BF),
+            jax.ShapeDtypeStruct((nh, ne, part // ne, width), BF),
+            jax.ShapeDtypeStruct((nh, ne, width // ne, cols), BF),
+            jax.ShapeDtypeStruct((tokens, width), F32),
+            jax.ShapeDtypeStruct(packed.shape, F32),
+            rows,
+            rows,
+        ],
+        scratch_shapes=[
+            pltpu.VMEM((nh, tokens, part), BF),
+            pltpu.VMEM((ne, tokens, width), BF),
+            pltpu.VMEM((ne, tokens, width), BF),
+            pltpu.VMEM((2, here, cap, width), BF),
+            DMA((2, nh, nseq)),
+            DMA((nh, nseq)),
+            DMA((ne,)),
+            DMA((ne,)),
+            DMA((nh,)),
+            DMA((nh,)),
+            DMA((nh,)),
+            DMA((nh,)),
+            DMA((nh,)),
+            DMA((nh,)),
+            DMA((2, here)),
+        ]
+        + gather_sems() * 4,
+        compiler_params=pltpu.CompilerParams(
+            collective_id=3, has_side_effects=True, vmem_limit_bytes=VMEM
+        ),
+        cost_estimate=pl.CostEstimate(flops=10**11, bytes_accessed=60 * 2**20, transcendentals=10**7),
+        name="front",
+    )(lengths, x, og, w_local, o_local, packed, attn_gain, moe_gain, *tables)
 
 
 def middle_kernel(count, len_ref, sum_ref, rows_ref, slot_ref, mid_ref, grad_ref, gain_ref, o_ref, qkv_ref, lse_ref,
@@ -1036,67 +1359,63 @@
     earlier = (order[:, None] < order[None, :]).astype(BF)
     before = dot(chosen.astype(BF), earlier)
     slot = jnp.where(chosen & (before < cap), before, -1.0)
-    packed = jnp.stack([slot.reshape(ne, here, tokens), weight_e.reshape(ne, here, tokens)], axis=1)
-    packed = lax.all_to_all(packed, "experts", split_axis=0, concat_axis=0, tiled=True)
-    packed = packed[me ^ jnp.arange(ne, dtype=jnp.int32)]
-    slots = packed[:, 0].astype(jnp.int32)
-    weights = packed[:, 1]
-
-    xf = local(layer_input).astype(F32)
-    inv_one = lax.rsqrt(jnp.mean(xf * xf, axis=-1, keepdims=True) + EPS)
-    attn_in = (xf * inv_one * attn_gain).astype(BF)
-    gathered = lax.all_gather(attn_in.reshape(nseq, seg, width), "heads", axis=0)
-
+    packed = jnp.concatenate([slot.reshape(ne, here, tokens), weight_e.reshape(ne, here, tokens)], axis=1)
     wq = query_matrix.reshape(width, groups, 128)
     wk = key_matrix.reshape(width, groups, HEAD)
     wv = value_matrix.reshape(width, groups, HEAD)
-    w_local = jnp.concatenate([wq, wk, wv], axis=2)
-    w_groups = jnp.transpose(w_local, (1, 0, 2))
-    rows_in = width // ne
-    rows_out = output_matrix.shape[0] // ne
-    w_local = w_local.reshape(width, groups * 256)
-    w_piece = lax.dynamic_slice_in_dim(w_local, me * rows_in, rows_in, 0)
-    o_piece = lax.dynamic_slice_in_dim(output_matrix, me * rows_out, rows_out, 0)
-    o_full = lax.all_gather(o_piece, ("heads", "experts"), axis=0, tiled=True)
-
+    w_local = jnp.concatenate([wq, wk, wv], axis=2).reshape(width, groups * 256)
     tables = rotary_tables(nh * seg)
-    qkv, heads_out, lse = attn_forward(gathered, w_groups, seq_lengths, tables)
-    heads_in = lax.all_to_all(heads_out, "heads", split_axis=0, concat_axis=0, tiled=True)
-    heads_in = heads_in.reshape(nh, tokens, groups * 128)
-    o_parts = o_full.reshape(nh, groups * 128, width)
-    branch = jnp.einsum("ztm,zmw->tw", heads_in, o_parts, preferred_element_type=F32)
-    mid = xf + branch
-    inv_two = lax.rsqrt(jnp.mean(mid * mid, axis=-1, keepdims=True) + EPS)
-    moe_in = (mid * inv_two * moe_gain).astype(BF)
-
-    grad = local(out_grad)
-    grads_all = plane_gather(grad, ne)
-    d_rows = gather_rows(slots, weights, grads_all, cap)
-    moe_in, d_rows = lax.optimization_barrier((moe_in, d_rows))
-    tokens_all = plane_gather(moe_in, ne)
-    x_rows = gather_rows(slots, None, tokens_all, cap)
-    w_piece, x_rows = lax.optimization_barrier((w_piece, x_rows))
-    w_full = lax.all_gather(w_piece, ("heads", "experts"), axis=0, tiled=True)
-    w_full = w_full.reshape(nh, width, groups * 256)
+    x, grad = local(layer_input), local(out_grad)
+    xf = x.astype(F32)
+    gain_a, gain_m = attn_gain.reshape(1, width), moe_gain.reshape(1, width)
+    fast = nh == 4 and ne == 8
+    if fast:
+        gathered, qkv, lse, heads_in, o_full, w_full, mid, pack, d_rows, x_rows = front(
+            seq_lengths, x, grad, w_local, output_matrix, packed, gain_a, gain_m, tables, nh, nseq, cap)
+        slots, weights = pack[:, :here].astype(jnp.int32), pack[:, here:]
+        w_full = w_full.reshape(nh, width, groups * 256)
+        o_parts = o_full.reshape(nh, groups * 128, width)
+    else:
+        packed = lax.all_to_all(packed, "experts", split_axis=0, concat_axis=0, tiled=True)
+        packed = packed[me ^ jnp.arange(ne, dtype=jnp.int32)]
+        slots, weights = packed[:, :here].astype(jnp.int32), packed[:, here:]
+        inv_one = lax.rsqrt(jnp.mean(xf * xf, axis=-1, keepdims=True) + EPS)
+        attn_in = (xf * inv_one * attn_gain).astype(BF)
+        gathered = lax.all_gather(attn_in.reshape(nseq, seg, width), "heads", axis=0)
+        w_groups = jnp.transpose(w_local.reshape(width, groups, 256), (1, 0, 2))
+        rows_in, rows_out = width // ne, output_matrix.shape[0] // ne
+        w_piece = lax.dynamic_slice_in_dim(w_local, me * rows_in, rows_in, 0)
+        o_piece = lax.dynamic_slice_in_dim(output_matrix, me * rows_out, rows_out, 0)
+        o_full = lax.all_gather(o_piece, ("heads", "experts"), axis=0, tiled=True)
+        w_full = lax.all_gather(w_piece, ("heads", "experts"), axis=0, tiled=True)
+        w_full = w_full.reshape(nh, width, groups * 256)
+        qkv, heads_out, lse = attn_forward(gathered, w_groups, seq_lengths, tables)
+        heads_in = lax.all_to_all(heads_out, "heads", split_axis=0, concat_axis=0, tiled=True)
+        heads_in = heads_in.reshape(nh, tokens, groups * 128)
+        o_parts = o_full.reshape(nh, groups * 128, width)
+        branch = jnp.einsum("ztm,zmw->tw", heads_in, o_parts, preferred_element_type=F32)
+        mid = xf + branch
+        inv_two = lax.rsqrt(jnp.mean(mid * mid, axis=-1, keepdims=True) + EPS)
+        moe_in = (mid * inv_two * moe_gain).astype(BF)
+        d_rows = gather_rows(slots, weights, plane_gather(grad, ne), cap)
+        x_rows = gather_rows(slots, None, plane_gather(moe_in, ne), cap)
+
     results, drows, sums = experts_call(slots, weights, x_rows, d_rows, expert_in, expert_down)
-    slots_t = jnp.swapaxes(slots, 1, 2)
-    if nh == 4 and ne == 8:
-        w_full, drows = lax.optimization_barrier((w_full, drows))
+    if fast:
         flat = sums.reshape(-1, width)
         chunks = flat.shape[0] // CHUNK
         half = (3 * chunks) // 8
-        slots8 = jnp.pad(packed[:, 0], ((0, 0), (0, 8 - here), (0, 0)), constant_values=-1.0)
         total, d_mid, gain_two, dqkv, parts = middle(
-            half, seq_lengths, flat, drows, slots8, mid, grad, moe_gain.reshape(1, width), o_parts, qkv, lse, tables,
-            heads_in, gathered.reshape(nh, tokens, width))
+            half, seq_lengths, flat, drows, pack, mid, grad, gain_m, o_parts, qkv, lse, tables,
+            heads_in, gathered)
         total, out, x_grad, gains, _, wide = last(
-            half, chunks - half, total, flat, results, slots8, mid, dqkv, w_full, local(layer_input), d_mid,
-            attn_gain.reshape(1, width), gain_two, parts)
+            half, chunks - half, total, flat, results, pack, mid, dqkv, w_full, x, d_mid, gain_a, gain_two, parts)
         o_grad, w_grad = weight_split(wide, groups * 128, groups * 256)
         gain_one, gain_two = gains[0], gains[1]
         totals = total.reshape(sums.shape).astype(F32)
         grad_in, grad_down = totals[:, :width], totals[:, width:]
     else:
+        slots_t = jnp.swapaxes(slots, 1, 2)
         d_parts = combine(slots_t, drows)
         moe_parts = combine(slots_t, results)
         totals = heads_sum(sums, z, nh)

time: 797 us -> 750 us (0.941)
  Pallas kernels: 531 us -> 681 us
  waiting for transfers between devices: 109 us -> 0 us
  local copies, waits for them, and re-layouts: 92.5 us -> 49.3 us
  starting transfers between devices: 17.7 us -> 0 us
  between operations: 14.3 us -> 1.28 us
  other arithmetic: 18.4 us -> 10.4 us
    pallas_call x3 -> x1, Pallas kernels: 45 us -> 194 us  [front(): pl.pallas_call(front_kernel, in_specs=[pl.BlockSpec(memory_space=pltpu.SM...]
    ppermute x14 -> x0, waiting for transfers between devices: 66.5 us -> none  [swap(): return lax.ppermute(x, 'experts', [(i, i ^ bit) for i in range(n)])]
    all_gather x3 -> x0, waiting for transfers between devices: 42.5 us -> none  [the longest x1 21 us: body(): o_full = lax.all_gather(o_piece, ('heads', 'experts'), axis=0, tiled=True)]
    unnamed x52 -> x18, local copies, waits for them, and re-layouts: 39.5 us -> 12 us
    ppermute x14 -> x0, starting transfers between devices: 8.61 us -> none  [swap(): return lax.ppermute(x, 'experts', [(i, i ^ bit) for i in range(n)])]
    all_to_all x2 -> x0, starting transfers between devices: 8.54 us -> none  [the longest x1 4.31 us: body(): lax.all_to_all(packed, 'experts', split_axis=0, concat_axis=0, tiled=True)]
  transfers between devices with their start and end apart: 19 -> 0, of which waited for: 7 -> 0; matrix products, arithmetic and copies ran while one was open for 7% -> 0% of each run, Pallas kernels for 12% -> 0%
where the time goes in v4:
time: 750 us; the launch traced here: 742 us
  Pallas kernels  681 us (91%)
  local copies, waits for them, and re-layouts  49.3 us (7%)
  other arithmetic  10.4 us (1%)
    pallas_call x1, Pallas kernels, last(): pl.pallas_call(functools.partial(last_kernel, first, count), in_specs=[hb...  265 us
    pallas_call x1, Pallas kernels, front(): pl.pallas_call(front_kernel, in_specs=[pl.BlockSpec(memory_space=pltpu.SM...  194 us
    pallas_call x1, Pallas kernels, middle(): pl.pallas_call(functools.partial(middle_kernel, count), in_specs=[pl.Bloc...  162 us
    pallas_call x1, Pallas kernels, experts_call(): pl.pallas_call(functools.partial(expert_kernel, steps), grid=(count, step...  60.2 us
    slice x2, local copies, waits for them, and re-layouts, body(): grad_in, grad_down = (totals[:, :width], totals[:, width:])  18.3 us

profile of v4, /device:TPU:0, one launch (start us, length us, event | category | flops | bytes accessed | tf_op | source)
XLA Modules:
  0.0 742.0 jit_solution(13270785557392323711)
XLA Ops:
  0.7 0.8 broadcast_compare_fusion
  1.6 0.7 copy.59
  2.3 0.8 fusion.7
  3.5 0.8 select_reduce_fusion
  4.3 0.7 pad_maximum_fusion.5.pk_ref
  5.0 1.1 copy.46
  6.5 1.1 copy.47
  8.2 2.2 pad_maximum_fusion
  10.4 1.2 copy.58
  11.6 1.2 copy.44
  12.9 1.2 copy.45
  14.1 2.0 fusion.9
  16.1 2.2 fusion.2
  18.2 193.7 %front.1 = (bf16[4,512,1024]{2,1,0:T(8,128)(2,1)}, bf16[2,2,1024,256]{3,2,1,0:T(8,128)(2,1)}, f32[2,2,4,512]{3,2,1,0:T(4,128)}, bf16[4,512,256]{2,1,0:T(8,128)(2...) custom-call(s32[2]{0:T(128)} %len_ref.3, ...), custom_call_target="tpu_custom_call" | custom-call | flops 99999997952 | bytes 62914560 | tf_op jit(solution)/shard_map/front/pallas_call | solution.py:989
  212.0 1.0 fusion.15
  213.6 0.7 broadcast_in_dim.40.slot_ref
  214.3 60.2 %experts.1 = (bf16[4,8,160,1024]{3,2,1,0:T(8,128)(2,1)}, bf16[4,8,160,1024]{3,2,1,0:T(8,128)(2,1)}, bf16[4,1536,1024]{2,1,0:T(8,128)(2,1)}) custom-call(s32[8,4,1,512]{3,2,1,0:T(1,128)} %broadcast_in_dim.40.slot_ref, f32[8,4,1,512]{3,2,1,0:T(1,128)} %broadcast_in_dim.41.weight_ref, bf16[4,8,160,1024]{3,2,1,0:T(8,128)(2,1)} %get-tuple-element.34.x_ref, ...), custom_call_target="tpu_custom_call" | custom-call | flops 48318382080 | bytes 67108864 | tf_op jit(solution)/shard_map/experts/pallas_call | solution.py:317
  274.5 162.1 %middle.1 = (bf16[6144,1024]{1,0:T(8,128)(2,1)}, f32[512,1024]{1,0:T(8,128)}, f32[1,1024]{1,0:T(1,128)}, bf16[4,512,512]{2,1,0:T(8,128)(2,1)}, f32[8,1536,128]{2,1,0:T(8,128)}) custom-call(s32[2]{0:T(128)} %len_ref.3, bf16[6144,1024]{1,0:T(8,128)(2,1)} %bitcast.83, bf16[4,8,160,1024]{3,2,1,0:T(8,128)(2,1)} %get-tuple-element.37.rows_ref, ...), custom_call_target="tpu_custom_call" | custom-call | flops 99999997952 | bytes 31457280 | tf_op jit(solution)/shard_map/middle/pallas_call | solution.py:1126
  436.6 264.6 %last.1 = (bf16[6144,1024]{1,0:T(8,128)(2,1)}, bf16[512,1024]{1,0:T(8,128)(2,1)}, f32[512,1024]{1,0:T(8,128)}, f32[8,1024]{1,0:T(8,128)}, f32[8,1536,128]{2,1,0:T(8,128)}, /*index=5*/f32[8,768,128]{2,1,0:T(8,128)}) custom-call(bf16[6144,1024]{1,0:T(8,128)(2,1)} %get-tuple-element.44.begun_ref, ...), custom_call_target="tpu_custom_call", output_to_operand_aliasing={{0}: (0, {})} | custom-call | flops 199999995904 | bytes 31457280 | tf_op jit(solution)/shard_map/last/pallas_call | solution.py:1287
  701.3 3.4 copy.63
  704.7 2.9 copy.62
  707.6 1.4 fusion.16
  709.3 1.8 copy.52
  711.1 1.7 reshape_reshape.3
  712.8 1.3 copy.53
  714.1 2.5 copy.57
  716.8 1.0 fusion.14
  717.8 2.0 copy.56
  719.8 2.0 copy.55
  721.9 1.3 copy.54
  723.2 6.6 slice.48
  729.8 11.7 %slice.47 = f32[4,1024,1024]{2,1,0:T(8,128)} slice(bf16[4,1536,1024]{2,1,0:T(8,128)(2,1)} %bitcast.51), slice={[0:4], [0:1024], [0:1024]} | slice | bytes 33554432 | tf_op jit(solution)/shard_map/slice | solution.py:1416
  (27 shorter events, 2.5 us)
Async XLA Ops:
  0.6 7.4 copy-start.4
  7.6 4.0 copy-start.2
  8.2 4.7 copy-start.3
  701.2 3.4 copy-start.1
  701.3 7.8 %copy-start = (f32[8,768,128]{2,1,0:T(8,128)S(1)}, f32[8,768,128]{2,1,0:T(8,128)}, u32[]{:S(2)}) copy-start(f32[8,768,128]{2,1,0:T(8,128)} %get-tuple-element.54) | copy-start | bytes 9437188

commit v5 on v4

--- a/solution.py
+++ b/solution.py
@@ -445,8 +445,9 @@
     return o, w.reshape(width, cols)
 
 
-CHUNK = 256
+CHUNK = 128
 LAG = 3
+FLIGHT = 6
 
 
 def remote(src, dst, send, recv, axis, index):
@@ -498,49 +499,75 @@
         def _():
             self.load(0).start()
 
-    def steps(self):
-        return self.count + LAG
-
-    def step(self, k):
+        @pl.when(jnp.logical_not(self.mid))
+        def _():
+            @pl.loop(0, FLIGHT)
+            def _(k):
+                self.up(k).start()
+
+    def pair(self, k):
+        @pl.when(k + 1 < self.count)
+        def _():
+            self.load(k + 1).start()
+
+        self.load(k).wait()
+        self.up(k).wait_recv()
+        own = self.buf[lax.rem(k, 2)].astype(F32)
+        self.a[k] = (self.a[k].astype(F32) + own).astype(BF)
+        self.across(k).start()
+
+    def total(self, j):
+        self.across(j).wait_recv()
+        self.b[j] = (self.a[j].astype(F32) + self.b[j].astype(F32)).astype(BF)
+        self.down(j).start()
+        self.store(self.b, j).start()
+
+    def take(self, j):
+        self.down(j).wait_recv()
+        self.store(self.a, j).start()
+
+    def step(self, k, lag=LAG):
         n = self.count
 
         @pl.when(self.mid)
         def _():
             @pl.when(k < n)
             def _():
-                @pl.when(k + 1 < n)
-                def _():
-                    self.load(k + 1).start()
-
-                self.load(k).wait()
-                self.up(k).wait_recv()
-                own = self.buf[lax.rem(k, 2)].astype(F32)
-                self.a[k] = (self.a[k].astype(F32) + own).astype(BF)
-                self.across(k).start()
-
-            @pl.when((k >= 1) & (k <= n))
+                self.pair(k)
+
+            @pl.when((k >= lag) & (k < n + lag))
             def _():
-                j = k - 1
-                self.across(j).wait_recv()
-                self.b[j] = (self.a[j].astype(F32) + self.b[j].astype(F32)).astype(BF)
-                self.down(j).start()
-                self.store(self.b, j).start()
+                self.total(k - lag)
 
         @pl.when(jnp.logical_not(self.mid))
         def _():
-            @pl.when(k < n)
+            @pl.when(k + FLIGHT < n)
             def _():
-                @pl.when(k >= LAG)
-                def _():
-                    self.up(k - LAG).wait_send()
-
-                self.up(k).start()
-
-            @pl.when(k >= LAG)
+                self.up(k).wait_send()
+                self.up(k + FLIGHT).start()
+
+            @pl.when((k >= lag + 2) & (k < n + lag + 2))
             def _():
-                j = k - LAG
-                self.down(j).wait_recv()
-                self.store(self.a, j).start()
+                self.take(k - lag - 2)
+
+    def rest(self, k):
+        n = self.count
+
+        @pl.when(self.mid)
+        def _():
+            @pl.loop(min(max(k - LAG, 0), n), min(max(k - 1, 0), n))
+            def _(j):
+                self.total(j)
+
+        @pl.when(jnp.logical_not(self.mid))
+        def _():
+            @pl.loop(min(max(k - LAG - 2, 0), n), min(max(k - 3, 0), n))
+            def _(j):
+                self.take(j)
+
+        @pl.loop(k, n + 3)
+        def _(i):
+            self.step(i, 1)
 
     def run(self, first, last):
         @pl.loop(first, last)
@@ -560,7 +587,7 @@
 
         @pl.when(jnp.logical_not(self.mid))
         def _():
-            @pl.loop(n - LAG, n)
+            @pl.loop(n - FLIGHT, n)
             def _(k):
                 self.up(k).wait_send()
 
@@ -639,12 +666,13 @@
                     self.chip(i).start()
                 else:
                     self.total[...] = value
-            if t == 3:
-                chain.run(step, step + 1)
-        chain.run(step + 1, step + 4)
+            if t % 2:
+                chain.step(step + t // 2)
+        return step + 4
+
+    def arrive(self):
         for i in self.order:
             self.chip(i).wait_recv()
-        return step + 4
 
     def rows_total(self, rows):
         d = self.total[rows]
@@ -677,6 +705,9 @@
 PLANE = 10
 
 
+ROWS = 128
+
+
 class Exchange:
     def __init__(self, src, dst, send, recv, nh):
         self.src, self.dst, self.ss, self.rs, self.nh = src, dst, send, recv, nh
@@ -684,25 +715,24 @@
 
     def send(self, d):
         to = lax.rem(self.z + d, self.nh)
-        return remote(self.src.at[to], self.dst.at[self.z], self.ss.at[d], self.rs.at[d], "heads", to)
+        return remote(self.src(to), self.dst(self.z), self.ss(d), self.rs(d), "heads", to)
 
     def start(self):
         for d in range(1, self.nh):
             self.send(d).start()
-        own = pl.ds(self.z, 1)
-        self.dst[own] = self.src[own]
 
     def wait_recv(self):
         for d in range(1, self.nh):
             at = lax.rem(self.z + self.nh - d, self.nh)
-            remote(self.src.at[at], self.dst.at[at], self.ss.at[d], self.rs.at[d], "heads", at).wait_recv()
+            remote(self.src(at), self.dst(at), self.ss(d), self.rs(d), "heads", at).wait_recv()
 
     def finish(self):
         for d in range(1, self.nh):
             self.send(d).wait_send()
 
 
-ROWS = 128
+def whole_exchange(src, dst, send, recv, nh):
+    return Exchange(lambda h: src.at[h], lambda h: dst.at[h], lambda d: send.at[d], lambda d: recv.at[d], nh)
 
 
 class PlaneGather:
@@ -782,7 +812,7 @@
 
 
 def front_kernel(len_ref, x_ref, og_ref, w_ref, om_ref, pk_ref, again_ref, mgain_ref, cq, sq, ckv, skv,
-                 xg_ref, qkv_ref, lse_ref, hin_ref, of_ref, wf_ref, mid_ref, pack_ref, drows_ref, xrows_ref,
+                 xg_ref, qkv_ref, lse_ref, hin_ref, of_ref, wz_ref, mid_ref, pack_ref, drows_ref, xrows_ref,
                  hs, ogb, mt, stage, ls, lr, ps, pr, hss, hrs, os_, or_, ws, wr, ss, *sems):
     nh, tokens, width = xg_ref.shape
     nseq, groups, full, _ = qkv_ref.shape
@@ -791,10 +821,19 @@
     here, _, cap, _ = drows_ref.shape
     z, me = lax.axis_index("heads"), lax.axis_index("experts")
     og = PlaneGather(og_ref, lambda e: ogb.at[e], sems[:GATHER])
-    og_moe = PlaneGather(mt.at[me], lambda e: mt.at[e], sems[GATHER : 2 * GATHER])
-    og_o = PlaneGather(of_ref.at[:, me], lambda e: of_ref.at[:, e], sems[2 * GATHER : 3 * GATHER])
-    og_w = PlaneGather(wf_ref.at[:, me], lambda e: wf_ref.at[:, e], sems[3 * GATHER : 4 * GATHER])
-    heads = Exchange(hs, hin_ref, hss, hrs, nh)
+    og_o = PlaneGather(of_ref.at[:, me], lambda e: of_ref.at[:, e], sems[GATHER : 2 * GATHER])
+
+    def moe(p):
+        at = pl.ds(p * seg, seg)
+        return PlaneGather(mt.at[me, at], lambda e: mt.at[e, at], sems[(2 + p) * GATHER : (3 + p) * GATHER])
+
+    moes = [moe(p) for p in range(nseq)]
+
+    def heads(p):
+        at = pl.ds(p * seg, seg)
+        return Exchange(
+            lambda h: hs.at[h, at], lambda h: hin_ref.at[h, at], lambda d: hss.at[p, d], lambda d: hrs.at[p, d], nh)
+
     picker = Picker(pack_ref, stage, ss, here, cap)
 
     @pl.loop(0, tokens // ROWS)
@@ -823,6 +862,12 @@
     def info(r):
         return remote(pk_ref.at[me ^ r], pack_ref.at[r], ps.at[r], pr.at[r], "experts", me ^ r)
 
+    rows_o, rows_w = of_ref.shape[2], wz_ref.shape[1]
+    of_ref[z, me] = om_ref[pl.ds(pl.multiple_of(me * rows_o, rows_o), rows_o)]
+    wz_ref[z] = w_ref[pl.ds(pl.multiple_of(me * rows_w, rows_w), rows_w)]
+    ofx = Exchange(lambda h: of_ref.at[z, me], lambda h: of_ref.at[h, me], lambda d: os_.at[d], lambda d: or_.at[d], nh)
+    wzx = Exchange(lambda h: wz_ref.at[z], lambda h: wz_ref.at[h], lambda d: ws.at[d], lambda d: wr.at[d], nh)
+    ofx.start()
     for r in range(1, ne):
         info(r).start()
     og.start()
@@ -841,7 +886,7 @@
     def _(p):
         project(z, p)
 
-    def round_of(t):
+    def round_of(t, then=None):
         @pl.loop(0, nseq)
         def _(p):
             @pl.when(z >= t)
@@ -865,6 +910,9 @@
                     hop(1, t, p, s, left).start()
 
                 project(s, p)
+
+            if then is not None:
+                then(p)
 
     picker.pick(0, og_ref[...], drows_ref, True)
     round_of(1)
@@ -877,21 +925,10 @@
         og.forward(i)
     for i in og.order:
         picker.pick(2 * i, ogb[me ^ (2 * i)], drows_ref, True)
-    round_of(3)
-
-    rows_o, rows_w = of_ref.shape[2], wf_ref.shape[2]
-    of_ref[z, me] = om_ref[pl.ds(pl.multiple_of(me * rows_o, rows_o), rows_o)]
-    wf_ref[z, me] = w_ref[pl.ds(pl.multiple_of(me * rows_w, rows_w), rows_w)]
-
-    def piece(ref, s, r, d, to, h):
-        return remote(ref.at[h, me], ref.at[h, me], s.at[d], r.at[d], "heads", to)
-
-    for ref, s, r in ((of_ref, os_, or_), (wf_ref, ws, wr)):
-        for d in range(1, nh):
-            piece(ref, s, r, d, lax.rem(z + d, nh), z).start()
-
-    @pl.loop(0, nseq)
-    def _(p):
+    ofx.wait_recv()
+    og_o.start()
+
+    def attend(p):
         length = len_ref[p]
         at = pl.ds(p * seg, seg)
         for g in range(groups):
@@ -911,59 +948,62 @@
                 prob = (e * (1.0 / total)).astype(BF)
                 lse_ref[p, g, i : i + 1, :] = m + jnp.log(total)
                 hs[i, at, g * 128 : (g + 1) * 128] = untwo(dot(vt[:, :n], prob), seg).astype(BF)
-
-    heads.start()
-    for ref, s, r, gather in ((of_ref, os_, or_, og_o), (wf_ref, ws, wr, og_w)):
-        for d in range(1, nh):
-            src = lax.rem(z + nh - d, nh)
-            piece(ref, s, r, d, src, src).wait_recv()
-        gather.start()
-    for i in (0,) + og.order:
-        if i:
-            og.core_arrive(i)
-            picker.pick(2 * i + 1, ogb[me ^ 1 ^ (2 * i)], drows_ref, True)
+        heads(p).start()
+        hin_ref[z, at] = hs[z, at]
+
+    round_of(3, attend)
+    wzx.start()
     for i in og.order:
         og_o.forward(i)
+    for i in og.order:
+        og.core_arrive(i)
+        picker.pick(2 * i + 1, ogb[me ^ 1 ^ (2 * i)], drows_ref, True)
     for i in range(4):
         og_o.core_arrive(i)
-    heads.wait_recv()
-
-    mid_ref[...] = x_ref[...].astype(F32) + dot(hin_ref[0], of_ref[0].reshape(-1, width))
-    for h in range(1, nh):
-        mid_ref[...] += dot(hin_ref[h], of_ref[h].reshape(-1, width))
-
-    @pl.loop(0, tokens // ROWS)
-    def _(i):
-        rows = pl.ds(i * ROWS, ROWS)
-        m = mid_ref[rows]
-        inv = lax.rsqrt(jnp.mean(m * m, axis=-1, keepdims=True) + EPS)
-        mt[me, rows] = (m * inv * mgain_ref[...]).astype(BF)
-
-    og_moe.start()
+
+    for p in range(nseq):
+        at = pl.ds(p * seg, seg)
+        heads(p).wait_recv()
+        mid_ref[at] = x_ref[at].astype(F32) + dot(hin_ref[0, at], of_ref[0].reshape(-1, width))
+        for h in range(1, nh):
+            mid_ref[at] += dot(hin_ref[h, at], of_ref[h].reshape(-1, width))
+
+        @pl.loop(0, seg // ROWS)
+        def _(i):
+            rows = pl.ds(p * seg + i * ROWS, ROWS)
+            m = mid_ref[rows]
+            inv = lax.rsqrt(jnp.mean(m * m, axis=-1, keepdims=True) + EPS)
+            mt[me, rows] = (m * inv * mgain_ref[...]).astype(BF)
+
+        moes[p].start()
+
     picker.pick(0, mt[me], xrows_ref, False)
-    og_moe.core_arrive(0)
+    for p in range(nseq):
+        moes[p].core_arrive(0)
     picker.pick(1, mt[me ^ 1], xrows_ref, False)
     for i in og.order:
-        og_w.forward(i)
-    for i in (1, 2, 3):
-        og_moe.forward(i)
+        for p in range(nseq - 1):
+            moes[p].forward(i)
+    for t, i in enumerate(og.order):
+        moes[-1].forward(i)
         picker.pick(2 * i, mt[me ^ (2 * i)], xrows_ref, False)
-        if i > 1:
-            og_moe.core_arrive(i - 1)
-            picker.pick(2 * i - 1, mt[me ^ 1 ^ (2 * i - 2)], xrows_ref, False)
-    og_moe.core_arrive(3)
-    picker.pick(7, mt[me ^ 7], xrows_ref, False)
+        if t:
+            last = og.order[t - 1]
+            for p in range(nseq):
+                moes[p].core_arrive(last)
+            picker.pick(2 * last + 1, mt[me ^ 1 ^ (2 * last)], xrows_ref, False)
+    last = og.order[-1]
+    for p in range(nseq):
+        moes[p].core_arrive(last)
+    picker.pick(2 * last + 1, mt[me ^ 1 ^ (2 * last)], xrows_ref, False)
     picker.finish()
-    for i in range(4):
-        og_w.core_arrive(i)
-    for gather in (og, og_moe, og_o, og_w):
+    wzx.wait_recv()
+    for gather in [og, og_o] + moes:
         gather.finish()
-    heads.finish()
+    for exchange in [ofx, wzx] + [heads(p) for p in range(nseq)]:
+        exchange.finish()
     for r in range(1, ne):
         info(r).wait_send()
-    for ref, s, r in ((of_ref, os_, or_), (wf_ref, ws, wr)):
-        for d in range(1, nh):
-            piece(ref, s, r, d, lax.rem(z + d, nh), z).wait_send()
     for p in range(nseq):
         for t in range(nh):
             @pl.when((z >= t) & (z < nh - 1))
@@ -996,7 +1036,7 @@
             jax.ShapeDtypeStruct((nseq, groups, nh, 2 * seg), F32),
             jax.ShapeDtypeStruct((nh, tokens, part), BF),
             jax.ShapeDtypeStruct((nh, ne, part // ne, width), BF),
-            jax.ShapeDtypeStruct((nh, ne, width // ne, cols), BF),
+            jax.ShapeDtypeStruct((nh, width // ne, cols), BF),
             jax.ShapeDtypeStruct((tokens, width), F32),
             jax.ShapeDtypeStruct(packed.shape, F32),
             rows,
@@ -1011,15 +1051,15 @@
             DMA((nh, nseq)),
             DMA((ne,)),
             DMA((ne,)),
-            DMA((nh,)),
-            DMA((nh,)),
+            DMA((nseq, nh)),
+            DMA((nseq, nh)),
             DMA((nh,)),
             DMA((nh,)),
             DMA((nh,)),
             DMA((nh,)),
             DMA((2, here)),
         ]
-        + gather_sems() * 4,
+        + gather_sems() * (2 + nseq),
         compiler_params=pltpu.CompilerParams(
             collective_id=3, has_side_effects=True, vmem_limit_bytes=VMEM
         ),
@@ -1029,18 +1069,22 @@
 
 
 def middle_kernel(count, len_ref, sum_ref, rows_ref, slot_ref, mid_ref, grad_ref, gain_ref, o_ref, qkv_ref, lse_ref,
-                  cq, sq, ckv, skv, hin_ref, x_ref, total_ref, dmid_ref, gtwo_ref, dqkv_ref, parts_ref,
-                  dbranch_ref, hs, hr, dmoe, dkv, hss, hrs, xs, *scratch):
+                  cq, sq, ckv, skv, hin_ref, x_ref, total_ref, dmid_ref, gtwo_ref, dqkv_ref, po_ref, pw_ref,
+                  dbranch_ref, wsum, hs, hr, dmoe, dkv, hss, hrs, xs, *scratch):
     nh, tokens, _ = dqkv_ref.shape
     nseq, groups = qkv_ref.shape[:2]
     seg = tokens // nseq
+    z = lax.axis_index("heads")
     chain = Chain(sum_ref, total_ref, scratch[PLANE:], 0, count)
     plane = PlaneSum(rows_ref, slot_ref, dmoe, scratch[:PLANE])
-    heads = Exchange(hs, hr, hss, hrs, nh)
+    heads = whole_exchange(hs, hr, hss, hrs, nh)
     greet(nh, (1, 2, 4, 6))
     chain.begin()
-    chain.run(0, 1)
-    step = plane.run(chain, 1)
+    chain.run(0, 2)
+    step = plane.run(chain, 2)
+    chain.run(step, step + 4)
+    step = step + 4
+    plane.arrive()
     gtwo_ref[...] = jnp.zeros_like(gtwo_ref)
 
     @pl.loop(0, tokens // ROWS)
@@ -1059,8 +1103,9 @@
             hs[h, rows] = dot_nt(db, o_ref[h]).astype(BF)
 
     heads.start()
-    chain.run(step, step + 3)
-    step = step + 3
+    hr[z] = hs[z]
+    chain.run(step, step + 4)
+    step = step + 4
     heads.wait_recv()
 
     @pl.loop(0, nseq)
@@ -1081,32 +1126,28 @@
                 dkv,
                 put,
             )
-        chain.step(step + s)
-
-    step = step + nseq
+            chain.step(step + groups * s + g)
+
+    step = step + groups * nseq
     for i in range(4):
         plane.core(i).wait_send()
     load = pltpu.make_async_copy(x_ref, plane.odd, xs)
     load.start()
-    ne, _, col = parts_ref.shape
-    part = hin_ref.shape[2]
+    ne, deep, _ = po_ref.shape
+    strip, row = deep // nh, pw_ref.shape[1]
     db = dbranch_ref[...]
     for h in range(nh):
-        o = dot_tn(hin_ref[h], db)
+        o = dot_tn(hin_ref[h], db).astype(BF)
         for e in range(ne):
-            parts_ref[e, h * part : (h + 1) * part] = o[:, e * col : (e + 1) * col]
-    chain.run(step, step + 1)
+            po_ref[e, h * strip : (h + 1) * strip] = o[e * strip : (e + 1) * strip]
+    chain.step(step)
     load.wait()
-    wsum = dmoe
-    wsum[...] = dot_tn(dqkv_ref[0], plane.odd[0])
+    wsum[...] = dot_tn(plane.odd[0], dqkv_ref[0])
     for h in range(1, nh):
-        wsum[...] += dot_tn(dqkv_ref[h], plane.odd[h])
-    row = wsum.shape[1] // ne
+        wsum[...] += dot_tn(plane.odd[h], dqkv_ref[h])
     for e in range(ne):
-        for c in range(wsum.shape[0] // col):
-            at = nh * part + c * row
-            parts_ref[e, at : at + row] = wsum[c * col : (c + 1) * col, e * row : (e + 1) * row].T
-    chain.run(step + 1, chain.steps())
+        pw_ref[e] = wsum[e * row : (e + 1) * row].astype(BF)
+    chain.rest(step + 1)
     chain.finish()
     for i in plane.order:
         plane.chip(i).wait_send()
@@ -1121,21 +1162,22 @@
     vmem = pl.BlockSpec(memory_space=pltpu.VMEM)
     hbm = pl.BlockSpec(memory_space=pl.ANY)
     heads = (nh, tokens, groups * 128)
-    col = width // ne
     cols = groups * 256
     return pl.pallas_call(
         functools.partial(middle_kernel, count),
         in_specs=[pl.BlockSpec(memory_space=pltpu.SMEM), hbm, hbm] + [vmem] * 12 + [hbm],
-        out_specs=[hbm] + [vmem] * 4,
+        out_specs=[hbm] + [vmem] * 5,
         out_shape=[
             jax.ShapeDtypeStruct(sums.shape, BF),
             jax.ShapeDtypeStruct((tokens, width), F32),
             jax.ShapeDtypeStruct((1, width), F32),
             jax.ShapeDtypeStruct((nh, tokens, cols), BF),
-            jax.ShapeDtypeStruct((ne, width + cols * width // (ne * col), col), F32),
+            jax.ShapeDtypeStruct((ne, nh * groups * 128 // ne, width), BF),
+            jax.ShapeDtypeStruct((ne, width // ne, cols), BF),
         ],
         scratch_shapes=[
             pltpu.VMEM((tokens, width), BF),
+            pltpu.VMEM((width, cols), F32),
             pltpu.VMEM(heads, BF),
             pltpu.VMEM(heads, BF),
             pltpu.VMEM((tokens, width), F32),
@@ -1154,61 +1196,142 @@
     )(lengths, sums, rows, slots, mid, grad, gain, o_parts, qkv, lse, *tables, heads_in, x)
 
 
-def last_kernel(first, count, begun_ref, sum_ref, rows_ref, slot_ref, mid_ref, dqkv_ref, w_ref, x_ref, dmid_ref, gain_ref, gtwo_ref,
-                parts_ref, total_ref, out_ref, xgrad_ref, gains_ref, got_ref, wide_ref,
-                br, moe, gp, gz, acc, stage, oz, fin, brs, brr, gps, gpr, gzs, gzr, ws, wr, wl, oss, ors, fs, fr, fl, *scratch):
+class PairSum:
+    order = (3, 1, 2)
+
+    def __init__(self, parts, scratch):
+        self.parts = parts
+        self.c, self.e, self.f, self.cs, self.cr, self.fs, self.fr = scratch
+        self.me = lax.axis_index("experts")
+
+    def core(self, i):
+        src = self.parts.at[self.me ^ 1 ^ (2 * i)]
+        return remote(src, self.c.at[i], self.cs.at[i], self.cr.at[i], "experts", self.me ^ 1)
+
+    def chip(self, i):
+        return remote(self.e.at[i - 1], self.f.at[i - 1], self.fs.at[i - 1], self.fr.at[i - 1], "experts", self.me ^ (2 * i))
+
+    def start(self):
+        for i in self.order + (0,):
+            self.core(i).start()
+
+    def both(self, i):
+        return self.parts[self.me ^ (2 * i)].astype(F32) + self.c[i].astype(F32)
+
+    def forward(self):
+        for i in self.order:
+            self.core(i).wait_recv()
+            self.e[i - 1] = self.both(i).astype(BF)
+            self.chip(i).start()
+        self.core(0).wait_recv()
+
+    def result(self):
+        value = self.both(0)
+        for i in self.order:
+            self.chip(i).wait_recv()
+        for r in range(3):
+            value = value + self.f[r].astype(F32)
+        return value
+
+    def finish(self):
+        for i in range(4):
+            self.core(i).wait_send()
+        for i in self.order:
+            self.chip(i).wait_send()
+
+
+PAIR = 7
+
+
+def pair_scratch(shape):
+    return [pltpu.VMEM((n,) + shape, BF) for n in (4, 3, 3)] + [DMA((4,)), DMA((4,)), DMA((3,)), DMA((3,))]
+
+
+def last_kernel(first, count, begun_ref, sum_ref, rows_ref, slot_ref, mid_ref, dqkv_ref, wz_ref, x_ref, dmid_ref,
+                gain_ref, gtwo_ref, po_ref, pw_ref, total_ref, out_ref, xgrad_ref, gains_ref, ograd_ref, wgrad_ref,
+                wf, br, moe, gp, gz, acc, oz, fo, fw, brs, brr, gps, gpr, gzs, gzr, oss, ors, fl, dl, *scratch):
     nh, tokens, _ = dqkv_ref.shape
     dattn = moe
     ne = rows_ref.shape[1]
     z, me = lax.axis_index("heads"), lax.axis_index("experts")
-    chain = Chain(sum_ref, total_ref, scratch[PLANE:], first, count)
-    plane = PlaneSum(rows_ref, slot_ref, moe, scratch[:PLANE])
-    back = Exchange(dqkv_ref, br, brs, brr, nh)
+    at = PLANE
+    plane = PlaneSum(rows_ref, slot_ref, moe, scratch[:at])
+    weights = PlaneGather(wz_ref, lambda e: wf.at[:, e], scratch[at : at + GATHER])
+    at += GATHER
+    strip, row = fo.shape[0], fw.shape[0]
+
+    def o_rows(e):
+        return ograd_ref.at[pl.ds(pl.multiple_of(e * strip, strip), strip)]
+
+    def w_rows(e):
+        return wgrad_ref.at[pl.ds(pl.multiple_of(e * row, row), row)]
+
+    spread_o = PlaneGather(fo, o_rows, scratch[at : at + GATHER])
+    at += GATHER
+    spread_w = PlaneGather(fw, w_rows, scratch[at : at + GATHER])
+    at += GATHER
+    sum_o = PairSum(po_ref, scratch[at : at + PAIR])
+    at += PAIR
+    sum_w = PairSum(pw_ref, scratch[at : at + PAIR])
+    at += PAIR
+    chain = Chain(sum_ref, total_ref, scratch[at:], first, count)
+    back = whole_exchange(dqkv_ref, br, brs, brr, nh)
+    pieces = Exchange(
+        lambda h: acc.at[pl.ds(pl.multiple_of(h * strip, strip), strip)],
+        lambda h: oz.at[h], lambda d: oss.at[d], lambda d: ors.at[d], nh)
+    first_part = pltpu.make_async_copy(dmid_ref, xgrad_ref, dl)
+    first_part.start()
     greet(nh, tuple(range(1, ne)))
     back.start()
+    sum_o.start()
+    sum_w.start()
     chain.begin()
-
-    def scatter(r, at):
-        return remote(parts_ref.at[me ^ r], got_ref.at[at], ws.at[r], wr.at[r], "experts", me ^ r)
-
-    for r in (6, 7, 2, 3, 4, 5, 1):
-        scatter(r, me).start()
-    chain.run(0, 3)
-    step = plane.run(chain, 3)
+    br[z] = dqkv_ref[z]
+    chain.run(0, 2)
+    sum_o.forward()
+    sum_w.forward()
+    weights.start()
+    wf[:, me] = wz_ref[...]
+    step = plane.run(chain, 2)
+    chain.run(step, step + 2)
+    step = step + 2
+    acc[...] = sum_o.result()
+    pieces.start()
+    oz[z] = acc[pl.ds(pl.multiple_of(z * strip, strip), strip)]
+    fw[...] = sum_w.result()
+    spread_w.start()
+    chain.run(step, step + 2)
+    step = step + 2
+    pieces.wait_recv()
+    fo[...] = oz[0] + oz[1] + oz[2] + oz[3]
+    spread_o.start()
+    keep = [pltpu.make_async_copy(fo, o_rows(me), fl.at[0]), pltpu.make_async_copy(fw, w_rows(me), fl.at[1])]
+    for c in keep:
+        c.start()
+    for i in weights.order:
+        weights.forward(i)
+    chain.run(step, step + 2)
+    step = step + 2
+    plane.arrive()
 
     @pl.loop(0, tokens // ROWS)
     def _(i):
         rows = pl.ds(i * ROWS, ROWS)
         out_ref[rows] = (mid_ref[rows] + plane.rows_total(rows)).astype(BF)
 
-    def fetch(r):
-        ref = got_ref.at[me ^ r] if r else parts_ref.at[me]
-        return pltpu.make_async_copy(ref, stage.at[r % 2], wl.at[r % 2])
-
-    for r in range(ne):
-        if r:
-            scatter(r, me ^ r).wait_recv()
-        fetch(r).start()
-        if r:
-            fetch(r - 1).wait()
-            acc[...] = stage[0] if r == 1 else acc[...] + stage[(r - 1) % 2]
-    fetch(ne - 1).wait()
-    acc[...] += stage[(ne - 1) % 2]
-    part = oz.shape[1]
-
-    def strip(d, to, at):
-        rows = pl.ds(pl.multiple_of(to * part, part), part)
-        return remote(acc.at[rows], oz.at[at], oss.at[d], ors.at[d], "heads", to)
-
-    for d in range(1, nh):
-        strip(d, lax.rem(z + d, nh), z).start()
-    oz[z] = acc[pl.ds(pl.multiple_of(z * part, part), part)]
-    chain.run(step, step + 1)
-    step = step + 1
+    chain.run(step, step + 2)
+    step = step + 2
+    for i in range(4):
+        weights.core_arrive(i)
     back.wait_recv()
-    dattn[...] = dot_nt(br[0], w_ref[0])
-    for h in range(1, nh):
-        dattn[...] += dot_nt(br[h], w_ref[h])
+    for h in range(nh):
+        term = dot_nt(br[h], wf[h].reshape(-1, wf.shape[3]))
+        if h:
+            dattn[...] += term
+        else:
+            dattn[...] = term
+    chain.run(step, step + 2)
+    step = step + 2
     pad = jnp.zeros((6, gtwo_ref.shape[1]), F32)
     own = jnp.zeros_like(gtwo_ref[...])
 
@@ -1218,9 +1341,10 @@
         x = x_ref[rows].astype(F32)
         inv = lax.rsqrt(jnp.mean(x * x, axis=-1, keepdims=True) + EPS)
         wed = gain_ref[...] * d
-        xgrad_ref[rows] = dmid_ref[rows] + inv * wed - x * (inv * inv * inv * jnp.mean(wed * x, axis=-1, keepdims=True))
+        xgrad_ref[rows] += inv * wed - x * (inv * inv * inv * jnp.mean(wed * x, axis=-1, keepdims=True))
         return total + jnp.sum(d * x * inv, axis=0, keepdims=True)
 
+    first_part.wait()
     own = lax.fori_loop(0, tokens // ROWS, rows_back, own)
     gp[me] = jnp.concatenate([own, gtwo_ref[...], pad], axis=0)
 
@@ -1229,106 +1353,120 @@
 
     for r in range(1, ne):
         near(r, me).start()
-    for d in range(1, nh):
-        src = lax.rem(z + nh - d, nh)
-        strip(d, src, src).wait_recv()
-    fin[:part] = oz[0] + oz[1] + oz[2] + oz[3]
-    fin[part:] = acc[nh * part :]
-
-    def spread(r, at):
-        return remote(fin, wide_ref.at[at], fs.at[r], fr.at[r], "experts", me ^ r)
-
-    for r in (6, 7, 2, 3, 4, 5, 1):
-        spread(r, me).start()
-    keep = pltpu.make_async_copy(fin, wide_ref.at[me], fl)
-    keep.start()
-    chain.run(step, step + 1)
-    total = None
+    chain.run(step, step + 2)
+    step = step + 2
+    for spread in (spread_w, spread_o):
+        for i in spread.order:
+            spread.forward(i)
     for r in range(1, ne):
         near(r, me ^ r).wait_recv()
-    for e in range(ne):
-        total = gp[e] if total is None else total + gp[e]
+    total = gp[0]
+    for e in range(1, ne):
+        total = total + gp[e]
     gz[z] = total
-
-    def far(d, to, at):
-        return remote(gz.at[z], gz.at[at], gzs.at[d], gzr.at[d], "heads", to)
-
-    for d in range(1, nh):
-        far(d, lax.rem(z + d, nh), z).start()
-    chain.run(step + 1, chain.steps())
-    total = None
-    for d in range(1, nh):
-        src = lax.rem(z + nh - d, nh)
-        far(d, src, src).wait_recv()
-    for h in range(nh):
-        total = gz[h] if total is None else total + gz[h]
+    gains = Exchange(lambda h: gz.at[z], lambda h: gz.at[h], lambda d: gzs.at[d], lambda d: gzr.at[d], nh)
+    gains.start()
+    chain.rest(step)
+    gains.wait_recv()
+    total = gz[0]
+    for h in range(1, nh):
+        total = total + gz[h]
     gains_ref[...] = total
+    for spread in (spread_w, spread_o):
+        for i in range(4):
+            spread.core_arrive(i)
     chain.finish()
-    plane.finish()
-    back.finish()
-    keep.wait()
+    for part in (plane, back, pieces, gains, weights, spread_w, spread_o, sum_o, sum_w):
+        part.finish()
+    for c in keep:
+        c.wait()
     for r in range(1, ne):
         near(r, me).wait_send()
-        scatter(r, me).wait_send()
-        spread(r, me ^ r).wait_recv()
-        spread(r, me).wait_send()
-    for d in range(1, nh):
-        far(d, lax.rem(z + d, nh), z).wait_send()
-        strip(d, lax.rem(z + d, nh), z).wait_send()
-
-
-def last(first, count, total, sums, rows, slots, mid, dqkv, w_full, x, d_mid, gain, gain_two, parts):
+
+
+def last(first, count, total, sums, rows, slots, mid, dqkv, w_pieces, x, d_mid, gain, gain_two, po, pw):
     nh, tokens, cols = dqkv.shape
     here, ne, cap, width = rows.shape
-    col = parts.shape[2]
-    deep = parts.shape[1] - width + width // nh
+    strip = po.shape[1] // nh
+    row = pw.shape[1]
     hbm = pl.BlockSpec(memory_space=pl.ANY)
     vmem = pl.BlockSpec(memory_space=pltpu.VMEM)
     return pl.pallas_call(
         functools.partial(last_kernel, first, count),
-        in_specs=[hbm, hbm, hbm] + [vmem] * 8 + [hbm],
+        in_specs=[hbm, hbm, hbm] + [vmem] * 5 + [hbm] + [vmem] * 4,
         input_output_aliases={0: 0},
-        out_specs=[hbm] + [vmem] * 3 + [hbm, hbm],
+        out_specs=[hbm] + [vmem] * 3 + [hbm] * 2,
         out_shape=[
             jax.ShapeDtypeStruct(sums.shape, BF),
             jax.ShapeDtypeStruct((tokens, width), BF),
             jax.ShapeDtypeStruct((tokens, width), F32),
             jax.ShapeDtypeStruct((8, width), F32),
-            jax.ShapeDtypeStruct(parts.shape, F32),
-            jax.ShapeDtypeStruct((ne, deep, col), F32),
+            jax.ShapeDtypeStruct((strip * ne, width), F32),
+            jax.ShapeDtypeStruct((row * ne, cols), F32),
         ],
         scratch_shapes=[
+            pltpu.VMEM((nh, ne, width // ne, cols), BF),
             pltpu.VMEM((nh, tokens, cols), BF),
             pltpu.VMEM((tokens, width), F32),
             pltpu.VMEM((ne, 8, width), F32),
             pltpu.VMEM((nh, 8, width), F32),
-            pltpu.VMEM(parts.shape[1:], F32),
-            pltpu.VMEM((2,) + parts.shape[1:], F32),
-            pltpu.VMEM((nh, width // nh, col), F32),
-            pltpu.VMEM((deep, col), F32),
+            pltpu.VMEM((nh * strip, width), F32),
+            pltpu.VMEM((nh, strip, width), F32),
+            pltpu.VMEM((strip, width), F32),
+            pltpu.VMEM((row, cols), F32),
             DMA((nh,)),
             DMA((nh,)),
             DMA((ne,)),
             DMA((ne,)),
             DMA((nh,)),
             DMA((nh,)),
-            DMA((ne,)),
-            DMA((ne,)),
-            DMA((2,)),
             DMA((nh,)),
             DMA((nh,)),
-            DMA((ne,)),
-            DMA((ne,)),
+            DMA((2,)),
             DMA,
         ]
         + plane_scratch(here, cap, tokens, width)
+        + gather_sems() * 3
+        + pair_scratch(po.shape[1:])
+        + pair_scratch(pw.shape[1:])
         + chain_scratch(count, width),
         compiler_params=pltpu.CompilerParams(
             collective_id=2, has_side_effects=True, vmem_limit_bytes=VMEM
         ),
         cost_estimate=pl.CostEstimate(flops=2 * 10**11, bytes_accessed=30 * 2**20, transcendentals=0),
         name="last",
-    )(total, sums, rows, slots, mid, dqkv, w_full, x, d_mid, gain, gain_two, parts)
+    )(total, sums, rows, slots, mid, dqkv, w_pieces, x, d_mid, gain, gain_two, po, pw)
+
+
+def widen_kernel(x_ref, in_ref, down_ref):
+    c = pl.program_id(1)
+
+    @pl.when(c < 2)
+    def _():
+        in_ref[...] = x_ref[...].astype(F32)
+
+    @pl.when(c == 2)
+    def _():
+        down_ref[...] = x_ref[...].astype(F32)
+
+
+def widen(sums, ff):
+    here, rows, width = sums.shape
+    return pl.pallas_call(
+        widen_kernel,
+        grid=(here, 3),
+        in_specs=[pl.BlockSpec((1, ff, width), lambda j, c: (j, c, 0))],
+        out_specs=[
+            pl.BlockSpec((1, ff, width), lambda j, c: (j, jnp.minimum(c, 1), 0)),
+            pl.BlockSpec((1, ff, width), lambda j, c: (j, 0, 0)),
+        ],
+        out_shape=[
+            jax.ShapeDtypeStruct((here, 2 * ff, width), F32),
+            jax.ShapeDtypeStruct((here, ff, width), F32),
+        ],
+        compiler_params=params(2),
+        name="widen",
+    )(sums)
 
 
 def body(layer_input, seq_lengths, expert_ids, route_weight, priority, attn_gain, moe_gain,
@@ -1370,10 +1508,9 @@
     gain_a, gain_m = attn_gain.reshape(1, width), moe_gain.reshape(1, width)
     fast = nh == 4 and ne == 8
     if fast:
-        gathered, qkv, lse, heads_in, o_full, w_full, mid, pack, d_rows, x_rows = front(
+        gathered, qkv, lse, heads_in, o_full, w_pieces, mid, pack, d_rows, x_rows = front(
             seq_lengths, x, grad, w_local, output_matrix, packed, gain_a, gain_m, tables, nh, nseq, cap)
         slots, weights = pack[:, :here].astype(jnp.int32), pack[:, here:]
-        w_full = w_full.reshape(nh, width, groups * 256)
         o_parts = o_full.reshape(nh, groups * 128, width)
     else:
         packed = lax.all_to_all(packed, "experts", split_axis=0, concat_axis=0, tiled=True)
@@ -1404,16 +1541,14 @@
     if fast:
         flat = sums.reshape(-1, width)
         chunks = flat.shape[0] // CHUNK
-        half = (3 * chunks) // 8
-        total, d_mid, gain_two, dqkv, parts = middle(
+        half = (5 * chunks) // 12
+        total, d_mid, gain_two, dqkv, po, pw = middle(
             half, seq_lengths, flat, drows, pack, mid, grad, gain_m, o_parts, qkv, lse, tables,
             heads_in, gathered)
-        total, out, x_grad, gains, _, wide = last(
-            half, chunks - half, total, flat, results, pack, mid, dqkv, w_full, x, d_mid, gain_a, gain_two, parts)
-        o_grad, w_grad = weight_split(wide, groups * 128, groups * 256)
+        total, out, x_grad, gains, o_grad, w_grad = last(
+            half, chunks - half, total, flat, results, pack, mid, dqkv, w_pieces, x, d_mid, gain_a, gain_two, po, pw)
         gain_one, gain_two = gains[0], gains[1]
-        totals = total.reshape(sums.shape).astype(F32)
-        grad_in, grad_down = totals[:, :width], totals[:, width:]
+        grad_in, grad_down = widen(total.reshape(sums.shape), expert_down.shape[1])
     else:
         slots_t = jnp.swapaxes(slots, 1, 2)
         d_parts = combine(slots_t, drows)
@@ -1440,14 +1575,17 @@
         gain_one = jnp.sum(d_attn * xf * inv_one, axis=0)
         gain_one, gain_two = lax.psum((gain_one, gain_two), ("heads", "experts"))
     w_grad = w_grad.reshape(width, groups, 256)
+    q_grad = w_grad[:, :, :128].reshape(query_matrix.shape)
+    k_grad = w_grad[:, :, 128:192].reshape(key_matrix.shape)
+    v_grad = w_grad[:, :, 192:].reshape(value_matrix.shape)
     return (
         unlocal(out),
         unlocal(x_grad),
         gain_one,
         gain_two,
-        w_grad[:, :, :128].reshape(query_matrix.shape),
-        w_grad[:, :, 128:192].reshape(key_matrix.shape),
-        w_grad[:, :, 192:].reshape(value_matrix.shape),
+        q_grad,
+        k_grad,
+        v_grad,
         o_grad,
         grad_in,
         grad_down,

time: 750 us -> 725 us (0.967)
  local copies, waits for them, and re-layouts: 49.3 us -> 28.5 us
    pallas_call x1, Pallas kernels: 194 us -> 163 us  [front(): pl.pallas_call(front_kernel, in_specs=[pl.BlockSpec(memory_space=pltpu.SM...]
    pallas_call x1, Pallas kernels: 162 us -> 179 us  [middle(): pl.pallas_call(functools.partial(middle_kernel, count), in_specs=[pl.Bloc...]
    pallas_call x0 -> x1, Pallas kernels: none -> 17.1 us  [widen(): pl.pallas_call(widen_kernel, grid=(here, 3), in_specs=[pl.BlockSpec((1, f...]
    slice x5 -> x2, local copies, waits for them, and re-layouts: 19.6 us -> 2.75 us  [the longest x1 2.39 us: body(): v_grad = w_grad[:, :, 192:].reshape(value_matrix.shape)]
    pallas_call x1, Pallas kernels: 265 us -> 257 us  [last(): pl.pallas_call(functools.partial(last_kernel, first, count), in_specs=[hb...]
where the time goes in v5:
time: 725 us; the launch traced here: 716 us
  Pallas kernels  676 us (93%)
  local copies, waits for them, and re-layouts  28.5 us (4%)
  other arithmetic  10.4 us (1%)
    pallas_call x1, Pallas kernels, last(): pl.pallas_call(functools.partial(last_kernel, first, count), in_specs=[hb...  257 us
    pallas_call x1, Pallas kernels, middle(): pl.pallas_call(functools.partial(middle_kernel, count), in_specs=[pl.Bloc...  179 us
    pallas_call x1, Pallas kernels, front(): pl.pallas_call(front_kernel, in_specs=[pl.BlockSpec(memory_space=pltpu.SM...  163 us
    pallas_call x1, Pallas kernels, experts_call(): pl.pallas_call(functools.partial(expert_kernel, steps), grid=(count, step...  60.2 us
    pallas_call x1, Pallas kernels, widen(): pl.pallas_call(widen_kernel, grid=(here, 3), in_specs=[pl.BlockSpec((1, f...  17.1 us

profile of v5, /device:TPU:0, one launch (start us, length us, event | category | flops | bytes accessed | tf_op | source)
XLA Modules:
  0.0 716.4 jit_solution(6369815273346488801)
XLA Ops:
  0.7 0.8 broadcast_compare_fusion
  1.7 0.7 copy.57
  2.4 0.8 fusion.7
  3.5 0.8 select_reduce_fusion
  4.4 0.7 pad_maximum_fusion.5.pk_ref
  5.0 1.1 copy.44
  6.1 0.4 copy.46
  7.3 2.2 pad_maximum_fusion
  9.5 1.2 copy.56
  10.7 1.2 copy.42
  11.9 1.2 copy.43
  13.2 2.0 fusion.9
  15.2 2.2 fusion.2
  17.3 162.5 %front.1 = (bf16[4,512,1024]{2,1,0:T(8,128)(2,1)}, bf16[2,2,1024,256]{3,2,1,0:T(8,128)(2,1)}, f32[2,2,4,512]{3,2,1,0:T(4,128)}, bf16[4,512,256]{2,1,0:T(8,128)(2...) custom-call(s32[2]{0:T(128)} %len_ref.3, ...), custom_call_target="tpu_custom_call" | custom-call | flops 99999997952 | bytes 62914560 | tf_op jit(solution)/shard_map/front/pallas_call | solution.py:1029
  179.8 1.0 fusion.15
  180.9 0.7 broadcast_in_dim.41.weight_ref
  181.5 0.7 broadcast_in_dim.40.slot_ref
  182.2 60.2 %experts.1 = (bf16[4,8,160,1024]{3,2,1,0:T(8,128)(2,1)}, bf16[4,8,160,1024]{3,2,1,0:T(8,128)(2,1)}, bf16[4,1536,1024]{2,1,0:T(8,128)(2,1)}) custom-call(s32[8,4,1,512]{3,2,1,0:T(1,128)} %broadcast_in_dim.40.slot_ref, f32[8,4,1,512]{3,2,1,0:T(1,128)} %broadcast_in_dim.41.weight_ref, bf16[4,8,160,1024]{3,2,1,0:T(8,128)(2,1)} %get-tuple-element.38.x_ref, ...), custom_call_target="tpu_custom_call" | custom-call | flops 48318382080 | bytes 67108864 | tf_op jit(solution)/shard_map/experts/pallas_call | solution.py:317
  242.4 179.2 %middle.1 = (bf16[6144,1024]{1,0:T(8,128)(2,1)}, f32[512,1024]{1,0:T(8,128)}, f32[1,1024]{1,0:T(1,128)}, bf16[4,512,512]{2,1,0:T(8,128)(2,1)}, bf16[8,128,1024]{...) custom-call(s32[2]{0:T(128)} %len_ref.3, bf16[6144,1024]{1,0:T(8,128)(2,1)} %bitcast.72, ...), custom_call_target="tpu_custom_call" | custom-call | flops 99999997952 | bytes 31457280 | tf_op jit(solution)/shard_map/middle/pallas_call | solution.py:1166
  421.6 256.9 %last.1 = (bf16[6144,1024]{1,0:T(8,128)(2,1)}, bf16[512,1024]{1,0:T(8,128)(2,1)}, f32[512,1024]{1,0:T(8,128)}, f32[8,1024]{1,0:T(8,128)}, f32[256,1024]{1,0:T(8,128)}, /*index=5*/f32[1024,512]{1,0:T(8,128)}) custom-call(bf16[6144,1024]{1,0:T(8,128)(2,1)} %get-tuple-element.48.begun_ref, ...), custom_call_target="tpu_custom_call", output_to_operand_aliasing={{0}: (0, {})} | custom-call | flops 199999995904 | bytes 31457280 | tf_op jit(solution)/shard_map/last/pallas_call | solution.py:1394
  678.5 3.4 copy.64
  681.9 2.9 copy.62
  684.8 1.4 fusion.16
  686.3 2.6 reshape.127
  689.2 1.0 copy.63
  690.3 2.4 fusion.14
  692.6 1.4 copy.55
  694.1 1.0 copy.53
  695.1 0.5 copy.54
  695.6 1.0 copy.52
  696.6 17.1 %widen.1 = (f32[4,1024,1024]{2,1,0:T(8,128)}, f32[4,512,1024]{2,1,0:T(8,128)}) custom-call(bf16[4,1536,1024]{2,1,0:T(8,128)(2,1)} %bitcast.42), custom_call_target="tpu_custom_call" | custom-call | tf_op jit(solution)/shard_map/widen/pallas_call | solution.py:1455
  713.6 2.3 copy.67
  (24 shorter events, 1.6 us)
Async XLA Ops:
  0.6 5.9 copy-start.4
  0.7 6.5 copy-start.3
  7.2 3.5 copy-start.1
  9.5 2.5 copy-start.2
  678.5 3.4 copy-start

commit v6 on v5

--- a/solution.py
+++ b/solution.py
@@ -447,7 +447,7 @@
 
 CHUNK = 128
 LAG = 3
-FLIGHT = 6
+FLIGHT = 3
 
 
 def remote(src, dst, send, recv, axis, index):
@@ -470,6 +470,7 @@
 class Chain:
     def __init__(self, src, out, scratch, first, count):
         self.src, self.out, self.first, self.count = src, out, first, count
+        self.flight = min(FLIGHT, count)
         self.a, self.b, self.buf, self.s1, self.r1, self.s2, self.r2, self.ls, self.os = scratch
         z = lax.axis_index("heads")
         self.mid = (z == 1) | (z == 2)
@@ -501,7 +502,7 @@
 
         @pl.when(jnp.logical_not(self.mid))
         def _():
-            @pl.loop(0, FLIGHT)
+            @pl.loop(0, self.flight)
             def _(k):
                 self.up(k).start()
 
@@ -541,10 +542,10 @@
 
         @pl.when(jnp.logical_not(self.mid))
         def _():
-            @pl.when(k + FLIGHT < n)
+            @pl.when(k + self.flight < n)
             def _():
                 self.up(k).wait_send()
-                self.up(k + FLIGHT).start()
+                self.up(k + self.flight).start()
 
             @pl.when((k >= lag + 2) & (k < n + lag + 2))
             def _():
@@ -587,7 +588,7 @@
 
         @pl.when(jnp.logical_not(self.mid))
         def _():
-            @pl.loop(n - FLIGHT, n)
+            @pl.loop(n - self.flight, n)
             def _(k):
                 self.up(k).wait_send()
 
@@ -608,6 +609,107 @@
         DMA((2,)),
         DMA((count,)),
     ]
+
+
+def experts_send_kernel(count, pack_ref, x_ref, d_ref, win_ref, wdown_ref,
+                        out_ref, drow_ref, grad_ref, total_ref, hid_ref, dgu_ref, early_ref, *scratch):
+    j, last_j = pl.program_id(0), pl.num_programs(0) - 1
+    nh = lax.axis_size("heads")
+    _, sources, cap, width = x_ref.shape
+    here = pack_ref.shape[1] // 2
+    ff = wdown_ref.shape[1]
+    chain = Chain(early_ref, total_ref, scratch, 0, count)
+    per = 2
+    parts = sources // per
+
+    def chain_step(t):
+        @pl.when(j > 0)
+        def _():
+            chain.step((j - 1) * 3 + t, 1)
+
+    @pl.when(j == 0)
+    def _():
+        greet(nh, ())
+
+    win, wdown = win_ref[0], wdown_ref[0]
+    for c in range(parts):
+        rows = slice(c * per * cap, (c + 1) * per * cap)
+        x = x_ref[0, c * per : (c + 1) * per].reshape(per * cap, width)
+        d = d_ref[0, c * per : (c + 1) * per].reshape(per * cap, width)
+        gu = dot(x, win)
+        gate, up = gu[:, :ff], gu[:, ff:]
+        sig = 1.0 / (1.0 + jnp.exp(-gate))
+        act = gate * sig
+        hidden = (act * up).astype(BF)
+        hid_ref[rows, :] = hidden
+        result = dot(hidden, wdown).astype(BF).astype(F32)
+        for b in range(per):
+            s = c * per + b
+            hit = pick_rows(pack_ref[s, pl.ds(j, 1)].astype(jnp.int32), cap)[0]
+            w = jnp.sum(jnp.where(hit, pack_ref[s, pl.ds(here + j, 1)], 0.0), axis=1, keepdims=True)
+            out_ref[0, s] = (result[b * cap : (b + 1) * cap] * w).astype(BF)
+        dh = dot_nt(d, wdown)
+        dgu_ref[rows, :ff] = (dh * up * (sig * (1.0 + gate * (1.0 - sig)))).astype(BF)
+        dgu_ref[rows, ff:] = (dh * act).astype(BF)
+        drow = dot_nt(dgu_ref[rows, :], win).astype(BF)
+        for b in range(per):
+            drow_ref[0, c * per + b] = drow[b * cap : (b + 1) * cap]
+        if c % 2:
+            chain_step(c // 2)
+    gin = dot_tn(x_ref[0].reshape(sources * cap, width), dgu_ref[...]).astype(BF)
+    grad_ref[0, :width] = gin
+    grad_ref[0, width:] = dot_tn(hid_ref[...], d_ref[0].reshape(sources * cap, width)).astype(BF)
+    chain_step(2)
+
+    @pl.when(j == 0)
+    def _():
+        early_ref[...] = gin[: early_ref.shape[0]]
+        chain.begin()
+
+    @pl.when(j == last_j)
+    def _():
+        chain.finish()
+
+
+def experts_send(count, pack, x, d, win, wdown):
+    here, sources, cap, width = x.shape
+    ff = wdown.shape[1]
+    rows = pl.BlockSpec((1, sources, cap, width), lambda j: (j, 0, 0, 0))
+    shape = jax.ShapeDtypeStruct((here, sources, cap, width), BF)
+    hbm = pl.BlockSpec(memory_space=pl.ANY)
+    return pl.pallas_call(
+        functools.partial(experts_send_kernel, count),
+        grid=(here,),
+        in_specs=[
+            pl.BlockSpec(memory_space=pltpu.VMEM),
+            rows,
+            rows,
+            pl.BlockSpec((1, width, 2 * ff), lambda j: (j, 0, 0)),
+            pl.BlockSpec((1, ff, width), lambda j: (j, 0, 0)),
+        ],
+        out_specs=[rows, rows, pl.BlockSpec((1, width + ff, width), lambda j: (j, 0, 0)), hbm],
+        out_shape=[
+            shape,
+            shape,
+            jax.ShapeDtypeStruct((here, width + ff, width), BF),
+            jax.ShapeDtypeStruct((here * (width + ff), width), BF),
+        ],
+        scratch_shapes=[
+            pltpu.VMEM((sources * cap, ff), BF),
+            pltpu.VMEM((sources * cap, 2 * ff), BF),
+            pltpu.VMEM((count * CHUNK, width), BF),
+        ]
+        + chain_scratch(count, width),
+        compiler_params=pltpu.CompilerParams(
+            dimension_semantics=("arbitrary",), collective_id=4, has_side_effects=True, vmem_limit_bytes=VMEM
+        ),
+        cost_estimate=pl.CostEstimate(
+            flops=18 * here * sources * cap * width * ff,
+            bytes_accessed=8 * here * sources * cap * width,
+            transcendentals=here * sources * cap * ff,
+        ),
+        name="experts_send",
+    )(pack, x, d, win, wdown)
 
 
 class PlaneSum:
@@ -718,8 +820,8 @@
         return remote(self.src(to), self.dst(self.z), self.ss(d), self.rs(d), "heads", to)
 
     def start(self):
-        for d in range(1, self.nh):
-            self.send(d).start()
+        for k in range(1, self.nh):
+            self.send(jnp.where(self.z < self.nh // 2, self.nh - k, k)).start()
 
     def wait_recv(self):
         for d in range(1, self.nh):
@@ -811,9 +913,9 @@
                 c.wait()
 
 
-def front_kernel(len_ref, x_ref, og_ref, w_ref, om_ref, pk_ref, again_ref, mgain_ref, cq, sq, ckv, skv,
+def front_kernel(len_ref, x_ref, og_ref, wq_ref, wk_ref, wv_ref, om_ref, pk_ref, again_ref, mgain_ref, cq, sq, ckv, skv,
                  xg_ref, qkv_ref, lse_ref, hin_ref, of_ref, wz_ref, mid_ref, pack_ref, drows_ref, xrows_ref,
-                 hs, ogb, mt, stage, ls, lr, ps, pr, hss, hrs, os_, or_, ws, wr, ss, *sems):
+                 w_ref, hs, ogb, mt, stage, ls, lr, ps, pr, hss, hrs, os_, or_, ws, wr, ss, *sems):
     nh, tokens, width = xg_ref.shape
     nseq, groups, full, _ = qkv_ref.shape
     ne = ogb.shape[0]
@@ -844,6 +946,10 @@
         xg_ref[z, rows] = (x * inv * again_ref[...]).astype(BF)
 
     greet(nh, tuple(range(1, ne)))
+    for g in range(groups):
+        head = slice(g * HEAD, (g + 1) * HEAD)
+        w_ref[:, g * 256 : g * 256 + 128] = wq_ref[:, g * 128 : (g + 1) * 128]
+        w_ref[:, g * 256 + 128 : (g + 1) * 256] = jnp.concatenate([wk_ref[:, head], wv_ref[:, head]], axis=1)
 
     def hop(way, t, p, s, to):
         ref = xg_ref.at[s, pl.ds(p * seg, seg)]
@@ -948,11 +1054,29 @@
                 prob = (e * (1.0 / total)).astype(BF)
                 lse_ref[p, g, i : i + 1, :] = m + jnp.log(total)
                 hs[i, at, g * 128 : (g + 1) * 128] = untwo(dot(vt[:, :n], prob), seg).astype(BF)
-        heads(p).start()
         hin_ref[z, at] = hs[z, at]
 
+        @pl.when(at_end)
+        def _():
+            heads(p).start()
+
+    at_end = (z == 0) | (z == nh - 1)
     round_of(3, attend)
-    wzx.start()
+    for p in range(nseq):
+        for t in range(nh):
+            @pl.when((z >= t) & (z < nh - 1))
+            def _():
+                hop(0, t, p, z - t, right).wait_send()
+
+            @pl.when((z + t < nh) & (z > 0))
+            def _():
+                hop(1, t, p, z + t, left).wait_send()
+
+    @pl.when(jnp.logical_not(at_end))
+    def _():
+        for p in range(nseq):
+            heads(p).start()
+
     for i in og.order:
         og_o.forward(i)
     for i in og.order:
@@ -977,6 +1101,7 @@
 
         moes[p].start()
 
+    wzx.start()
     picker.pick(0, mt[me], xrows_ref, False)
     for p in range(nseq):
         moes[p].core_arrive(0)
@@ -1004,22 +1129,13 @@
         exchange.finish()
     for r in range(1, ne):
         info(r).wait_send()
-    for p in range(nseq):
-        for t in range(nh):
-            @pl.when((z >= t) & (z < nh - 1))
-            def _():
-                hop(0, t, p, z - t, right).wait_send()
-
-            @pl.when((z + t < nh) & (z > 0))
-            def _():
-                hop(1, t, p, z + t, left).wait_send()
-
-
-def front(lengths, x, og, w_local, o_local, packed, attn_gain, moe_gain, tables, nh, nseq, cap):
+
+
+def front(lengths, x, og, wq, wk, wv, o_local, packed, attn_gain, moe_gain, tables, nh, nseq, cap):
     ne, info, _ = packed.shape
     tokens, width = x.shape
     here = info // 2
-    cols = w_local.shape[1]
+    cols = 2 * wq.shape[1]
     groups, seg = cols // 256, tokens // nseq
     full = nh * seg
     part = o_local.shape[0]
@@ -1028,7 +1144,7 @@
     rows = jax.ShapeDtypeStruct((here, ne, cap, width), BF)
     return pl.pallas_call(
         front_kernel,
-        in_specs=[pl.BlockSpec(memory_space=pltpu.SMEM)] + [vmem] * 11,
+        in_specs=[pl.BlockSpec(memory_space=pltpu.SMEM)] + [vmem] * 13,
         out_specs=[vmem] * 8 + [hbm, hbm],
         out_shape=[
             jax.ShapeDtypeStruct((nh, tokens, width), BF),
@@ -1043,6 +1159,7 @@
             rows,
         ],
         scratch_shapes=[
+            pltpu.VMEM((width, cols), BF),
             pltpu.VMEM((nh, tokens, part), BF),
             pltpu.VMEM((ne, tokens, width), BF),
             pltpu.VMEM((ne, tokens, width), BF),
@@ -1065,17 +1182,17 @@
         ),
         cost_estimate=pl.CostEstimate(flops=10**11, bytes_accessed=60 * 2**20, transcendentals=10**7),
         name="front",
-    )(lengths, x, og, w_local, o_local, packed, attn_gain, moe_gain, *tables)
-
-
-def middle_kernel(count, len_ref, sum_ref, rows_ref, slot_ref, mid_ref, grad_ref, gain_ref, o_ref, qkv_ref, lse_ref,
+    )(lengths, x, og, wq, wk, wv, o_local, packed, attn_gain, moe_gain, *tables)
+
+
+def middle_kernel(first, count, len_ref, begun_ref, sum_ref, rows_ref, slot_ref, mid_ref, grad_ref, gain_ref, o_ref, qkv_ref, lse_ref,
                   cq, sq, ckv, skv, hin_ref, x_ref, total_ref, dmid_ref, gtwo_ref, dqkv_ref, po_ref, pw_ref,
                   dbranch_ref, wsum, hs, hr, dmoe, dkv, hss, hrs, xs, *scratch):
     nh, tokens, _ = dqkv_ref.shape
     nseq, groups = qkv_ref.shape[:2]
     seg = tokens // nseq
     z = lax.axis_index("heads")
-    chain = Chain(sum_ref, total_ref, scratch[PLANE:], 0, count)
+    chain = Chain(sum_ref, total_ref, scratch[PLANE:], first, count)
     plane = PlaneSum(rows_ref, slot_ref, dmoe, scratch[:PLANE])
     heads = whole_exchange(hs, hr, hss, hrs, nh)
     greet(nh, (1, 2, 4, 6))
@@ -1154,7 +1271,7 @@
     heads.finish()
 
 
-def middle(count, lengths, sums, rows, slots, mid, grad, gain, o_parts, qkv, lse, tables, heads_in, x):
+def middle(first, count, lengths, total, sums, rows, slots, mid, grad, gain, o_parts, qkv, lse, tables, heads_in, x):
     nseq, groups, full, _ = qkv.shape
     nh = o_parts.shape[0]
     tokens, width = mid.shape
@@ -1164,8 +1281,9 @@
     heads = (nh, tokens, groups * 128)
     cols = groups * 256
     return pl.pallas_call(
-        functools.partial(middle_kernel, count),
-        in_specs=[pl.BlockSpec(memory_space=pltpu.SMEM), hbm, hbm] + [vmem] * 12 + [hbm],
+        functools.partial(middle_kernel, first, count),
+        in_specs=[pl.BlockSpec(memory_space=pltpu.SMEM), hbm, hbm, hbm] + [vmem] * 12 + [hbm],
+        input_output_aliases={1: 0},
         out_specs=[hbm] + [vmem] * 5,
         out_shape=[
             jax.ShapeDtypeStruct(sums.shape, BF),
@@ -1193,7 +1311,7 @@
         ),
         cost_estimate=pl.CostEstimate(flops=10**11, bytes_accessed=30 * 2**20, transcendentals=10**7),
         name="middle",
-    )(lengths, sums, rows, slots, mid, grad, gain, o_parts, qkv, lse, *tables, heads_in, x)
+    )(lengths, total, sums, rows, slots, mid, grad, gain, o_parts, qkv, lse, *tables, heads_in, x)
 
 
 class PairSum:
@@ -1248,8 +1366,8 @@
 
 
 def last_kernel(first, count, begun_ref, sum_ref, rows_ref, slot_ref, mid_ref, dqkv_ref, wz_ref, x_ref, dmid_ref,
-                gain_ref, gtwo_ref, po_ref, pw_ref, total_ref, out_ref, xgrad_ref, gains_ref, ograd_ref, wgrad_ref,
-                wf, br, moe, gp, gz, acc, oz, fo, fw, brs, brr, gps, gpr, gzs, gzr, oss, ors, fl, dl, *scratch):
+                gain_ref, gtwo_ref, po_ref, pw_ref, total_ref, out_ref, xgrad_ref, gains_ref, ograd_ref, qgrad_ref, kgrad_ref, vgrad_ref,
+                wf, br, moe, gp, gz, acc, oz, fo, fq, fk, fv, brs, brr, gps, gpr, gzs, gzr, oss, ors, fl, dl, *scratch):
     nh, tokens, _ = dqkv_ref.shape
     dattn = moe
     ne = rows_ref.shape[1]
@@ -1258,18 +1376,20 @@
     plane = PlaneSum(rows_ref, slot_ref, moe, scratch[:at])
     weights = PlaneGather(wz_ref, lambda e: wf.at[:, e], scratch[at : at + GATHER])
     at += GATHER
-    strip, row = fo.shape[0], fw.shape[0]
+    strip, row = fo.shape[0], fq.shape[0]
 
     def o_rows(e):
         return ograd_ref.at[pl.ds(pl.multiple_of(e * strip, strip), strip)]
 
-    def w_rows(e):
-        return wgrad_ref.at[pl.ds(pl.multiple_of(e * row, row), row)]
+    def w_rows(ref, e):
+        return ref.at[pl.ds(pl.multiple_of(e * row, row), row)]
 
     spread_o = PlaneGather(fo, o_rows, scratch[at : at + GATHER])
     at += GATHER
-    spread_w = PlaneGather(fw, w_rows, scratch[at : at + GATHER])
-    at += GATHER
+    spreads = [spread_o]
+    for mine, whole in ((fq, qgrad_ref), (fk, kgrad_ref), (fv, vgrad_ref)):
+        spreads.append(PlaneGather(mine, functools.partial(w_rows, whole), scratch[at : at + GATHER]))
+        at += GATHER
     sum_o = PairSum(po_ref, scratch[at : at + PAIR])
     at += PAIR
     sum_w = PairSum(pw_ref, scratch[at : at + PAIR])
@@ -1298,14 +1418,20 @@
     acc[...] = sum_o.result()
     pieces.start()
     oz[z] = acc[pl.ds(pl.multiple_of(z * strip, strip), strip)]
-    fw[...] = sum_w.result()
-    spread_w.start()
+    w = sum_w.result()
+    for g in range(fq.shape[1] // 128):
+        head = slice(g * HEAD, (g + 1) * HEAD)
+        fq[:, g * 128 : (g + 1) * 128] = w[:, g * 256 : g * 256 + 128]
+        fk[:, head] = w[:, g * 256 + 128 : g * 256 + 192]
+        fv[:, head] = w[:, g * 256 + 192 : (g + 1) * 256]
+    for spread in spreads[1:]:
+        spread.start()
     chain.run(step, step + 2)
     step = step + 2
     pieces.wait_recv()
     fo[...] = oz[0] + oz[1] + oz[2] + oz[3]
     spread_o.start()
-    keep = [pltpu.make_async_copy(fo, o_rows(me), fl.at[0]), pltpu.make_async_copy(fw, w_rows(me), fl.at[1])]
+    keep = [pltpu.make_async_copy(g.own, g.slot(me), fl.at[t]) for t, g in enumerate(spreads)]
     for c in keep:
         c.start()
     for i in weights.order:
@@ -1355,7 +1481,7 @@
         near(r, me).start()
     chain.run(step, step + 2)
     step = step + 2
-    for spread in (spread_w, spread_o):
+    for spread in spreads[1:] + spreads[:1]:
         for i in spread.order:
             spread.forward(i)
     for r in range(1, ne):
@@ -1372,11 +1498,11 @@
     for h in range(1, nh):
         total = total + gz[h]
     gains_ref[...] = total
-    for spread in (spread_w, spread_o):
+    for spread in spreads:
         for i in range(4):
             spread.core_arrive(i)
     chain.finish()
-    for part in (plane, back, pieces, gains, weights, spread_w, spread_o, sum_o, sum_w):
+    for part in [plane, back, pieces, gains, weights, sum_o, sum_w] + spreads:
         part.finish()
     for c in keep:
         c.wait()
@@ -1395,14 +1521,16 @@
         functools.partial(last_kernel, first, count),
         in_specs=[hbm, hbm, hbm] + [vmem] * 5 + [hbm] + [vmem] * 4,
         input_output_aliases={0: 0},
-        out_specs=[hbm] + [vmem] * 3 + [hbm] * 2,
+        out_specs=[hbm] + [vmem] * 3 + [hbm] * 4,
         out_shape=[
             jax.ShapeDtypeStruct(sums.shape, BF),
             jax.ShapeDtypeStruct((tokens, width), BF),
             jax.ShapeDtypeStruct((tokens, width), F32),
             jax.ShapeDtypeStruct((8, width), F32),
             jax.ShapeDtypeStruct((strip * ne, width), F32),
-            jax.ShapeDtypeStruct((row * ne, cols), F32),
+            jax.ShapeDtypeStruct((row * ne, cols // 2), F32),
+            jax.ShapeDtypeStruct((row * ne, cols // 4), F32),
+            jax.ShapeDtypeStruct((row * ne, cols // 4), F32),
         ],
         scratch_shapes=[
             pltpu.VMEM((nh, ne, width // ne, cols), BF),
@@ -1413,7 +1541,9 @@
             pltpu.VMEM((nh * strip, width), F32),
             pltpu.VMEM((nh, strip, width), F32),
             pltpu.VMEM((strip, width), F32),
-            pltpu.VMEM((row, cols), F32),
+            pltpu.VMEM((row, cols // 2), F32),
+            pltpu.VMEM((row, cols // 4), F32),
+            pltpu.VMEM((row, cols // 4), F32),
             DMA((nh,)),
             DMA((nh,)),
             DMA((ne,)),
@@ -1422,11 +1552,11 @@
             DMA((nh,)),
             DMA((nh,)),
             DMA((nh,)),
-            DMA((2,)),
+            DMA((4,)),
             DMA,
         ]
         + plane_scratch(here, cap, tokens, width)
-        + gather_sems() * 3
+        + gather_sems() * 5
         + pair_scratch(po.shape[1:])
         + pair_scratch(pw.shape[1:])
         + chain_scratch(count, width),
@@ -1498,10 +1628,6 @@
     before = dot(chosen.astype(BF), earlier)
     slot = jnp.where(chosen & (before < cap), before, -1.0)
     packed = jnp.concatenate([slot.reshape(ne, here, tokens), weight_e.reshape(ne, here, tokens)], axis=1)
-    wq = query_matrix.reshape(width, groups, 128)
-    wk = key_matrix.reshape(width, groups, HEAD)
-    wv = value_matrix.reshape(width, groups, HEAD)
-    w_local = jnp.concatenate([wq, wk, wv], axis=2).reshape(width, groups * 256)
     tables = rotary_tables(nh * seg)
     x, grad = local(layer_input), local(out_grad)
     xf = x.astype(F32)
@@ -1509,10 +1635,13 @@
     fast = nh == 4 and ne == 8
     if fast:
         gathered, qkv, lse, heads_in, o_full, w_pieces, mid, pack, d_rows, x_rows = front(
-            seq_lengths, x, grad, w_local, output_matrix, packed, gain_a, gain_m, tables, nh, nseq, cap)
-        slots, weights = pack[:, :here].astype(jnp.int32), pack[:, here:]
+            seq_lengths, x, grad, query_matrix, key_matrix, value_matrix, output_matrix, packed, gain_a, gain_m, tables, nh, nseq, cap)
         o_parts = o_full.reshape(nh, groups * 128, width)
     else:
+        wq = query_matrix.reshape(width, groups, 128)
+        wk = key_matrix.reshape(width, groups, HEAD)
+        wv = value_matrix.reshape(width, groups, HEAD)
+        w_local = jnp.concatenate([wq, wk, wv], axis=2).reshape(width, groups * 256)
         packed = lax.all_to_all(packed, "experts", split_axis=0, concat_axis=0, tiled=True)
         packed = packed[me ^ jnp.arange(ne, dtype=jnp.int32)]
         slots, weights = packed[:, :here].astype(jnp.int32), packed[:, here:]
@@ -1537,19 +1666,20 @@
         d_rows = gather_rows(slots, weights, plane_gather(grad, ne), cap)
         x_rows = gather_rows(slots, None, plane_gather(moe_in, ne), cap)
 
-    results, drows, sums = experts_call(slots, weights, x_rows, d_rows, expert_in, expert_down)
     if fast:
+        chunks = expert_in.shape[0] * (width + expert_down.shape[1]) // CHUNK
+        early, half = chunks // 12, (5 * chunks) // 12
+        results, drows, sums, total = experts_send(early, pack, x_rows, d_rows, expert_in, expert_down)
         flat = sums.reshape(-1, width)
-        chunks = flat.shape[0] // CHUNK
-        half = (5 * chunks) // 12
         total, d_mid, gain_two, dqkv, po, pw = middle(
-            half, seq_lengths, flat, drows, pack, mid, grad, gain_m, o_parts, qkv, lse, tables,
+            early, half, seq_lengths, total, flat, drows, pack, mid, grad, gain_m, o_parts, qkv, lse, tables,
             heads_in, gathered)
-        total, out, x_grad, gains, o_grad, w_grad = last(
-            half, chunks - half, total, flat, results, pack, mid, dqkv, w_pieces, x, d_mid, gain_a, gain_two, po, pw)
+        total, out, x_grad, gains, o_grad, q_grad, k_grad, v_grad = last(
+            early + half, chunks - early - half, total, flat, results, pack, mid, dqkv, w_pieces, x, d_mid, gain_a, gain_two, po, pw)
         gain_one, gain_two = gains[0], gains[1]
         grad_in, grad_down = widen(total.reshape(sums.shape), expert_down.shape[1])
     else:
+        results, drows, sums = experts_call(slots, weights, x_rows, d_rows, expert_in, expert_down)
         slots_t = jnp.swapaxes(slots, 1, 2)
         d_parts = combine(slots_t, drows)
         moe_parts = combine(slots_t, results)
@@ -1574,10 +1704,10 @@
         x_grad = d_mid + inv_one * wed - xf * (inv_one ** 3 * jnp.mean(wed * xf, axis=-1, keepdims=True))
         gain_one = jnp.sum(d_attn * xf * inv_one, axis=0)
         gain_one, gain_two = lax.psum((gain_one, gain_two), ("heads", "experts"))
-    w_grad = w_grad.reshape(width, groups, 256)
-    q_grad = w_grad[:, :, :128].reshape(query_matrix.shape)
-    k_grad = w_grad[:, :, 128:192].reshape(key_matrix.shape)
-    v_grad = w_grad[:, :, 192:].reshape(value_matrix.shape)
+        w_grad = w_grad.reshape(width, groups, 256)
+        q_grad = w_grad[:, :, :128].reshape(query_matrix.shape)
+        k_grad = w_grad[:, :, 128:192].reshape(key_matrix.shape)
+        v_grad = w_grad[:, :, 192:].reshape(value_matrix.shape)
     return (
         unlocal(out),
         unlocal(x_grad),

time: 725 us -> 694 us (0.957)
  Pallas kernels: 676 us -> 654 us
    pallas_call x1, Pallas kernels: 257 us -> 234 us  [last(): pl.pallas_call(functools.partial(last_kernel, first, count), in_specs=[hb...]
    pallas_call x2, Pallas kernels: 239 us -> 248 us  [the longest x1 178 us: middle(): pl.pallas_call(functools.partial(middle_kernel, first, count), in_specs=[...]
where the time goes in v6:
time: 694 us; the launch traced here: 685 us
  Pallas kernels  654 us (94%)
  local copies, waits for them, and re-layouts  22.3 us (3%)
  other arithmetic  7.14 us (1%)
    pallas_call x1, Pallas kernels, last(): pl.pallas_call(functools.partial(last_kernel, first, count), in_specs=[hb...  234 us
    pallas_call x1, Pallas kernels, middle(): pl.pallas_call(functools.partial(middle_kernel, first, count), in_specs=[...  178 us
    pallas_call x1, Pallas kernels, front(): pl.pallas_call(front_kernel, in_specs=[pl.BlockSpec(memory_space=pltpu.SM...  155 us
    pallas_call x1, Pallas kernels, experts_send(): pl.pallas_call(functools.partial(experts_send_kernel, count), grid=(here,...  69.3 us
    pallas_call x1, Pallas kernels, widen(): pl.pallas_call(widen_kernel, grid=(here, 3), in_specs=[pl.BlockSpec((1, f...  17.1 us

profile of v6, /device:TPU:0, one launch (start us, length us, event | category | flops | bytes accessed | tf_op | source)
XLA Modules:
  0.0 685.2 jit_solution(6830729945457295327)
XLA Ops:
  0.7 0.7 broadcast_compare_fusion
  1.4 0.1 pad.2.clone
  1.5 0.1 pad.5.clone
  1.6 0.7 copy.39
  2.3 0.8 fusion.7
  3.1 0.4 and_select_fusion
  3.4 0.8 select_reduce_fusion
  4.3 0.7 pad_maximum_fusion.4.pk_ref
  5.0 2.5 copy.35
  7.4 2.5 copy.36
  9.9 2.0 fusion.9
  11.8 2.2 fusion.2
  14.0 155.5 %front.1 = (bf16[4,512,1024]{2,1,0:T(8,128)(2,1)}, bf16[2,2,1024,256]{3,2,1,0:T(8,128)(2,1)}, f32[2,2,4,512]{3,2,1,0:T(4,128)}, bf16[4,512,256]{2,1,0:T(8,128)(2...) custom-call(s32[2]{0:T(128)} %len_ref.3, ...), custom_call_target="tpu_custom_call" | custom-call | flops 99999997952 | bytes 62914560 | tf_op jit(solution)/shard_map/front/pallas_call | solution.py:1145
  169.5 69.3 %experts_send.1 = (bf16[4,8,160,1024]{3,2,1,0:T(8,128)(2,1)}, bf16[4,8,160,1024]{3,2,1,0:T(8,128)(2,1)}, bf16[4,1536,1024]{2,1,0:T(8,128)(2,1)}, bf16[6144,1024]{1,0:T(8,128)(2,1)}) custom-call(f32[8,8,512]{2,1,0:T(8,128)} %get-tuple-element.40.pack_ref.slot_ref, bf16[4,8,160,1024]{3,2,1,0:T(8,128)(2,1)} %get-tuple-element.41.x_ref, ...), custom_call_target="tpu_custom_call" | custom-call | flops 48318382080 | bytes 41943040 | tf_op jit(solution)/shard_map/experts_send/pallas_call | solution.py:680
  238.7 178.3 %middle.1 = (bf16[6144,1024]{1,0:T(8,128)(2,1)}, f32[512,1024]{1,0:T(8,128)}, f32[1,1024]{1,0:T(1,128)}, bf16[4,512,512]{2,1,0:T(8,128)(2,1)}, bf16[8,128,1024]{...) custom-call(s32[2]{0:T(128)} %len_ref.3, ...), custom_call_target="tpu_custom_call", output_to_operand_aliasing={{0}: (1, {})} | custom-call | flops 99999997952 | bytes 31457280 | tf_op jit(solution)/shard_map/middle/pallas_call | solution.py:1283
  417.0 234.4 %last.1 = (bf16[6144,1024]{1,0:T(8,128)(2,1)}, bf16[512,1024]{1,0:T(8,128)(2,1)}, f32[512,1024]{1,0:T(8,128)}, f32[8,1024]{1,0:T(8,128)}, f32[256,1024]{1,0:T(8,...) custom-call(bf16[6144,1024]{1,0:T(8,128)(2,1)} %get-tuple-element.52., ...), custom_call_target="tpu_custom_call", output_to_operand_aliasing={{0}: (0, {})} | custom-call | flops 199999995904 | bytes 31457280 | tf_op jit(solution)/shard_map/last/pallas_call | solution.py:1520
  651.4 3.3 copy.43
  654.7 4.5 copy.42
  659.2 0.0 copy-start
  659.2 1.4 fusion.14
  660.7 17.1 %widen.1 = (f32[4,1024,1024]{2,1,0:T(8,128)}, f32[4,512,1024]{2,1,0:T(8,128)}) custom-call(bf16[4,1536,1024]{2,1,0:T(8,128)(2,1)} %bitcast.32), custom_call_target="tpu_custom_call" | custom-call | tf_op jit(solution)/shard_map/widen/pallas_call | solution.py:1585
  677.8 2.3 copy.50
  680.0 1.9 copy.51
  681.9 0.0 copy-done
  681.9 0.8 copy.52
  682.7 2.3 copy.53
  (7 shorter events, 0.1 us)
Async XLA Ops:
  659.2 22.7 %copy-start = (f32[1024,128]{1,0:T(8,128)S(1)}, f32[1024,128]{1,0:T(8,128)}, u32[]{:S(2)}) copy-start(f32[1024,128]{1,0:T(8,128)} %get-tuple-element.97) | copy-start | bytes 1572868

commit v7 on v6

--- a/solution.py
+++ b/solution.py
@@ -446,7 +446,7 @@
 
 
 CHUNK = 128
-LAG = 3
+LAG = 2
 FLIGHT = 3
 
 
@@ -749,7 +749,7 @@
         rows = self.buf[at].reshape(self.here * self.cap, self.width)
         return dot(hot.astype(F32).astype(BF), rows)
 
-    def run(self, chain, step):
+    def run(self, chain=None, step=0):
         turns = [2 * i + 1 for i in self.order + (0,)] + [2 * i for i in self.order + (0,)]
         for c in self.load(turns[0], 0):
             c.start()
@@ -768,9 +768,8 @@
                     self.chip(i).start()
                 else:
                     self.total[...] = value
-            if t % 2:
+            if chain is not None and t % 2:
                 chain.step(step + t // 2)
-        return step + 4
 
     def arrive(self):
         for i in self.order:
@@ -1197,10 +1196,9 @@
     heads = whole_exchange(hs, hr, hss, hrs, nh)
     greet(nh, (1, 2, 4, 6))
     chain.begin()
-    chain.run(0, 2)
-    step = plane.run(chain, 2)
-    chain.run(step, step + 4)
-    step = step + 4
+    plane.run(chain, 0)
+    step = 4 + 5
+    chain.run(4, step)
     plane.arrive()
     gtwo_ref[...] = jnp.zeros_like(gtwo_ref)
 
@@ -1407,14 +1405,11 @@
     sum_w.start()
     chain.begin()
     br[z] = dqkv_ref[z]
-    chain.run(0, 2)
     sum_o.forward()
     sum_w.forward()
     weights.start()
     wf[:, me] = wz_ref[...]
-    step = plane.run(chain, 2)
-    chain.run(step, step + 2)
-    step = step + 2
+    plane.run()
     acc[...] = sum_o.result()
     pieces.start()
     oz[z] = acc[pl.ds(pl.multiple_of(z * strip, strip), strip)]
@@ -1426,8 +1421,8 @@
         fv[:, head] = w[:, g * 256 + 192 : (g + 1) * 256]
     for spread in spreads[1:]:
         spread.start()
-    chain.run(step, step + 2)
-    step = step + 2
+    step = 4
+    chain.run(0, step)
     pieces.wait_recv()
     fo[...] = oz[0] + oz[1] + oz[2] + oz[3]
     spread_o.start()
@@ -1436,8 +1431,8 @@
         c.start()
     for i in weights.order:
         weights.forward(i)
-    chain.run(step, step + 2)
-    step = step + 2
+    chain.run(step, step + 4)
+    step = step + 4
     plane.arrive()
 
     @pl.loop(0, tokens // ROWS)
@@ -1668,7 +1663,7 @@
 
     if fast:
         chunks = expert_in.shape[0] * (width + expert_down.shape[1]) // CHUNK
-        early, half = chunks // 12, (5 * chunks) // 12
+        early, half = chunks // 8, (3 * chunks) // 8
         results, drows, sums, total = experts_send(early, pack, x_rows, d_rows, expert_in, expert_down)
         flat = sums.reshape(-1, width)
         total, d_mid, gain_two, dqkv, po, pw = middle(

time: 694 us -> 657 us (0.947)
  Pallas kernels: 654 us -> 616 us
    pallas_call x1, Pallas kernels: 234 us -> 212 us  [last(): pl.pallas_call(functools.partial(last_kernel, first, count), in_specs=[hb...]
    pallas_call x1, Pallas kernels: 178 us -> 159 us  [middle(): pl.pallas_call(functools.partial(middle_kernel, first, count), in_specs=[...]
where the time goes in v7:
time: 657 us; the launch traced here: 647 us
  Pallas kernels  616 us (94%)
  local copies, waits for them, and re-layouts  22.3 us (3%)
  other arithmetic  7.14 us (1%)
    pallas_call x1, Pallas kernels, last(): pl.pallas_call(functools.partial(last_kernel, first, count), in_specs=[hb...  212 us
    pallas_call x1, Pallas kernels, middle(): pl.pallas_call(functools.partial(middle_kernel, first, count), in_specs=[...  159 us
    pallas_call x1, Pallas kernels, front(): pl.pallas_call(front_kernel, in_specs=[pl.BlockSpec(memory_space=pltpu.SM...  155 us
    pallas_call x1, Pallas kernels, experts_send(): pl.pallas_call(functools.partial(experts_send_kernel, count), grid=(here,...  72.8 us
    pallas_call x1, Pallas kernels, widen(): pl.pallas_call(widen_kernel, grid=(here, 3), in_specs=[pl.BlockSpec((1, f...  17.1 us

profile of v7, /device:TPU:0, one launch (start us, length us, event | category | flops | bytes accessed | tf_op | source)
XLA Modules:
  0.0 646.8 jit_solution(7189624442023849279)
XLA Ops:
  0.7 0.7 broadcast_compare_fusion
  1.4 0.1 pad.2.clone
  1.5 0.1 pad.5.clone
  1.6 0.7 copy.39
  2.3 0.8 fusion.7
  3.1 0.4 and_select_fusion
  3.4 0.8 select_reduce_fusion
  4.3 0.7 pad_maximum_fusion.4.pk_ref
  5.0 2.5 copy.35
  7.4 2.5 copy.36
  9.9 2.0 fusion.9
  11.8 2.2 fusion.2
  14.0 155.4 %front.1 = (bf16[4,512,1024]{2,1,0:T(8,128)(2,1)}, bf16[2,2,1024,256]{3,2,1,0:T(8,128)(2,1)}, f32[2,2,4,512]{3,2,1,0:T(4,128)}, bf16[4,512,256]{2,1,0:T(8,128)(2...) custom-call(s32[2]{0:T(128)} %len_ref.3, ...), custom_call_target="tpu_custom_call" | custom-call | flops 99999997952 | bytes 62914560 | tf_op jit(solution)/shard_map/front/pallas_call | solution.py:1144
  169.5 72.8 %experts_send.1 = (bf16[4,8,160,1024]{3,2,1,0:T(8,128)(2,1)}, bf16[4,8,160,1024]{3,2,1,0:T(8,128)(2,1)}, bf16[4,1536,1024]{2,1,0:T(8,128)(2,1)}, bf16[6144,1024]{1,0:T(8,128)(2,1)}) custom-call(f32[8,8,512]{2,1,0:T(8,128)} %get-tuple-element.40.pack_ref.slot_ref, bf16[4,8,160,1024]{3,2,1,0:T(8,128)(2,1)} %get-tuple-element.41.x_ref, ...), custom_call_target="tpu_custom_call" | custom-call | flops 48318382080 | bytes 41943040 | tf_op jit(solution)/shard_map/experts_send/pallas_call | solution.py:680
  242.3 158.7 %middle.1 = (bf16[6144,1024]{1,0:T(8,128)(2,1)}, f32[512,1024]{1,0:T(8,128)}, f32[1,1024]{1,0:T(1,128)}, bf16[4,512,512]{2,1,0:T(8,128)(2,1)}, bf16[8,128,1024]{...) custom-call(s32[2]{0:T(128)} %len_ref.3, ...), custom_call_target="tpu_custom_call", output_to_operand_aliasing={{0}: (1, {})} | custom-call | flops 99999997952 | bytes 31457280 | tf_op jit(solution)/shard_map/middle/pallas_call | solution.py:1281
  401.0 212.0 %last.1 = (bf16[6144,1024]{1,0:T(8,128)(2,1)}, bf16[512,1024]{1,0:T(8,128)(2,1)}, f32[512,1024]{1,0:T(8,128)}, f32[8,1024]{1,0:T(8,128)}, f32[256,1024]{1,0:T(8,...) custom-call(bf16[6144,1024]{1,0:T(8,128)(2,1)} %get-tuple-element.52., ...), custom_call_target="tpu_custom_call", output_to_operand_aliasing={{0}: (0, {})} | custom-call | flops 199999995904 | bytes 31457280 | tf_op jit(solution)/shard_map/last/pallas_call | solution.py:1515
  613.0 3.3 copy.43
  616.3 4.5 copy.42
  620.8 0.0 copy-start
  620.8 1.4 fusion.14
  622.3 17.1 %widen.1 = (f32[4,1024,1024]{2,1,0:T(8,128)}, f32[4,512,1024]{2,1,0:T(8,128)}) custom-call(bf16[4,1536,1024]{2,1,0:T(8,128)(2,1)} %bitcast.32), custom_call_target="tpu_custom_call" | custom-call | tf_op jit(solution)/shard_map/widen/pallas_call | solution.py:1580
  639.4 2.3 copy.50
  641.6 1.9 copy.51
  643.5 0.0 copy-done
  643.5 0.8 copy.52
  644.3 2.3 copy.53
  (7 shorter events, 0.1 us)
Async XLA Ops:
  620.8 22.7 %copy-start = (f32[1024,128]{1,0:T(8,128)S(1)}, f32[1024,128]{1,0:T(8,128)}, u32[]{:S(2)}) copy-start(f32[1024,128]{1,0:T(8,128)} %get-tuple-element.97) | copy-start | bytes 1572868

commit v8 on v7

--- a/solution.py
+++ b/solution.py
@@ -3,6 +3,7 @@
 
 import jax
 import jax.numpy as jnp
+import numpy as np
 from jax import lax
 from jax.experimental import pallas as pl
 from jax.experimental.pallas import tpu as pltpu
@@ -195,16 +196,16 @@
 
 def rotary_tables(length):
     half = HEAD // 2
-    frequency = jnp.exp(jnp.arange(half, dtype=F32) * (-2.0 * math.log(10000.0) / HEAD))
-    angles = jnp.arange(length, dtype=F32)[:, None] * frequency[None, :]
-    cos, sin = jnp.cos(angles), jnp.sin(angles)
-    c1 = jnp.concatenate([cos, cos], axis=1)
-    s1 = jnp.concatenate([-sin, sin], axis=1)
-    cq = jnp.concatenate([c1, c1], axis=1)
-    sq = jnp.concatenate([s1, s1], axis=1)
-    ckv = jnp.concatenate([c1, jnp.ones_like(c1)], axis=1)
-    skv = jnp.concatenate([s1, jnp.zeros_like(s1)], axis=1)
-    return cq, sq, ckv, skv
+    exponent = np.arange(half, dtype=np.float32) * np.float32(-2.0 * math.log(10000.0) / HEAD)
+    angles = np.arange(length, dtype=np.float32)[:, None] * np.exp(exponent)[None, :]
+    cos, sin = np.cos(angles), np.sin(angles)
+    c1 = np.concatenate([cos, cos], axis=1)
+    s1 = np.concatenate([-sin, sin], axis=1)
+    cq = np.concatenate([c1, c1], axis=1)
+    sq = np.concatenate([s1, s1], axis=1)
+    ckv = np.concatenate([c1, np.ones_like(c1)], axis=1)
+    skv = np.concatenate([s1, np.zeros_like(s1)], axis=1)
+    return tuple(jnp.asarray(t, F32) for t in (cq, sq, ckv, skv))
 
 
 def pick_rows(slots, cap):
@@ -913,8 +914,8 @@
 
 
 def front_kernel(len_ref, x_ref, og_ref, wq_ref, wk_ref, wv_ref, om_ref, pk_ref, again_ref, mgain_ref, cq, sq, ckv, skv,
-                 xg_ref, qkv_ref, lse_ref, hin_ref, of_ref, wz_ref, mid_ref, pack_ref, drows_ref, xrows_ref,
-                 w_ref, hs, ogb, mt, stage, ls, lr, ps, pr, hss, hrs, os_, or_, ws, wr, ss, *sems):
+                 xg_out, qkv_out, lse_ref, hin_out, of_out, wz_ref, mid_out, pack_ref, drows_ref, xrows_ref,
+                 xg_ref, qkv_ref, hin_ref, of_ref, mid_ref, outs, w_ref, hs, ogb, mt, stage, ls, lr, ps, pr, hss, hrs, os_, or_, ws, wr, ss, *sems):
     nh, tokens, width = xg_ref.shape
     nseq, groups, full, _ = qkv_ref.shape
     ne = ogb.shape[0]
@@ -1059,6 +1060,12 @@
         def _():
             heads(p).start()
 
+    done = [
+        pltpu.make_async_copy(src, dst, outs.at[t])
+        for t, (src, dst) in enumerate(
+            ((xg_ref, xg_out), (qkv_ref, qkv_out), (of_ref, of_out), (hin_ref, hin_out), (mid_ref, mid_out))
+        )
+    ]
     at_end = (z == 0) | (z == nh - 1)
     round_of(3, attend)
     for p in range(nseq):
@@ -1083,6 +1090,8 @@
         picker.pick(2 * i + 1, ogb[me ^ 1 ^ (2 * i)], drows_ref, True)
     for i in range(4):
         og_o.core_arrive(i)
+    for c in done[:3]:
+        c.start()
 
     for p in range(nseq):
         at = pl.ds(p * seg, seg)
@@ -1100,6 +1109,8 @@
 
         moes[p].start()
 
+    for c in done[3:]:
+        c.start()
     wzx.start()
     picker.pick(0, mt[me], xrows_ref, False)
     for p in range(nseq):
@@ -1121,6 +1132,8 @@
         moes[p].core_arrive(last)
     picker.pick(2 * last + 1, mt[me ^ 1 ^ (2 * last)], xrows_ref, False)
     picker.finish()
+    for c in done:
+        c.wait()
     wzx.wait_recv()
     for gather in [og, og_o] + moes:
         gather.finish()
@@ -1144,7 +1157,7 @@
     return pl.pallas_call(
         front_kernel,
         in_specs=[pl.BlockSpec(memory_space=pltpu.SMEM)] + [vmem] * 13,
-        out_specs=[vmem] * 8 + [hbm, hbm],
+        out_specs=[hbm, hbm, vmem, hbm, hbm, vmem, hbm, vmem, hbm, hbm],
         out_shape=[
             jax.ShapeDtypeStruct((nh, tokens, width), BF),
             jax.ShapeDtypeStruct((nseq, groups, full, 256), BF),
@@ -1158,6 +1171,12 @@
             rows,
         ],
         scratch_shapes=[
+            pltpu.VMEM((nh, tokens, width), BF),
+            pltpu.VMEM((nseq, groups, full, 256), BF),
+            pltpu.VMEM((nh, tokens, part), BF),
+            pltpu.VMEM((nh, ne, part // ne, width), BF),
+            pltpu.VMEM((tokens, width), F32),
+            DMA((5,)),
             pltpu.VMEM((width, cols), BF),
             pltpu.VMEM((nh, tokens, part), BF),
             pltpu.VMEM((ne, tokens, width), BF),
@@ -1184,8 +1203,9 @@
     )(lengths, x, og, wq, wk, wv, o_local, packed, attn_gain, moe_gain, *tables)
 
 
-def middle_kernel(first, count, len_ref, begun_ref, sum_ref, rows_ref, slot_ref, mid_ref, grad_ref, gain_ref, o_ref, qkv_ref, lse_ref,
-                  cq, sq, ckv, skv, hin_ref, x_ref, total_ref, dmid_ref, gtwo_ref, dqkv_ref, po_ref, pw_ref,
+def middle_kernel(first, count, len_ref, begun_ref, sum_ref, rows_ref, slot_ref, mid_in, grad_in, gain_ref, o_in, qkv_in, lse_ref,
+                  cq_in, sq_in, ckv_in, skv_in, hin_in, x_ref, total_ref, dmid_ref, gtwo_ref, dqkv_ref, po_ref, pw_ref,
+                  mid_ref, grad_ref, o_ref, qkv_ref, cq, sq, ckv, skv, hin_ref, inputs,
                   dbranch_ref, wsum, hs, hr, dmoe, dkv, hss, hrs, xs, *scratch):
     nh, tokens, _ = dqkv_ref.shape
     nseq, groups = qkv_ref.shape[:2]
@@ -1194,12 +1214,32 @@
     chain = Chain(sum_ref, total_ref, scratch[PLANE:], first, count)
     plane = PlaneSum(rows_ref, slot_ref, dmoe, scratch[:PLANE])
     heads = whole_exchange(hs, hr, hss, hrs, nh)
+    late = [
+        pltpu.make_async_copy(src, dst, inputs.at[t])
+        for t, (src, dst) in enumerate(
+            (
+                (mid_in, mid_ref),
+                (grad_in, grad_ref),
+                (o_in, o_ref),
+                (qkv_in, qkv_ref),
+                (cq_in, cq),
+                (sq_in, sq),
+                (ckv_in, ckv),
+                (skv_in, skv),
+                (hin_in, hin_ref),
+            )
+        )
+    ]
+    for c in late:
+        c.start()
     greet(nh, (1, 2, 4, 6))
     chain.begin()
     plane.run(chain, 0)
     step = 4 + 5
     chain.run(4, step)
     plane.arrive()
+    for c in late:
+        c.wait()
     gtwo_ref[...] = jnp.zeros_like(gtwo_ref)
 
     @pl.loop(0, tokens // ROWS)
@@ -1280,7 +1320,7 @@
     cols = groups * 256
     return pl.pallas_call(
         functools.partial(middle_kernel, first, count),
-        in_specs=[pl.BlockSpec(memory_space=pltpu.SMEM), hbm, hbm, hbm] + [vmem] * 12 + [hbm],
+        in_specs=[pl.BlockSpec(memory_space=pltpu.SMEM), hbm, hbm, hbm, vmem, hbm, hbm, vmem, hbm, hbm, vmem] + [hbm] * 6,
         input_output_aliases={1: 0},
         out_specs=[hbm] + [vmem] * 5,
         out_shape=[
@@ -1291,7 +1331,9 @@
             jax.ShapeDtypeStruct((ne, nh * groups * 128 // ne, width), BF),
             jax.ShapeDtypeStruct((ne, width // ne, cols), BF),
         ],
-        scratch_shapes=[
+        scratch_shapes=[pltpu.VMEM(v.shape, v.dtype) for v in (mid, grad, o_parts, qkv) + tuple(tables) + (heads_in,)]
+        + [
+            DMA((9,)),
             pltpu.VMEM((tokens, width), BF),
             pltpu.VMEM((width, cols), F32),
             pltpu.VMEM(heads, BF),
@@ -1363,9 +1405,9 @@
     return [pltpu.VMEM((n,) + shape, BF) for n in (4, 3, 3)] + [DMA((4,)), DMA((4,)), DMA((3,)), DMA((3,))]
 
 
-def last_kernel(first, count, begun_ref, sum_ref, rows_ref, slot_ref, mid_ref, dqkv_ref, wz_ref, x_ref, dmid_ref,
+def last_kernel(first, count, begun_ref, sum_ref, rows_ref, slot_ref, mid_in, dqkv_ref, wz_ref, x_in, dmid_ref,
                 gain_ref, gtwo_ref, po_ref, pw_ref, total_ref, out_ref, xgrad_ref, gains_ref, ograd_ref, qgrad_ref, kgrad_ref, vgrad_ref,
-                wf, br, moe, gp, gz, acc, oz, fo, fq, fk, fv, brs, brr, gps, gpr, gzs, gzr, oss, ors, fl, dl, *scratch):
+                mid_ref, x_ref, inputs, wf, br, moe, gp, gz, acc, oz, fo, fq, fk, fv, brs, brr, gps, gpr, gzs, gzr, oss, ors, fl, dl, *scratch):
     nh, tokens, _ = dqkv_ref.shape
     dattn = moe
     ne = rows_ref.shape[1]
@@ -1399,12 +1441,18 @@
         lambda h: oz.at[h], lambda d: oss.at[d], lambda d: ors.at[d], nh)
     first_part = pltpu.make_async_copy(dmid_ref, xgrad_ref, dl)
     first_part.start()
+    late = [
+        pltpu.make_async_copy(mid_in, mid_ref, inputs.at[0]),
+        pltpu.make_async_copy(x_in, x_ref, inputs.at[1]),
+        pltpu.make_async_copy(dqkv_ref.at[z], br.at[z], inputs.at[2]),
+    ]
+    for c in late:
+        c.start()
     greet(nh, tuple(range(1, ne)))
     back.start()
     sum_o.start()
     sum_w.start()
     chain.begin()
-    br[z] = dqkv_ref[z]
     sum_o.forward()
     sum_w.forward()
     weights.start()
@@ -1434,6 +1482,8 @@
     chain.run(step, step + 4)
     step = step + 4
     plane.arrive()
+    for c in late:
+        c.wait()
 
     @pl.loop(0, tokens // ROWS)
     def _(i):
@@ -1514,7 +1564,7 @@
     vmem = pl.BlockSpec(memory_space=pltpu.VMEM)
     return pl.pallas_call(
         functools.partial(last_kernel, first, count),
-        in_specs=[hbm, hbm, hbm] + [vmem] * 5 + [hbm] + [vmem] * 4,
+        in_specs=[hbm, hbm, hbm, vmem, hbm, hbm, vmem, hbm, hbm] + [vmem] * 4,
         input_output_aliases={0: 0},
         out_specs=[hbm] + [vmem] * 3 + [hbm] * 4,
         out_shape=[
@@ -1528,6 +1578,9 @@
             jax.ShapeDtypeStruct((row * ne, cols // 4), F32),
         ],
         scratch_shapes=[
+            pltpu.VMEM(mid.shape, mid.dtype),
+            pltpu.VMEM(x.shape, x.dtype),
+            DMA((3,)),
             pltpu.VMEM((nh, ne, width // ne, cols), BF),
             pltpu.VMEM((nh, tokens, cols), BF),
             pltpu.VMEM((tokens, width), F32),

time: 657 us -> 641 us (0.976)
  Pallas kernels: 616 us -> 608 us
where the time goes in v8:
time: 641 us; the launch traced here: 634 us
  Pallas kernels  608 us (95%)
  local copies, waits for them, and re-layouts  22.1 us (3%)
    pallas_call x1, Pallas kernels, last(): pl.pallas_call(functools.partial(last_kernel, first, count), in_specs=[hb...  211 us
    pallas_call x1, Pallas kernels, middle(): pl.pallas_call(functools.partial(middle_kernel, first, count), in_specs=[...  156 us
    pallas_call x1, Pallas kernels, front(): pl.pallas_call(front_kernel, in_specs=[pl.BlockSpec(memory_space=pltpu.SM...  152 us
    pallas_call x1, Pallas kernels, experts_send(): pl.pallas_call(functools.partial(experts_send_kernel, count), grid=(here,...  72.8 us
    pallas_call x1, Pallas kernels, widen(): pl.pallas_call(widen_kernel, grid=(here, 3), in_specs=[pl.BlockSpec((1, f...  17.1 us

profile of v8, /device:TPU:0, one launch (start us, length us, event | category | flops | bytes accessed | tf_op | source)
XLA Modules:
  0.0 634.4 jit_solution(13872289854948661765)
XLA Ops:
  0.7 0.7 broadcast_compare_fusion
  1.4 0.7 copy.43
  2.1 0.8 fusion.3
  2.9 0.4 and_select_fusion
  3.3 0.8 select_reduce_fusion
  4.1 0.7 pad_maximum_fusion.pk_ref
  4.8 2.5 copy.39
  7.2 2.5 copy.40
  9.7 151.8 %front.1 = (bf16[4,512,1024]{2,1,0:T(8,128)(2,1)}, bf16[2,2,1024,256]{3,2,1,0:T(8,128)(2,1)}, f32[2,2,4,512]{3,2,1,0:T(4,128)}, bf16[4,512,256]{2,1,0:T(8,128)(2...) custom-call(s32[2]{0:T(128)} %len_ref.3, ...), custom_call_target="tpu_custom_call" | custom-call | flops 99999997952 | bytes 62914560 | tf_op jit(solution)/shard_map/front/pallas_call | solution.py:1157
  161.5 72.8 %experts_send.1 = (bf16[4,8,160,1024]{3,2,1,0:T(8,128)(2,1)}, bf16[4,8,160,1024]{3,2,1,0:T(8,128)(2,1)}, bf16[4,1536,1024]{2,1,0:T(8,128)(2,1)}, bf16[6144,1024]{1,0:T(8,128)(2,1)}) custom-call(f32[8,8,512]{2,1,0:T(8,128)} %get-tuple-element.40.pack_ref.slot_ref, bf16[4,8,160,1024]{3,2,1,0:T(8,128)(2,1)} %get-tuple-element.41.x_ref, ...), custom_call_target="tpu_custom_call" | custom-call | flops 48318382080 | bytes 41943040 | tf_op jit(solution)/shard_map/experts_send/pallas_call | solution.py:681
  234.4 155.6 %middle.1 = (bf16[6144,1024]{1,0:T(8,128)(2,1)}, f32[512,1024]{1,0:T(8,128)}, f32[1,1024]{1,0:T(1,128)}, bf16[4,512,512]{2,1,0:T(8,128)(2,1)}, bf16[8,128,1024]{...) custom-call(s32[2]{0:T(128)} %len_ref.3, ...), custom_call_target="tpu_custom_call", output_to_operand_aliasing={{0}: (1, {})} | custom-call | flops 99999997952 | bytes 31457280 | tf_op jit(solution)/shard_map/middle/pallas_call | solution.py:1321
  389.9 210.7 %last.1 = (bf16[6144,1024]{1,0:T(8,128)(2,1)}, bf16[512,1024]{1,0:T(8,128)(2,1)}, f32[512,1024]{1,0:T(8,128)}, f32[8,1024]{1,0:T(8,128)}, f32[256,1024]{1,0:T(8,...) custom-call(bf16[6144,1024]{1,0:T(8,128)(2,1)} %get-tuple-element.52., ...), custom_call_target="tpu_custom_call", output_to_operand_aliasing={{0}: (0, {})} | custom-call | flops 199999995904 | bytes 31457280 | tf_op jit(solution)/shard_map/last/pallas_call | solution.py:1565
  600.6 3.3 copy.47
  603.9 4.5 copy.46
  608.4 0.0 copy-start
  608.4 1.4 fusion.9
  609.9 17.1 %widen.1 = (f32[4,1024,1024]{2,1,0:T(8,128)}, f32[4,512,1024]{2,1,0:T(8,128)}) custom-call(bf16[4,1536,1024]{2,1,0:T(8,128)(2,1)} %bitcast.32), custom_call_target="tpu_custom_call" | custom-call | tf_op jit(solution)/shard_map/widen/pallas_call | solution.py:1633
  626.9 2.3 copy.54
  629.2 1.9 copy.55
  631.1 0.0 copy-done
  631.1 0.8 copy.56
  631.9 2.3 copy.57
  (4 shorter events, 0.1 us)
Async XLA Ops:
  608.4 22.7 %copy-start = (f32[1024,128]{1,0:T(8,128)S(1)}, f32[1024,128]{1,0:T(8,128)}, u32[]{:S(2)}) copy-start(f32[1024,128]{1,0:T(8,128)} %get-tuple-element.88) | copy-start | bytes 1572868

commit v9 on v8

--- a/solution.py
+++ b/solution.py
@@ -1204,8 +1204,8 @@
 
 
 def middle_kernel(first, count, len_ref, begun_ref, sum_ref, rows_ref, slot_ref, mid_in, grad_in, gain_ref, o_in, qkv_in, lse_ref,
-                  cq_in, sq_in, ckv_in, skv_in, hin_in, x_ref, total_ref, dmid_ref, gtwo_ref, dqkv_ref, po_ref, pw_ref,
-                  mid_ref, grad_ref, o_ref, qkv_ref, cq, sq, ckv, skv, hin_ref, inputs,
+                  cq_in, sq_in, ckv_in, skv_in, hin_in, x_ref, total_ref, dmid_out, gtwo_ref, dqkv_out, po_out, pw_ref,
+                  dmid_ref, dqkv_ref, po_ref, outs, mid_ref, grad_ref, o_ref, qkv_ref, cq, sq, ckv, skv, hin_ref, inputs,
                   dbranch_ref, wsum, hs, hr, dmoe, dkv, hss, hrs, xs, *scratch):
     nh, tokens, _ = dqkv_ref.shape
     nseq, groups = qkv_ref.shape[:2]
@@ -1257,7 +1257,12 @@
         for h in range(nh):
             hs[h, rows] = dot_nt(db, o_ref[h]).astype(BF)
 
+    done = [
+        pltpu.make_async_copy(src, dst, outs.at[t])
+        for t, (src, dst) in enumerate(((dmid_ref, dmid_out), (dqkv_ref, dqkv_out), (po_ref, po_out)))
+    ]
     heads.start()
+    done[0].start()
     hr[z] = hs[z]
     chain.run(step, step + 4)
     step = step + 4
@@ -1288,6 +1293,7 @@
         plane.core(i).wait_send()
     load = pltpu.make_async_copy(x_ref, plane.odd, xs)
     load.start()
+    done[1].start()
     ne, deep, _ = po_ref.shape
     strip, row = deep // nh, pw_ref.shape[1]
     db = dbranch_ref[...]
@@ -1295,6 +1301,7 @@
         o = dot_tn(hin_ref[h], db).astype(BF)
         for e in range(ne):
             po_ref[e, h * strip : (h + 1) * strip] = o[e * strip : (e + 1) * strip]
+    done[2].start()
     chain.step(step)
     load.wait()
     wsum[...] = dot_tn(plane.odd[0], dqkv_ref[0])
@@ -1307,6 +1314,8 @@
     for i in plane.order:
         plane.chip(i).wait_send()
     heads.finish()
+    for c in done:
+        c.wait()
 
 
 def middle(first, count, lengths, total, sums, rows, slots, mid, grad, gain, o_parts, qkv, lse, tables, heads_in, x):
@@ -1322,7 +1331,7 @@
         functools.partial(middle_kernel, first, count),
         in_specs=[pl.BlockSpec(memory_space=pltpu.SMEM), hbm, hbm, hbm, vmem, hbm, hbm, vmem, hbm, hbm, vmem] + [hbm] * 6,
         input_output_aliases={1: 0},
-        out_specs=[hbm] + [vmem] * 5,
+        out_specs=[hbm, hbm, vmem, hbm, hbm, vmem],
         out_shape=[
             jax.ShapeDtypeStruct(sums.shape, BF),
             jax.ShapeDtypeStruct((tokens, width), F32),
@@ -1331,7 +1340,13 @@
             jax.ShapeDtypeStruct((ne, nh * groups * 128 // ne, width), BF),
             jax.ShapeDtypeStruct((ne, width // ne, cols), BF),
         ],
-        scratch_shapes=[pltpu.VMEM(v.shape, v.dtype) for v in (mid, grad, o_parts, qkv) + tuple(tables) + (heads_in,)]
+        scratch_shapes=[
+            pltpu.VMEM((tokens, width), F32),
+            pltpu.VMEM((nh, tokens, cols), BF),
+            pltpu.VMEM((ne, nh * groups * 128 // ne, width), BF),
+            DMA((3,)),
+        ]
+        + [pltpu.VMEM(v.shape, v.dtype) for v in (mid, grad, o_parts, qkv) + tuple(tables) + (heads_in,)]
         + [
             DMA((9,)),
             pltpu.VMEM((tokens, width), BF),
@@ -1406,8 +1421,8 @@
 
 
 def last_kernel(first, count, begun_ref, sum_ref, rows_ref, slot_ref, mid_in, dqkv_ref, wz_ref, x_in, dmid_ref,
-                gain_ref, gtwo_ref, po_ref, pw_ref, total_ref, out_ref, xgrad_ref, gains_ref, ograd_ref, qgrad_ref, kgrad_ref, vgrad_ref,
-                mid_ref, x_ref, inputs, wf, br, moe, gp, gz, acc, oz, fo, fq, fk, fv, brs, brr, gps, gpr, gzs, gzr, oss, ors, fl, dl, *scratch):
+                gain_ref, gtwo_ref, po_ref, pw_ref, total_ref, out_out, xgrad_out, gains_ref, ograd_ref, qgrad_ref, kgrad_ref, vgrad_ref,
+                out_ref, xgrad_ref, outs, mid_ref, x_ref, inputs, wf, br, moe, gp, gz, acc, oz, fo, fq, fk, fv, brs, brr, gps, gpr, gzs, gzr, oss, ors, fl, dl, *scratch):
     nh, tokens, _ = dqkv_ref.shape
     dattn = moe
     ne = rows_ref.shape[1]
@@ -1490,6 +1505,8 @@
         rows = pl.ds(i * ROWS, ROWS)
         out_ref[rows] = (mid_ref[rows] + plane.rows_total(rows)).astype(BF)
 
+    done = [pltpu.make_async_copy(out_ref, out_out, outs.at[0]), pltpu.make_async_copy(xgrad_ref, xgrad_out, outs.at[1])]
+    done[0].start()
     chain.run(step, step + 2)
     step = step + 2
     for i in range(4):
@@ -1517,6 +1534,7 @@
 
     first_part.wait()
     own = lax.fori_loop(0, tokens // ROWS, rows_back, own)
+    done[1].start()
     gp[me] = jnp.concatenate([own, gtwo_ref[...], pad], axis=0)
 
     def near(r, at):
@@ -1549,7 +1567,7 @@
     chain.finish()
     for part in [plane, back, pieces, gains, weights, sum_o, sum_w] + spreads:
         part.finish()
-    for c in keep:
+    for c in keep + done:
         c.wait()
     for r in range(1, ne):
         near(r, me).wait_send()
@@ -1566,7 +1584,7 @@
         functools.partial(last_kernel, first, count),
         in_specs=[hbm, hbm, hbm, vmem, hbm, hbm, vmem, hbm, hbm] + [vmem] * 4,
         input_output_aliases={0: 0},
-        out_specs=[hbm] + [vmem] * 3 + [hbm] * 4,
+        out_specs=[hbm] * 3 + [vmem] + [hbm] * 4,
         out_shape=[
             jax.ShapeDtypeStruct(sums.shape, BF),
             jax.ShapeDtypeStruct((tokens, width), BF),
@@ -1578,6 +1596,9 @@
             jax.ShapeDtypeStruct((row * ne, cols // 4), F32),
         ],
         scratch_shapes=[
+            pltpu.VMEM((tokens, width), BF),
+            pltpu.VMEM((tokens, width), F32),
+            DMA((2,)),
             pltpu.VMEM(mid.shape, mid.dtype),
             pltpu.VMEM(x.shape, x.dtype),
             DMA((3,)),
@@ -1616,8 +1637,10 @@
     )(total, sums, rows, slots, mid, dqkv, w_pieces, x, d_mid, gain, gain_two, po, pw)
 
 
-def widen_kernel(x_ref, in_ref, down_ref):
+def widen_kernel(x_ref, *refs):
     c = pl.program_id(1)
+    count = (len(refs) - 2) // 2
+    in_ref, down_ref = refs[count : count + 2]
 
     @pl.when(c < 2)
     def _():
@@ -1627,24 +1650,32 @@
     def _():
         down_ref[...] = x_ref[...].astype(F32)
 
-
-def widen(sums, ff):
+    @pl.when(c == 0)
+    def _():
+        for src, dst in zip(refs[:count], refs[count + 2 :]):
+            dst[...] = src[...]
+
+
+def widen(sums, ff, others):
     here, rows, width = sums.shape
+    blocks = [pl.BlockSpec((v.shape[0] // here, v.shape[1]), lambda j, c: (j, 0)) for v in others]
     return pl.pallas_call(
         widen_kernel,
         grid=(here, 3),
-        in_specs=[pl.BlockSpec((1, ff, width), lambda j, c: (j, c, 0))],
+        in_specs=[pl.BlockSpec((1, ff, width), lambda j, c: (j, c, 0))] + blocks,
         out_specs=[
             pl.BlockSpec((1, ff, width), lambda j, c: (j, jnp.minimum(c, 1), 0)),
             pl.BlockSpec((1, ff, width), lambda j, c: (j, 0, 0)),
-        ],
+        ]
+        + blocks,
         out_shape=[
             jax.ShapeDtypeStruct((here, 2 * ff, width), F32),
             jax.ShapeDtypeStruct((here, ff, width), F32),
-        ],
+        ]
+        + [jax.ShapeDtypeStruct(v.shape, v.dtype) for v in others],
         compiler_params=params(2),
         name="widen",
-    )(sums)
+    )(sums, *others)
 
 
 def body(layer_input, seq_lengths, expert_ids, route_weight, priority, attn_gain, moe_gain,
@@ -1725,7 +1756,8 @@
         total, out, x_grad, gains, o_grad, q_grad, k_grad, v_grad = last(
             early + half, chunks - early - half, total, flat, results, pack, mid, dqkv, w_pieces, x, d_mid, gain_a, gain_two, po, pw)
         gain_one, gain_two = gains[0], gains[1]
-        grad_in, grad_down = widen(total.reshape(sums.shape), expert_down.shape[1])
+        grad_in, grad_down, o_grad, q_grad, k_grad, v_grad = widen(
+            total.reshape(sums.shape), expert_down.shape[1], (o_grad, q_grad, k_grad, v_grad))
     else:
         results, drows, sums = experts_call(slots, weights, x_rows, d_rows, expert_in, expert_down)
         slots_t = jnp.swapaxes(slots, 1, 2)

time: 641 us -> 632 us (0.986)
  local copies, waits for them, and re-layouts: 22.1 us -> 14.9 us
    unnamed x7 -> x1, local copies, waits for them, and re-layouts: 7.91 us -> 0.68 us
where the time goes in v9:
time: 632 us; the launch traced here: 625 us
  Pallas kernels  606 us (96%)
  local copies, waits for them, and re-layouts  14.9 us (2%)
    pallas_call x1, Pallas kernels, last(): pl.pallas_call(functools.partial(last_kernel, first, count), in_specs=[hb...  210 us
    pallas_call x1, Pallas kernels, middle(): pl.pallas_call(functools.partial(middle_kernel, first, count), in_specs=[...  154 us
    pallas_call x1, Pallas kernels, front(): pl.pallas_call(front_kernel, in_specs=[pl.BlockSpec(memory_space=pltpu.SM...  152 us
    pallas_call x1, Pallas kernels, experts_send(): pl.pallas_call(functools.partial(experts_send_kernel, count), grid=(here,...  72.8 us
    pallas_call x1, Pallas kernels, widen(): pl.pallas_call(widen_kernel, grid=(here, 3), in_specs=[pl.BlockSpec((1, f...  18.3 us

profile of v9, /device:TPU:0, one launch (start us, length us, event | category | flops | bytes accessed | tf_op | source)
XLA Modules:
  0.0 625.5 jit_solution(11931187365467080058)
XLA Ops:
  0.7 0.7 broadcast_compare_fusion
  1.4 0.7 copy.43
  2.1 0.8 fusion.3
  2.9 0.4 and_select_fusion
  3.3 0.8 select_reduce_fusion
  4.1 0.7 pad_maximum_fusion.pk_ref
  4.8 2.5 copy.39
  7.2 2.5 copy.40
  9.7 151.8 %front.1 = (bf16[4,512,1024]{2,1,0:T(8,128)(2,1)}, bf16[2,2,1024,256]{3,2,1,0:T(8,128)(2,1)}, f32[2,2,4,512]{3,2,1,0:T(4,128)}, bf16[4,512,256]{2,1,0:T(8,128)(2...) custom-call(s32[2]{0:T(128)} %len_ref.3, ...), custom_call_target="tpu_custom_call" | custom-call | flops 99999997952 | bytes 62914560 | tf_op jit(solution)/shard_map/front/pallas_call | solution.py:1157
  161.5 72.8 %experts_send.1 = (bf16[4,8,160,1024]{3,2,1,0:T(8,128)(2,1)}, bf16[4,8,160,1024]{3,2,1,0:T(8,128)(2,1)}, bf16[4,1536,1024]{2,1,0:T(8,128)(2,1)}, bf16[6144,1024]{1,0:T(8,128)(2,1)}) custom-call(f32[8,8,512]{2,1,0:T(8,128)} %get-tuple-element.44.pack_ref.slot_ref, bf16[4,8,160,1024]{3,2,1,0:T(8,128)(2,1)} %get-tuple-element.45.x_ref, ...), custom_call_target="tpu_custom_call" | custom-call | flops 48318382080 | bytes 41943040 | tf_op jit(solution)/shard_map/experts_send/pallas_call | solution.py:681
  234.3 153.7 %middle.1 = (bf16[6144,1024]{1,0:T(8,128)(2,1)}, f32[512,1024]{1,0:T(8,128)}, f32[1,1024]{1,0:T(1,128)}, bf16[4,512,512]{2,1,0:T(8,128)(2,1)}, bf16[8,128,1024]{...) custom-call(s32[2]{0:T(128)} %len_ref.3, ...), custom_call_target="tpu_custom_call", output_to_operand_aliasing={{0}: (1, {})} | custom-call | flops 99999997952 | bytes 31457280 | tf_op jit(solution)/shard_map/middle/pallas_call | solution.py:1330
  388.0 209.6 %last.1 = (bf16[6144,1024]{1,0:T(8,128)(2,1)}, bf16[512,1024]{1,0:T(8,128)(2,1)}, f32[512,1024]{1,0:T(8,128)}, f32[8,1024]{1,0:T(8,128)}, f32[256,1024]{1,0:T(8,...) custom-call(bf16[6144,1024]{1,0:T(8,128)(2,1)} %get-tuple-element.56., ...), custom_call_target="tpu_custom_call", output_to_operand_aliasing={{0}: (0, {})} | custom-call | flops 199999995904 | bytes 31457280 | tf_op jit(solution)/shard_map/last/pallas_call | solution.py:1583
  597.7 3.3 copy.47
  600.9 4.5 copy.46
  605.5 1.4 fusion.9
  606.9 18.3 %widen.1 = (f32[4,1024,1024]{2,1,0:T(8,128)}, f32[4,512,1024]{2,1,0:T(8,128)}, f32[256,1024]{1,0:T(8,128)}, f32[1024,256]{1,0:T(8,128)}, f32[1024,128]{1,0:T(8,128)}, /*index=5*/f32[1024,128]{1,0:T(8,128)}) custom-call(bf16[4,1536,1024]{2,1,0:T(8,128)(2,1)} %bitcast.32, f32[256,1024]{1,0:T(8,128)} %get-tuple-element.68.refs_0_, ...), custom_call_target="tpu_custom_call" | custom-call | tf_op jit(solution)/shard_map/widen/pallas_call | solution.py:1662
  (4 shorter events, 0.1 us)

commit v10 on v9

--- a/solution.py
+++ b/solution.py
@@ -1653,29 +1653,39 @@
     @pl.when(c == 0)
     def _():
         for src, dst in zip(refs[:count], refs[count + 2 :]):
-            dst[...] = src[...]
-
-
-def widen(sums, ff, others):
+            if len(dst.shape) == 2:
+                dst[...] = src[...]
+            else:
+                for q in range(dst.shape[1]):
+                    dst[:, q, :] = src[q]
+
+
+def widen(sums, ff, others, turned):
     here, rows, width = sums.shape
     blocks = [pl.BlockSpec((v.shape[0] // here, v.shape[1]), lambda j, c: (j, 0)) for v in others]
+    count, length, _ = turned.shape
+    part = length // here
+    turn_in = pl.BlockSpec((count, part, width), lambda j, c: (0, j, 0))
+    turn_out = pl.BlockSpec((part, count, width), lambda j, c: (j, 0, 0))
     return pl.pallas_call(
         widen_kernel,
         grid=(here, 3),
-        in_specs=[pl.BlockSpec((1, ff, width), lambda j, c: (j, c, 0))] + blocks,
+        in_specs=[pl.BlockSpec((1, ff, width), lambda j, c: (j, c, 0))] + blocks + [turn_in],
         out_specs=[
             pl.BlockSpec((1, ff, width), lambda j, c: (j, jnp.minimum(c, 1), 0)),
             pl.BlockSpec((1, ff, width), lambda j, c: (j, 0, 0)),
         ]
-        + blocks,
+        + blocks
+        + [turn_out],
         out_shape=[
             jax.ShapeDtypeStruct((here, 2 * ff, width), F32),
             jax.ShapeDtypeStruct((here, ff, width), F32),
         ]
-        + [jax.ShapeDtypeStruct(v.shape, v.dtype) for v in others],
+        + [jax.ShapeDtypeStruct(v.shape, v.dtype) for v in others]
+        + [jax.ShapeDtypeStruct((length, count, width), turned.dtype)],
         compiler_params=params(2),
         name="widen",
-    )(sums, *others)
+    )(sums, *others, turned)
 
 
 def body(layer_input, seq_lengths, expert_ids, route_weight, priority, attn_gain, moe_gain,
@@ -1756,8 +1766,9 @@
         total, out, x_grad, gains, o_grad, q_grad, k_grad, v_grad = last(
             early + half, chunks - early - half, total, flat, results, pack, mid, dqkv, w_pieces, x, d_mid, gain_a, gain_two, po, pw)
         gain_one, gain_two = gains[0], gains[1]
-        grad_in, grad_down, o_grad, q_grad, k_grad, v_grad = widen(
-            total.reshape(sums.shape), expert_down.shape[1], (o_grad, q_grad, k_grad, v_grad))
+        grad_in, grad_down, o_grad, q_grad, k_grad, v_grad, x_grad = widen(
+            total.reshape(sums.shape), expert_down.shape[1], (o_grad, q_grad, k_grad, v_grad),
+            x_grad.reshape(nseq, seg, width))
     else:
         results, drows, sums = experts_call(slots, weights, x_rows, d_rows, expert_in, expert_down)
         slots_t = jnp.swapaxes(slots, 1, 2)
@@ -1790,7 +1801,7 @@
         v_grad = w_grad[:, :, 192:].reshape(value_matrix.shape)
     return (
         unlocal(out),
-        unlocal(x_grad),
+        x_grad if fast else unlocal(x_grad),
         gain_one,
         gain_two,
         q_grad,

time: 632 us -> 629 us (level)
  no operation moved by 1% of the time
where the time goes in v10:
time: 629 us; the launch traced here: 622 us
  Pallas kernels  607 us (97%)
  local copies, waits for them, and re-layouts  10.4 us (2%)
    pallas_call x1, Pallas kernels, last(): pl.pallas_call(functools.partial(last_kernel, first, count), in_specs=[hb...  210 us
    pallas_call x1, Pallas kernels, middle(): pl.pallas_call(functools.partial(middle_kernel, first, count), in_specs=[...  154 us
    pallas_call x1, Pallas kernels, front(): pl.pallas_call(front_kernel, in_specs=[pl.BlockSpec(memory_space=pltpu.SM...  152 us
    pallas_call x1, Pallas kernels, experts_send(): pl.pallas_call(functools.partial(experts_send_kernel, count), grid=(here,...  72.8 us
    pallas_call x1, Pallas kernels, widen(): pl.pallas_call(widen_kernel, grid=(here, 3), in_specs=[pl.BlockSpec((1, f...  19.3 us

profile of v10, /device:TPU:0, one launch (start us, length us, event | category | flops | bytes accessed | tf_op | source)
XLA Modules:
  0.0 621.9 jit_solution(15031394536407025733)
XLA Ops:
  0.7 0.7 broadcast_compare_fusion
  1.4 0.7 copy.40
  2.1 0.8 fusion.3
  2.9 0.4 and_select_fusion
  3.3 0.8 select_reduce_fusion
  4.1 0.7 pad_maximum_fusion.pk_ref
  4.8 2.5 copy.37
  7.2 2.5 copy.38
  9.7 151.8 %front.1 = (bf16[4,512,1024]{2,1,0:T(8,128)(2,1)}, bf16[2,2,1024,256]{3,2,1,0:T(8,128)(2,1)}, f32[2,2,4,512]{3,2,1,0:T(4,128)}, bf16[4,512,256]{2,1,0:T(8,128)(2...) custom-call(s32[2]{0:T(128)} %len_ref.3, ...), custom_call_target="tpu_custom_call" | custom-call | flops 99999997952 | bytes 62914560 | tf_op jit(solution)/shard_map/front/pallas_call | solution.py:1157
  161.5 72.8 %experts_send.1 = (bf16[4,8,160,1024]{3,2,1,0:T(8,128)(2,1)}, bf16[4,8,160,1024]{3,2,1,0:T(8,128)(2,1)}, bf16[4,1536,1024]{2,1,0:T(8,128)(2,1)}, bf16[6144,1024]{1,0:T(8,128)(2,1)}) custom-call(f32[8,8,512]{2,1,0:T(8,128)} %get-tuple-element.45.pack_ref.slot_ref, bf16[4,8,160,1024]{3,2,1,0:T(8,128)(2,1)} %get-tuple-element.46.x_ref, ...), custom_call_target="tpu_custom_call" | custom-call | flops 48318382080 | bytes 41943040 | tf_op jit(solution)/shard_map/experts_send/pallas_call | solution.py:681
  234.3 153.7 %middle.1 = (bf16[6144,1024]{1,0:T(8,128)(2,1)}, f32[512,1024]{1,0:T(8,128)}, f32[1,1024]{1,0:T(1,128)}, bf16[4,512,512]{2,1,0:T(8,128)(2,1)}, bf16[8,128,1024]{...) custom-call(s32[2]{0:T(128)} %len_ref.3, ...), custom_call_target="tpu_custom_call", output_to_operand_aliasing={{0}: (1, {})} | custom-call | flops 99999997952 | bytes 31457280 | tf_op jit(solution)/shard_map/middle/pallas_call | solution.py:1330
  388.0 209.6 %last.1 = (bf16[6144,1024]{1,0:T(8,128)(2,1)}, bf16[512,1024]{1,0:T(8,128)(2,1)}, f32[512,1024]{1,0:T(8,128)}, f32[8,1024]{1,0:T(8,128)}, f32[256,1024]{1,0:T(8,...) custom-call(bf16[6144,1024]{1,0:T(8,128)(2,1)} %get-tuple-element.57., ...), custom_call_target="tpu_custom_call", output_to_operand_aliasing={{0}: (0, {})} | custom-call | flops 199999995904 | bytes 31457280 | tf_op jit(solution)/shard_map/last/pallas_call | solution.py:1583
  597.7 3.3 copy.42
  600.9 1.4 fusion.9
  602.4 19.3 %widen.1 = (f32[4,1024,1024]{2,1,0:T(8,128)}, f32[4,512,1024]{2,1,0:T(8,128)}, f32[256,1024]{1,0:T(8,128)}, f32[1024,256]{1,0:T(8,128)}, f32[1024,128]{1,0:T(8,1...) custom-call(bf16[4,1536,1024]{2,1,0:T(8,128)(2,1)} %bitcast.29, f32[256,1024]{1,0:T(8,128)} %get-tuple-element.67.refs_0_, ...), custom_call_target="tpu_custom_call" | custom-call | tf_op jit(solution)/shard_map/widen/pallas_call | solution.py:1670
  (4 shorter events, 0.1 us)
